TPU v7x, 512 devices: a whole 4x8x8 slice. The times are simulated.
512 devices in a mesh: expert: 64 (over z_lo, y, core), mp: 8 (over x, z_hi).
Axes of the slice: x: 4, y: 8, z: 8 (z_hi: 2, z_lo: 4; z = z_hi * 4 + z_lo), core: 2. Of those that a mesh axis runs over, the one named last changes fastest.
Arguments:
- queries: bfloat16 [16384, 2048], P('expert', 'mp'), may hold values from -8 to 8
- src_keys: bfloat16 [16384, 2048], P(('expert', 'mp')), may hold values from -8 to 8
- src_values: bfloat16 [16384, 2048], P(('expert', 'mp')), may hold values from -9 to 9
- tgt_doc: int32 [64, 256], P('expert'), may hold values from 0 to 3, never falling along the last dimension, each value on 1 to 128 neighbouring positions
- src_doc: int32 [64, 256], P('expert'), may hold values from 0 to 3, never falling along the last dimension, each value on 1 to 128 neighbouring positions
- hidden_in: bfloat16 [16384, 4096], P('expert', 'mp'), may hold values from -6 to 6
- out_proj: bfloat16 [2048, 4096], P('expert', 'mp'), may hold values from -0.375 to 0.375
- norm_gain: float32 [4096], P('mp'), may hold values from 0.1 to 1.9
- router: bfloat16 [4096, 64], P('mp'), may hold values from -0.09375 to 0.09375
- expert_ids: int32 [64, 256], P('expert'), may hold values from 0 to 63, as said below
- expert_slots: int32 [64, 256], P('expert'), may hold values from 0 to 7, as said below
- w_in: bfloat16 [64, 4096, 2048], P('expert', None, 'mp'), may hold values from -0.09375 to 0.09375
- w_out: bfloat16 [64, 2048, 4096], P('expert', 'mp'), may hold values from -0.125 to 0.125
Outputs:
- layer_out: bfloat16 [16384, 4096], P('expert', 'mp')
Inputs may be any that keep to these rules, and one draw needn't show every extreme that they name: `expert_ids`: within a group no two rows share an expert and a slot; an expert has at most 8 rows of one group, and one expert has exactly 8 rows of every group. `expert_slots`: slots are numbered within the expert's slots for the group. `tgt_doc`: each group's target rows name every document id from 0 to 3. `src_doc`: each group's source rows name every document id from 0 to 3.
All inputs are finite; a program needn't handle non-finite values.
Results may differ from a plain program's by a relative error of at most 0.011.
Values may be sent and summed in bfloat16 or wider, within the bound.
No kernel may reach another device: no remote copies, remote signals or barrier semaphores. Data moves between devices by JAX's collectives and lax.ppermute only.
A program may use at most 64 MiB of HBM per device.

v0:
```python
import jax
import jax.numpy as jnp
from jax import lax
from jax.sharding import PartitionSpec as P

D = 4096
HEAD_DIM = 64


def body(
    queries,
    src_keys,
    src_values,
    tgt_doc,
    src_doc,
    hidden_in,
    out_proj,
    norm_gain,
    router,
    expert_ids,
    expert_slots,
    w_in,
    w_out,
):
    keys_local, values_local = (
        lax.all_to_all(src_keys, "mp", split_axis=1, concat_axis=0, tiled=True),
        lax.all_to_all(src_values, "mp", split_axis=1, concat_axis=0, tiled=True),
    )
    target_rows = queries.shape[0]
    head_width = queries.shape[1]
    heads_here = head_width // HEAD_DIM
    factor = 1.0 / HEAD_DIM**0.5
    query_heads = queries.reshape(target_rows, heads_here, HEAD_DIM)
    key_heads = keys_local.reshape(-1, heads_here, HEAD_DIM)
    value_heads = values_local.reshape(-1, heads_here, HEAD_DIM)
    scores = (
        jnp.einsum("thd,shd->hts", query_heads, key_heads, preferred_element_type=jnp.float32)
        * factor
    )
    same = tgt_doc[0][:, None] == src_doc[0][None, :]
    scores = jnp.where(same[None], scores, jnp.float32(-1e30))
    peak = jnp.max(scores, axis=2, keepdims=True)
    expo = jnp.exp(scores - peak)
    weights = (expo / jnp.sum(expo, axis=2, keepdims=True)).astype(jnp.bfloat16)
    attended = jnp.einsum("hts,shd->thd", weights, value_heads, preferred_element_type=jnp.float32)
    attended = attended.astype(jnp.bfloat16).reshape(target_rows, head_width)
    attended_all = lax.all_gather(attended, "mp", axis=1, tiled=True)
    attn_out = jnp.dot(
        attended_all,
        lax.all_gather(out_proj, "expert", axis=0, tiled=True),
        preferred_element_type=jnp.float32,
    )
    mixed = hidden_in.astype(jnp.float32) + attn_out
    gated = mixed * norm_gain
    part_squares = jnp.sum(mixed * mixed, axis=1)
    part_logits = jnp.dot(gated, router.astype(jnp.float32), precision=lax.Precision.HIGHEST)
    sum_squares, logits_raw = (
        lax.psum(part_squares.astype(jnp.bfloat16), "mp").astype(jnp.float32),
        lax.psum(part_logits.astype(jnp.bfloat16), "mp").astype(jnp.float32),
    )
    inverse_rms = lax.rsqrt(sum_squares / D + 1e-06)
    normed = (gated * inverse_rms[:, None]).astype(jnp.bfloat16)
    logits = logits_raw * inverse_rms[:, None]
    experts = router.shape[1]
    specialist_room = 2 * target_rows // experts
    chosen_ids = expert_ids[0]
    expert_column = lax.broadcasted_iota(jnp.int32, (target_rows, experts), 1)
    picked = jnp.sum(jnp.where(expert_column == chosen_ids[:, None], logits, 0.0), axis=1)
    gate = jax.nn.sigmoid(picked)
    slot_index = chosen_ids * specialist_room + expert_slots[0]
    slot_column = lax.broadcasted_iota(jnp.int32, (target_rows, experts * specialist_room), 1)
    placing = (slot_column == slot_index[:, None]).astype(jnp.bfloat16)
    dispatched = jnp.einsum(
        "rp,rf->pf", placing, normed, preferred_element_type=jnp.float32
    ).astype(jnp.bfloat16)
    received = lax.all_to_all(dispatched, "expert", split_axis=0, concat_axis=0, tiled=True)
    first_weight = w_in[0]
    pre = jnp.dot(
        lax.all_gather(received, "mp", axis=1, tiled=True),
        first_weight,
        preferred_element_type=jnp.float32,
    )
    hidden = jax.nn.relu(pre).astype(jnp.bfloat16)
    block_out = jnp.dot(hidden, w_out[0], preferred_element_type=jnp.float32).astype(jnp.bfloat16)
    returned = lax.all_to_all(block_out, "expert", split_axis=0, concat_axis=0, tiled=True)
    row_terms = jnp.take(returned, slot_index, axis=0).astype(jnp.float32)
    expert_rows = lax.psum_scatter(
        row_terms.astype(jnp.bfloat16), "mp", scatter_dimension=1, tiled=True
    )
    result = mixed + gate[:, None] * expert_rows.astype(jnp.float32)
    return result.astype(jnp.bfloat16)


def solution(mesh):
    placed = (
        P("expert", "mp"),
        P(("expert", "mp"), None),
        P(("expert", "mp"), None),
        P("expert", None),
        P("expert", None),
        P("expert", "mp"),
        P("expert", "mp"),
        P("mp"),
        P("mp", None),
        P("expert", None),
        P("expert", None),
        P("expert", None, "mp"),
        P("expert", "mp", None),
    )
    return jax.shard_map(
        body, mesh=mesh, in_specs=placed, out_specs=P("expert", "mp"), check_vma=False
    )
```

profile of v0, /device:TPU:8, one launch (start us, length us, event | category | flops | bytes accessed | tf_op | source)
XLA Modules:
  0.0 653.1 jit_solution(8615272973895912360)
XLA Ops:
  6.5 1.7 copy.37
  8.3 12.7 %all-to-all-start = ((bf16[32,8,256]{2,0,1:T(8,128)(2,1)}), bf16[32,8,256]{2,0,1:T(8,128)(2,1)S(1)}, u32[]{:S(2)}, u32[]{:S(2)}) async-start(bf16[32,8,256]{2,0,1:T(8,128)(2,1)} %bitcast.44), calls=%async_computation | async-start | bytes 262144 | tf_op jit(solution)/shard_map/all_to_all | solution.py:26
  21.0 1.0 copy.18
  22.0 1.6 copy.38
  23.6 0.8 broadcast_compare_fusion
  24.4 7.2 %all-to-all-done = bf16[32,8,256]{2,0,1:T(8,128)(2,1)S(1)} async-done(((bf16[32,8,256]{2,0,1:T(8,128)(2,1)}), bf16[32,8,256]{2,0,1:T(8,128)(2,1)S(1)}, u32[]{:S(2)}, u32[]{:S(2)}) %all-to-all-start) | async-done | bytes 131104 | tf_op jit(solution)/shard_map/all_to_all | solution.py:26
  31.6 3.4 all-to-all-start.1
  35.0 0.0 all-gather.4.cloned.1.call-start
  35.1 0.2 reshape.112
  35.2 0.5 fusion.31
  35.7 1.2 fusion.7
  36.9 8.6 %all-to-all-done.1 = bf16[32,8,256]{2,0,1:T(8,128)(2,1)S(1)} async-done(((bf16[32,8,256]{2,0,1:T(8,128)(2,1)}), bf16[32,8,256]{2,0,1:T(8,128)(2,1)S(1)}, u32[]{:S(2)}, u32[]{:S(2)}) %all-to-all-start.1) | async-done | bytes 131104 | tf_op jit(solution)/shard_map/all_to_all | solution.py:27
  45.5 0.2 reshape.113
  45.7 1.0 convolution_convert_fusion.2
  46.8 0.0 all-gather.6.cloned.1.call-start
  46.8 0.7 all-gather.6.cloned.1.call-update
  47.6 64.0 %all-gather.4.cloned.1.call-done = bf16[256,2048]{0,1:T(8,128)(2,1)} async-done(((bf16[256,256]{0,1:T(8,128)(2,1)}), bf16[256,2048]{0,1:T(8,128)(2,1)}) %all-gather.4.cloned.1.call-update) | async-done | bytes 1048592 | tf_op jit(solution)/shard_map/all_gather | solution.py:47
  111.6 115.1 %all-gather.6.cloned.1.call-done = bf16[2048,512]{1,0:T(8,128)(2,1)} async-done(((bf16[32,512]{1,0:T(8,128)(2,1)}), bf16[2048,512]{1,0:T(8,128)(2,1)}) %all-gather.6.cloned.1.call-update) | async-done | bytes 2097168 | tf_op jit(solution)/shard_map/all_gather | solution.py:50
  226.7 2.7 multiply_reduce_fusion
  229.4 0.4 convolution_convert_fusion.3
  229.8 54.5 %all-reduce = (bf16[256]{0:T(256)(128)(2,1)S(1)}, bf16[256,64]{0,1:T(8,128)(2,1)S(1)}) all-reduce(bf16[256]{0:T(256)(128)(2,1)S(1)} %get-tuple-element.9, bf16[256,64]{0,1:T(8,128)(2,1)S(1)} %convolution_convert_fusion.3), channel_id=1, replica_groups=mesh['expert'=64,'mp'=8] {'mp'}, use_global_device_ids=true, to_apply=%region_4.5 | all-reduce | flops 16640 | bytes 66560 | tf_op jit(solution)/shard_map/psum | solution.py:58
  284.3 0.4 fusion.8
  284.8 24.3 %all_to_all.56 = bf16[64,8,512]{2,1,0:T(8,128)(2,1)} all-to-all(bf16[64,8,512]{2,1,0:T(8,128)(2,1)S(1)} %fusion.8), channel_id=1, replica_groups=mesh['expert'=64,'mp'=8] {'expert'}, dimensions={0} | all-to-all | bytes 1048576 | tf_op jit(solution)/shard_map/all_to_all | solution.py:76
  309.1 109.1 %all-gather.8.cloned.1.call-done = bf16[512,4096]{1,0:T(8,128)(2,1)} async-done(((bf16[512,512]{1,0:T(8,128)(2,1)}), bf16[512,4096]{1,0:T(8,128)(2,1)}) %all-gather.8.cloned.1.call-update) | async-done | bytes 4194320 | tf_op jit(solution)/shard_map/all_gather | solution.py:79
  418.2 9.3 %fusion.1 = bf16[64,8,4096]{2,1,0:T(8,128)(2,1)} fusion(bf16[1,256,4096]{2,1,0:T(8,128)(2,1)S(1)} %copy-done, bf16[512,4096]{1,0:T(8,128)(2,1)} %all-gather.8.cloned.1.call-done, bf16[1,4096,256]{2,1,0:T(8,128)(2,1)} %param.24), kind=kOutput, calls=%fused_computation.3 | convolution fusion | flops 2149842944 | bytes 12582912 | tf_op jit(solution)/shard_map/dot_general | solution.py:84
  427.5 9.1 %all-to-all-start.3 = ((bf16[64,8,4096]{2,1,0:T(8,128)(2,1)}), bf16[64,8,4096]{2,1,0:T(8,128)(2,1)}, u32[]{:S(2)}, u32[]{:S(2)}) async-start(bf16[64,8,4096]{2,1,0:T(8,128)(2,1)} %fusion.1), calls=%async_computation.3 | async-start | bytes 8388608 | tf_op jit(solution)/shard_map/all_to_all | solution.py:85
  436.7 0.2 reduce-scatter.2.cloned.1.call-start
  436.9 96.2 %all-to-all-done.3 = bf16[64,8,4096]{2,1,0:T(8,128)(2,1)} async-done(((bf16[64,8,4096]{2,1,0:T(8,128)(2,1)}), bf16[64,8,4096]{2,1,0:T(8,128)(2,1)}, u32[]{:S(2)}, u32[]{:S(2)}) %all-to-all-start.3) | async-done | bytes 4194336 | tf_op jit(solution)/shard_map/all_to_all | solution.py:85
  533.1 7.9 %gather_fusion = bf16[256,4096]{1,0:T(8,128)(2,1)} fusion(bf16[512,4096]{1,0:T(8,128)(2,1)} %bitcast.14, s32[1024]{0:T(1024)S(1)} %pad_clamp_fusion), kind=kCustom, calls=%fused_computation | custom fusion | bytes 4195328 | tf_op jit(solution)/shard_map/jit(_take)/gather | solution.py:86
  541.1 3.2 broadcast_select_fusion
  544.3 100.4 %reduce-scatter.2.cloned.1.call-done = bf16[256,512]{1,0:T(8,128)(2,1)} async-done(((bf16[256,4096]{1,0:T(8,128)(2,1)}), bf16[256,512]{1,0:T(8,128)(2,1)}) %reduce-scatter.2.cloned.1.call-update) | async-done | bytes 262160 | tf_op jit(solution)/shard_map/reduce_scatter | solution.py:87
  644.8 1.8 add_convert_fusion
  (24 shorter events, 0.2 us)
Async XLA Ops:
  6.5 411.6 %copy-start = (bf16[1,256,4096]{2,1,0:T(8,128)(2,1)S(1)}, bf16[1,256,4096]{2,1,0:T(8,128)(2,1)}, u32[]{:S(2)}) copy-start(bf16[1,256,4096]{2,1,0:T(8,128)(2,1)} %param.25) | copy-start | bytes 6291460
  8.3 23.4 %all-to-all-start = ((bf16[32,8,256]{2,0,1:T(8,128)(2,1)}), bf16[32,8,256]{2,0,1:T(8,128)(2,1)S(1)}, u32[]{:S(2)}, u32[]{:S(2)}) async-start(bf16[32,8,256]{2,0,1:T(8,128)(2,1)} %bitcast.44), calls=%async_computation | async-start | bytes 262144 | tf_op jit(solution)/shard_map/all_to_all | solution.py:26
  22.0 13.2 %copy-start.1 = (bf16[256,256]{0,1:T(8,128)(2,1)}, bf16[256,256]{0,1:T(8,128)(2,1)S(1)}, u32[]{:S(2)}) copy-start(bf16[256,256]{0,1:T(8,128)(2,1)S(1)} %copy.18) | copy-start | bytes 393220
  24.4 10.8 %copy-start.2 = (pred[256,256]{0,1:T(8,128)(4,1)}, pred[256,256]{0,1:T(8,128)(4,1)S(1)}, u32[]{:S(2)}) copy-start(pred[256,256]{0,1:T(8,128)(4,1)S(1)} %broadcast_compare_fusion) | copy-start | bytes 196612
  31.6 13.9 %all-to-all-start.1 = ((bf16[32,8,256]{2,0,1:T(8,128)(2,1)}), bf16[32,8,256]{2,0,1:T(8,128)(2,1)S(1)}, u32[]{:S(2)}, u32[]{:S(2)}) async-start(bf16[32,8,256]{2,0,1:T(8,128)(2,1)} %bitcast.45), calls=%async_computation.1 | async-start | bytes 262144 | tf_op jit(solution)/shard_map/all_to_all | solution.py:27
  35.0 76.6 %all-gather.4.cloned.1.call-start = ((), (), s32[]{:S(2)}) async-start(), calls=%async_computation.5 | async-start | bytes 1179648 | tf_op jit(solution)/shard_map/all_gather | solution.py:47
  45.7 1.9 copy-start.4
  45.7 1.9 copy-start.6
  46.8 179.9 %all-gather.6.cloned.1.call-start = ((), (), s32[]{:S(2)}) async-start(), calls=%async_computation.6 | async-start | bytes 2129920 | tf_op jit(solution)/shard_map/all_gather | solution.py:50
  47.5 370.6 %all-gather.8.cloned.1.call-start = ((), (), s32[]{:S(2)}) async-start(), calls=%async_computation.7 | async-start | bytes 4718592 | tf_op jit(solution)/shard_map/all_gather | solution.py:79
  47.6 181.8 %copy-start.3 = (bf16[512,64]{0,1:T(8,128)(2,1)S(1)}, bf16[512,64]{0,1:T(8,128)(2,1)}, u32[]{:S(2)}) copy-start(bf16[512,64]{0,1:T(8,128)(2,1)} %param.21) | copy-start | bytes 196612
  47.6 181.8 %copy-start.5 = (f32[512]{0:T(512)S(1)}, f32[512]{0:T(512)}, u32[]{:S(2)}) copy-start(f32[512]{0:T(512)} %param.20) | copy-start | bytes 6148
  427.5 105.6 %all-to-all-start.3 = ((bf16[64,8,4096]{2,1,0:T(8,128)(2,1)}), bf16[64,8,4096]{2,1,0:T(8,128)(2,1)}, u32[]{:S(2)}, u32[]{:S(2)}) async-start(bf16[64,8,4096]{2,1,0:T(8,128)(2,1)} %fusion.1), calls=%async_computation.3 | async-start | bytes 8388608 | tf_op jit(solution)/shard_map/all_to_all | solution.py:85
  436.7 208.1 %reduce-scatter.2.cloned.1.call-start = ((), (), s32[]{:S(2)}) async-start(), calls=%async_computation.8 | async-start | bytes 2359296 | tf_op jit(solution)/shard_map/reduce_scatter | solution.py:87
Sparse Core Ops, SparseCore 0:
  46.9 64.6 all-gather.3
  113.8 112.8 all-gather.5
  309.2 108.9 all-gather.7
  544.4 100.3 reduce-scatter.1
where the time goes:
time: 654 us; the launch traced here: 653 us
  waiting for transfers between devices  501 us (77%)
  blocking collectives  78.8 us (12%)
  starting transfers between devices  25.6 us (4%)
  matrix products  15.6 us (2%)
  between operations  13.3 us (2%)
  local copies, waits for them, and re-layouts  12.6 us (2%)
    all_gather x1, waiting for transfers between devices, body(): lax.all_gather(out_proj, 'expert', axis=0, tiled=True)  115 us
    all_gather x1, waiting for transfers between devices, body(): lax.all_gather(received, 'mp', axis=1, tiled=True)  109 us
    reduce_scatter x1, waiting for transfers between devices, body(): lax.psum_scatter(row_terms.astype(jnp.bfloat16), 'mp', scatter_dimension=...  100 us
    all_to_all x1, waiting for transfers between devices, body(): lax.all_to_all(block_out, 'expert', split_axis=0, concat_axis=0, tiled=True)  96.2 us
    all_gather x1, waiting for transfers between devices, body(): attended_all = lax.all_gather(attended, 'mp', axis=1, tiled=True)  64 us
    psum x1, blocking collectives, body(): lax.psum(part_squares.astype(jnp.bfloat16), 'mp').astype(jnp.float32)  54.5 us
    all_to_all x1, blocking collectives, body(): lax.all_to_all(dispatched, 'expert', split_axis=0, concat_axis=0, tiled=T...  24.3 us
  transfers between devices with their start and end apart: 7, of which 7 were waited for; matrix products, arithmetic and copies ran while one was open for 1% of the time, Pallas kernels for 0%

commit v1 on v0

v1 whole, which is shorter than its diff:
```python
import jax
import jax.numpy as jnp
from jax import lax
from jax.sharding import Mesh, PartitionSpec as P

D = 4096
HEAD_DIM = 64
ROWS = 256
ROOM = 8
EXPERT = ("zl", "y", "c")
MP = ("x", "zh")
BF16 = jnp.bfloat16
F32 = jnp.float32


def exchange(blocks, axes):
    return lax.all_to_all(blocks, axes, split_axis=0, concat_axis=0, tiled=True)


def spread(block, axes, count):
    return exchange(jnp.broadcast_to(block[None], (count,) + block.shape), axes)


def dot32(left, right, dims=(((1,), (0,)), ((), ()))):
    return lax.dot_general(left, right, dims, preferred_element_type=F32)


def body(
    queries,
    src_keys,
    src_values,
    tgt_doc,
    src_doc,
    hidden_in,
    out_proj,
    norm_gain,
    router,
    expert_ids,
    expert_slots,
    w_in,
    w_out,
):
    width = queries.shape[1]
    heads = width // HEAD_DIM
    both = jnp.stack([src_keys.reshape(32, 8, width), src_values.reshape(32, 8, width)])
    both = exchange(both.transpose(2, 0, 1, 3), MP)
    keys = both[:, 0].reshape(ROWS, heads, HEAD_DIM)
    values = both[:, 1].reshape(ROWS, heads, HEAD_DIM)
    first = exchange(w_in[0].reshape(4, 1024, 256), "x")
    second = exchange(w_out[0].reshape(256, 4, 1024).transpose(1, 0, 2), "x")
    proj = spread(out_proj, EXPERT, 64).reshape(2048, 512)

    query_heads = queries.reshape(ROWS, heads, HEAD_DIM)
    scores = jnp.einsum("thd,shd->hts", query_heads, keys, preferred_element_type=F32)
    scores = scores * (1.0 / HEAD_DIM**0.5)
    same = tgt_doc[0][:, None] == src_doc[0][None, :]
    scores = jnp.where(same[None], scores, F32(-1e30))
    peak = jnp.max(scores, axis=2, keepdims=True)
    expo = jnp.exp(scores - peak)
    weights = (expo / jnp.sum(expo, axis=2, keepdims=True)).astype(BF16)
    attended = jnp.einsum("hts,shd->thd", weights, values, preferred_element_type=F32)
    attended = attended.astype(BF16).reshape(ROWS, width)
    attended = spread(attended, MP, 8)
    attended = attended.transpose(1, 0, 2).reshape(ROWS, 8 * width)
    mixed = hidden_in.astype(F32) + dot32(attended, proj)
    gated = mixed * norm_gain

    chosen = expert_ids[0]
    slot = chosen * ROOM + expert_slots[0]
    placing = (lax.broadcasted_iota(jnp.int32, (ROWS, 512), 1) == slot[:, None]).astype(BF16)
    placed = dot32(placing, gated.astype(BF16), (((0,), (0,)), ((), ()))).astype(BF16)
    placed = placed.reshape(1, 64, ROOM, 512)
    received = exchange(
        jnp.broadcast_to(placed, (2, 64, ROOM, 512)).reshape(128, ROOM, 512), ("zh",) + EXPERT
    )
    received = received.reshape(2, 512, 512)

    router32 = router.astype(F32)
    logits = jnp.dot(gated, router32, precision=lax.Precision.HIGHEST)
    column = lax.broadcasted_iota(jnp.int32, (ROWS, 64), 1)
    picked = jnp.sum(jnp.where(column == chosen[:, None], logits, 0.0), axis=1)
    stats = jnp.stack([jnp.sum(mixed * mixed, axis=1), picked])
    stats = jnp.sum(lax.all_gather(stats, MP, axis=0), axis=0)
    inverse_rms = lax.rsqrt(stats[0] / D + 1e-06)
    factor = jax.nn.sigmoid(stats[1] * inverse_rms) * inverse_rms

    first = first.reshape(4, 2, 512, 256)
    pre = jnp.stack(
        [(dot32(received[0], first[i, 0]) + dot32(received[1], first[i, 1])).astype(BF16) for i in range(4)]
    )
    pre = exchange(pre, "x")
    hidden = jax.nn.relu(jnp.sum(pre.astype(F32), axis=0)).astype(BF16)
    hidden = spread(hidden, "x", 4)
    result = sum(dot32(hidden[i], second[i]) for i in range(4)).astype(BF16)
    result = result.reshape(64, ROOM, 2, 512).transpose(2, 0, 1, 3).reshape(128, ROOM, 512)
    returned = exchange(result, ("zh",) + EXPERT).reshape(2, 512, 512)
    rows = dot32(placing, returned[0]) + dot32(placing, returned[1])
    return (mixed + factor[:, None] * rows).astype(BF16)


def solution(mesh):
    fine = Mesh(mesh.devices.reshape(4, 8, 2, 4, 2), EXPERT + MP)
    placed = (
        P(EXPERT, MP),
        P(EXPERT + MP, None),
        P(EXPERT + MP, None),
        P(EXPERT, None),
        P(EXPERT, None),
        P(EXPERT, MP),
        P(EXPERT, MP),
        P(MP),
        P(MP, None),
        P(EXPERT, None),
        P(EXPERT, None),
        P(EXPERT, None, MP),
        P(EXPERT, MP, None),
    )
    return jax.shard_map(
        body, mesh=fine, in_specs=placed, out_specs=P(EXPERT, MP), check_vma=False
    )
```

time: 654 us -> 330 us (0.50)
  the two profiles are of different devices: /device:TPU:8 before, /device:TPU:96 now
where the time goes in v1:
time: 330 us; the launch traced here: 329 us
  blocking collectives  200 us (61%)
  waiting for transfers between devices  72.7 us (22%)
  starting transfers between devices  33.7 us (10%)
  matrix products  10.3 us (3%)
  local copies, waits for them, and re-layouts  9.72 us (3%)
    all_to_all x4, blocking collectives, exchange(): return lax.all_to_all(blocks, axes, split_axis=0, concat_axis=0, tiled=True)  142 us
    all_to_all x5, waiting for transfers between devices, exchange(): return lax.all_to_all(blocks, axes, split_axis=0, concat_axis=0, tiled=True)  72.7 us
    all_gather x1, blocking collectives, body(): stats = jnp.sum(lax.all_gather(stats, MP, axis=0), axis=0)  57.9 us
    all_to_all x5, starting transfers between devices, exchange(): return lax.all_to_all(blocks, axes, split_axis=0, concat_axis=0, tiled=True)  33.7 us
    dot_general x16, matrix products, dot32(): return lax.dot_general(left, right, dims, preferred_element_type=F32)  8.81 us
    unnamed x24, local copies, waits for them, and re-layouts  7.13 us
  transfers between devices with their start and end apart: 5, of which 4 were waited for; matrix products, arithmetic and copies ran while one was open for 3% of the time, Pallas kernels for 0%

profile of v1, /device:TPU:96, one launch (start us, length us, event | category | flops | bytes accessed | tf_op | source)
XLA Modules:
  0.0 329.4 jit_solution(12815266806717177289)
XLA Ops:
  0.0 1.0 copy.60
  1.0 0.9 copy.61
  2.0 0.8 copy.48
  2.7 11.8 %all-to-all-start = ((bf16[8,2,32,256]{3,2,1,0:T(8,128)(2,1)}), bf16[8,2,32,256]{3,2,1,0:T(8,128)(2,1)S(1)}, u32[]{:S(2)}, u32[]{:S(2)}) async-start(bf16[8,2,32,256]{3,2,1,0:T(8,128)(2,1)} %copy.48), calls=%async_computation | async-start | bytes 524288 | tf_op jit(solution)/shard_map/all_to_all | solution.py:17
  14.8 13.8 %all-to-all-done = bf16[8,2,32,256]{3,2,1,0:T(8,128)(2,1)S(1)} async-done(((bf16[8,2,32,256]{3,2,1,0:T(8,128)(2,1)}), bf16[8,2,32,256]{3,2,1,0:T(8,128)(2,1)S(1)}, u32[]{:S(2)}, u32[]{:S(2)}) %all-to-all-start) | async-done | bytes 262176 | tf_op jit(solution)/shard_map/all_to_all | solution.py:17
  28.7 0.5 fusion.43
  29.7 0.4 convolution_convert_fusion.1
  30.1 30.0 %all_to_all.45 = bf16[8,256,256]{1,2,0:T(8,128)(2,1)} all-to-all(bf16[8,256,256]{1,2,0:T(8,128)(2,1)S(1)} %broadcast_in_dim.51), channel_id=1, replica_groups=mesh['zl'=4,'y'=8,'c'=2,'x'=4,'zh'=2] {'x','zh'}, dimensions={0} | all-to-all | bytes 2097152 | tf_op jit(solution)/shard_map/all_to_all | solution.py:17
  60.4 59.1 %all_to_all.46 = bf16[64,32,512]{2,1,0:T(8,128)(2,1)} all-to-all(bf16[64,32,512]{2,1,0:T(8,128)(2,1)S(1)} %broadcast_in_dim.52), channel_id=1, replica_groups=mesh['zl'=4,'y'=8,'c'=2,'x'=4,'zh'=2] {'zl','y','c'}, dimensions={0} | all-to-all | bytes 4194304 | tf_op jit(solution)/shard_map/all_to_all | solution.py:17
  119.5 3.7 %all-to-all-start.4 = ((bf16[4,1024,256]{2,1,0:T(8,128)(2,1)}), bf16[4,1024,256]{2,1,0:T(8,128)(2,1)S(1)}, u32[]{:S(2)}, u32[]{:S(2)}) async-start(bf16[4,1024,256]{2,1,0:T(8,128)(2,1)} %bitcast.145), calls=%async_computation.4 | async-start | bytes 4194304 | tf_op jit(solution)/shard_map/all_to_all | solution.py:17
  123.3 2.7 multiply_reduce_fusion
  126.1 0.4 fusion.5
  126.5 22.5 %all-to-all-done.4 = bf16[4,1024,256]{2,1,0:T(8,128)(2,1)S(1)} async-done(((bf16[4,1024,256]{2,1,0:T(8,128)(2,1)}), bf16[4,1024,256]{2,1,0:T(8,128)(2,1)S(1)}, u32[]{:S(2)}, u32[]{:S(2)}) %all-to-all-start.4) | async-done | bytes 2097184 | tf_op jit(solution)/shard_map/all_to_all | solution.py:17
  149.1 36.4 %all_to_all.47 = bf16[128,8,512]{2,1,0:T(8,128)(2,1)S(1)} all-to-all(bf16[128,8,512]{2,1,0:T(8,128)(2,1)S(1)} %bitcast.143), channel_id=1, replica_groups=mesh['zl'=4,'y'=8,'c'=2,'x'=4,'zh'=2] {'zh','zl','y','c'}, dimensions={0} | all-to-all | bytes 2097152 | tf_op jit(solution)/shard_map/all_to_all | solution.py:17
  187.9 1.1 pad_maximum_fusion
  189.0 3.5 %all-to-all-start.5 = ((bf16[4,512,256]{2,1,0:T(8,128)(2,1)}), bf16[4,512,256]{2,1,0:T(8,128)(2,1)S(1)}, u32[]{:S(2)}, u32[]{:S(2)}) async-start(bf16[4,512,256]{2,1,0:T(8,128)(2,1)} %pad_maximum_fusion), calls=%async_computation.5 | async-start | bytes 2097152 | tf_op jit(solution)/shard_map/all_to_all | solution.py:17
  192.5 4.1 %copy.53 = bf16[1,256,4096]{1,2,0:T(8,128)(2,1)} copy(bf16[1,256,4096]{2,1,0:T(8,128)(2,1)} %param.25) | data formatting | bytes 4194304 | tf_op args[12]
  196.6 11.7 %all-to-all-done.5 = bf16[4,512,256]{2,1,0:T(8,128)(2,1)S(1)} async-done(((bf16[4,512,256]{2,1,0:T(8,128)(2,1)}), bf16[4,512,256]{2,1,0:T(8,128)(2,1)S(1)}, u32[]{:S(2)}, u32[]{:S(2)}) %all-to-all-start.5) | async-done | bytes 1048608 | tf_op jit(solution)/shard_map/all_to_all | solution.py:17
  208.3 1.0 copy-done.1
  209.3 3.6 %all-to-all-start.7 = ((bf16[4,256,1024]{1,2,0:T(8,128)(2,1)}), bf16[4,256,1024]{1,2,0:T(8,128)(2,1)S(1)}, u32[]{:S(2)}, u32[]{:S(2)}) async-start(bf16[4,256,1024]{1,2,0:T(8,128)(2,1)} %bitcast.142), calls=%async_computation.7 | async-start | bytes 4194304 | tf_op jit(solution)/shard_map/all_to_all | solution.py:17
  212.9 1.4 convert_reduce_fusion
  214.3 24.8 %all-to-all-done.7 = bf16[4,256,1024]{1,2,0:T(8,128)(2,1)S(1)} async-done(((bf16[4,256,1024]{1,2,0:T(8,128)(2,1)}), bf16[4,256,1024]{1,2,0:T(8,128)(2,1)S(1)}, u32[]{:S(2)}, u32[]{:S(2)}) %all-to-all-start.7) | async-done | bytes 2097184 | tf_op jit(solution)/shard_map/all_to_all | solution.py:17
  239.2 16.5 %all_to_all.48 = bf16[4,512,256]{2,1,0:T(8,128)(2,1)S(1)} all-to-all(bf16[4,512,256]{2,1,0:T(8,128)(2,1)S(1)} %broadcast_in_dim.56), channel_id=1, replica_groups=mesh['zl'=4,'y'=8,'c'=2,'x'=4,'zh'=2] {'x'}, dimensions={0} | all-to-all | bytes 2097152 | tf_op jit(solution)/shard_map/all_to_all | solution.py:17
  255.7 0.5 fusion.19
  256.1 0.5 fusion.20
  256.6 0.5 fusion.21
  257.1 0.5 add_convert_fusion
  257.6 1.1 copy.58
  258.6 11.0 %all-to-all-start.8 = ((bf16[128,8,512]{2,1,0:T(8,128)(2,1)}), bf16[128,8,512]{2,1,0:T(8,128)(2,1)S(1)}, u32[]{:S(2)}, u32[]{:S(2)}) async-start(bf16[128,8,512]{2,1,0:T(8,128)(2,1)} %bitcast.47), calls=%async_computation.8 | async-start | bytes 2097152 | tf_op jit(solution)/shard_map/all_to_all | solution.py:17
  269.6 0.4 fusion.17
  270.1 57.9 %all-gather.1 = f32[8,2,256]{2,1,0:T(2,128)S(1)} all-gather(f32[1,2,256]{2,1,0:T(2,128)S(1)} %maximum_bitcast_fusion.1), channel_id=2, replica_groups=mesh['zl'=4,'y'=8,'c'=2,'x'=4,'zh'=2] {'x','zh'}, dimensions={0}, use_global_device_ids=true | all-gather | bytes 18432 | tf_op jit(solution)/shard_map/all_gather | solution.py:83
  328.3 1.1 fusion.12
  (46 shorter events, 4.1 us)
Async XLA Ops:
  0.0 269.6 %copy-start = (bf16[512,64]{0,1:T(8,128)(2,1)S(1)}, bf16[512,64]{0,1:T(8,128)(2,1)}, u32[]{:S(2)}) copy-start(bf16[512,64]{0,1:T(8,128)(2,1)} %param.21) | copy-start | bytes 196612
  0.0 14.6 %copy-start.2 = (bf16[256,256]{1,0:T(8,128)(2,1)S(1)}, bf16[256,256]{1,0:T(8,128)(2,1)}, u32[]{:S(2)}) copy-start(bf16[256,256]{1,0:T(8,128)(2,1)} %param.13) | copy-start | bytes 393220
  0.0 14.7 %copy-start.7 = (s32[1,256]{1,0:T(1,128)S(1)}, s32[1,256]{1,0:T(1,128)}, u32[]{:S(2)}) copy-start(s32[1,256]{1,0:T(1,128)} %param.17) | copy-start | bytes 3076
  0.0 14.7 %copy-start.6 = (s32[1,256]{1,0:T(1,128)S(1)}, s32[1,256]{1,0:T(1,128)}, u32[]{:S(2)}) copy-start(s32[1,256]{1,0:T(1,128)} %param.16) | copy-start | bytes 3076
  2.7 25.8 %all-to-all-start = ((bf16[8,2,32,256]{3,2,1,0:T(8,128)(2,1)}), bf16[8,2,32,256]{3,2,1,0:T(8,128)(2,1)S(1)}, u32[]{:S(2)}, u32[]{:S(2)}) async-start(bf16[8,2,32,256]{3,2,1,0:T(8,128)(2,1)} %copy.48), calls=%async_computation | async-start | bytes 524288 | tf_op jit(solution)/shard_map/all_to_all | solution.py:17
  30.0 30.1 %copy-start.3 = (bf16[32,512]{1,0:T(8,128)(2,1)S(1)}, bf16[32,512]{1,0:T(8,128)(2,1)}, u32[]{:S(2)}) copy-start(bf16[32,512]{1,0:T(8,128)(2,1)} %param.19) | copy-start | bytes 98308
  119.5 3.8 %copy-start.5 = (s32[1,256]{1,0:T(1,128)S(1)}, s32[1,256]{1,0:T(1,128)}, u32[]{:S(2)}) copy-start(s32[1,256]{1,0:T(1,128)} %param.22) | copy-start | bytes 3076
  119.5 3.8 %copy-start.8 = (s32[1,256]{1,0:T(1,128)S(1)}, s32[1,256]{1,0:T(1,128)}, u32[]{:S(2)}) copy-start(s32[1,256]{1,0:T(1,128)} %param.23) | copy-start | bytes 3076
  119.5 3.8 %copy-start.9 = (bf16[256,512]{1,0:T(8,128)(2,1)S(1)}, bf16[256,512]{1,0:T(8,128)(2,1)}, u32[]{:S(2)}) copy-start(bf16[256,512]{1,0:T(8,128)(2,1)} %param.18) | copy-start | bytes 786436
  119.5 29.5 %all-to-all-start.4 = ((bf16[4,1024,256]{2,1,0:T(8,128)(2,1)}), bf16[4,1024,256]{2,1,0:T(8,128)(2,1)S(1)}, u32[]{:S(2)}, u32[]{:S(2)}) async-start(bf16[4,1024,256]{2,1,0:T(8,128)(2,1)} %bitcast.145), calls=%async_computation.4 | async-start | bytes 4194304 | tf_op jit(solution)/shard_map/all_to_all | solution.py:17
  123.3 2.7 copy-start.4
  189.0 19.3 %all-to-all-start.5 = ((bf16[4,512,256]{2,1,0:T(8,128)(2,1)}), bf16[4,512,256]{2,1,0:T(8,128)(2,1)S(1)}, u32[]{:S(2)}, u32[]{:S(2)}) async-start(bf16[4,512,256]{2,1,0:T(8,128)(2,1)} %pad_maximum_fusion), calls=%async_computation.5 | async-start | bytes 2097152 | tf_op jit(solution)/shard_map/all_to_all | solution.py:17
  208.3 1.0 copy-start.1
  209.3 29.8 %all-to-all-start.7 = ((bf16[4,256,1024]{1,2,0:T(8,128)(2,1)}), bf16[4,256,1024]{1,2,0:T(8,128)(2,1)S(1)}, u32[]{:S(2)}, u32[]{:S(2)}) async-start(bf16[4,256,1024]{1,2,0:T(8,128)(2,1)} %bitcast.142), calls=%async_computation.7 | async-start | bytes 4194304 | tf_op jit(solution)/shard_map/all_to_all | solution.py:17
  258.6 69.3 %all-to-all-start.8 = ((bf16[128,8,512]{2,1,0:T(8,128)(2,1)}), bf16[128,8,512]{2,1,0:T(8,128)(2,1)S(1)}, u32[]{:S(2)}, u32[]{:S(2)}) async-start(bf16[128,8,512]{2,1,0:T(8,128)(2,1)} %bitcast.47), calls=%async_computation.8 | async-start | bytes 2097152 | tf_op jit(solution)/shard_map/all_to_all | solution.py:17

commit v2 on v1

--- a/solution.py
+++ b/solution.py
@@ -19,6 +19,12 @@
 
 def spread(block, axes, count):
     return exchange(jnp.broadcast_to(block[None], (count,) + block.shape), axes)
+
+
+def shift(block, places):
+    if places == 0:
+        return block
+    return lax.ppermute(block, "x", [(i, (i + places) % 4) for i in range(4)])
 
 
 def dot32(left, right, dims=(((1,), (0,)), ((), ()))):
@@ -46,9 +52,17 @@
     both = exchange(both.transpose(2, 0, 1, 3), MP)
     keys = both[:, 0].reshape(ROWS, heads, HEAD_DIM)
     values = both[:, 1].reshape(ROWS, heads, HEAD_DIM)
-    first = exchange(w_in[0].reshape(4, 1024, 256), "x")
-    second = exchange(w_out[0].reshape(256, 4, 1024).transpose(1, 0, 2), "x")
-    proj = spread(out_proj, EXPERT, 64).reshape(2048, 512)
+    x = lax.axis_index("x")
+    first = [
+        shift(lax.dynamic_slice(w_in[0], (1024 * ((x + k) % 4), 0), (1024, 256)), k)
+        for k in range(4)
+    ]
+    half = lax.all_gather(out_proj, "zl", axis=0)
+    half = lax.all_gather(half, "y", axis=0)
+    other = lax.ppermute(half, "c", [(0, 1), (1, 0)])
+    low = lax.axis_index("c") == 0
+    proj = jnp.stack([jnp.where(low, half, other), jnp.where(low, other, half)])
+    proj = proj.transpose(2, 1, 0, 3, 4).reshape(2048, 512)
 
     query_heads = queries.reshape(ROWS, heads, HEAD_DIM)
     scores = jnp.einsum("thd,shd->hts", query_heads, keys, preferred_element_type=F32)
@@ -74,24 +88,30 @@
         jnp.broadcast_to(placed, (2, 64, ROOM, 512)).reshape(128, ROOM, 512), ("zh",) + EXPERT
     )
     received = received.reshape(2, 512, 512)
+    w_out, stat_mixed, placed = lax.optimization_barrier((w_out, mixed, placed))
+    second = [
+        shift(lax.dynamic_slice(w_out[0], (0, 1024 * ((x + k) % 4)), (256, 1024)), k)
+        for k in range(4)
+    ]
 
     router32 = router.astype(F32)
-    logits = jnp.dot(gated, router32, precision=lax.Precision.HIGHEST)
+    logits = jnp.dot(stat_mixed * norm_gain, router32, precision=lax.Precision.HIGHEST)
     column = lax.broadcasted_iota(jnp.int32, (ROWS, 64), 1)
     picked = jnp.sum(jnp.where(column == chosen[:, None], logits, 0.0), axis=1)
-    stats = jnp.stack([jnp.sum(mixed * mixed, axis=1), picked])
-    stats = jnp.sum(lax.all_gather(stats, MP, axis=0), axis=0)
+    stats = jnp.stack([jnp.sum(stat_mixed * stat_mixed, axis=1), picked])
+    stats = stats + lax.ppermute(stats, "zh", [(0, 1), (1, 0)])
+    stats = stats + lax.ppermute(stats, "x", [(0, 1), (1, 0), (2, 3), (3, 2)])
+    stats = stats + lax.ppermute(stats, "x", [(0, 3), (3, 0), (1, 2), (2, 1)])
     inverse_rms = lax.rsqrt(stats[0] / D + 1e-06)
     factor = jax.nn.sigmoid(stats[1] * inverse_rms) * inverse_rms
 
-    first = first.reshape(4, 2, 512, 256)
-    pre = jnp.stack(
-        [(dot32(received[0], first[i, 0]) + dot32(received[1], first[i, 1])).astype(BF16) for i in range(4)]
-    )
-    pre = exchange(pre, "x")
-    hidden = jax.nn.relu(jnp.sum(pre.astype(F32), axis=0)).astype(BF16)
-    hidden = spread(hidden, "x", 4)
-    result = sum(dot32(hidden[i], second[i]) for i in range(4)).astype(BF16)
+    pre = [
+        (dot32(received[0], first[k][:512]) + dot32(received[1], first[k][512:])).astype(BF16)
+        for k in range(4)
+    ]
+    pre = sum(shift(pre[k], -k).astype(F32) for k in range(4))
+    hidden = jax.nn.relu(pre).astype(BF16)
+    result = sum(dot32(shift(hidden, k), second[k]) for k in range(4)).astype(BF16)
     result = result.reshape(64, ROOM, 2, 512).transpose(2, 0, 1, 3).reshape(128, ROOM, 512)
     returned = exchange(result, ("zh",) + EXPERT).reshape(2, 512, 512)
     rows = dot32(placing, returned[0]) + dot32(placing, returned[1])

time: 330 us -> 249 us (0.75)
  blocking collectives: 200 us -> 16.2 us
  starting transfers between devices: 33.7 us -> 89.5 us
  waiting for transfers between devices: 72.7 us -> 93.8 us
  between operations: 0.35 us -> 14 us
  matrix products: 10.3 us -> 20.2 us
    all_to_all x4 -> x0, blocking collectives: 142 us -> none  [exchange(): return lax.all_to_all(blocks, axes, split_axis=0, concat_axis=0, tiled=True)]
    ppermute x0 -> x16, waiting for transfers between devices: none -> 56.1 us  [the longest x12 26.7 us: shift(): return lax.ppermute(block, 'x', [(i, (i + places) % 4) for i in range(4)])]
    ppermute x0 -> x16, starting transfers between devices: none -> 51.5 us  [the longest x12 37 us: shift(): return lax.ppermute(block, 'x', [(i, (i + places) % 4) for i in range(4)])]
    all_to_all x5 -> x4, waiting for transfers between devices: 72.7 us -> 27 us  [exchange(): return lax.all_to_all(blocks, axes, split_axis=0, concat_axis=0, tiled=True)]
    all_gather x1, blocking collectives: 57.9 us -> 16.2 us  [body(): half = lax.all_gather(out_proj, 'zl', axis=0)]
    all_gather x0 -> x1, waiting for transfers between devices: none -> 10.6 us  [body(): half = lax.all_gather(half, 'y', axis=0)]
    dot_general x16, matrix products: 8.81 us -> 18.6 us  [dot32(): return lax.dot_general(left, right, dims, preferred_element_type=F32)]
    unnamed x24 -> x19, local copies, waits for them, and re-layouts: 7.13 us -> 2 us
  transfers between devices with their start and end apart: 5 -> 21, of which waited for: 4 -> 13; matrix products, arithmetic and copies ran while one was open for 3% -> 11% of each run, Pallas kernels for 0% -> 0%
where the time goes in v2:
time: 249 us; the launch traced here: 247 us
  waiting for transfers between devices  93.8 us (38%)
  starting transfers between devices  89.5 us (36%)
  matrix products  20.2 us (8%)
  blocking collectives  16.2 us (7%)
  between operations  14 us (6%)
  local copies, waits for them, and re-layouts  11.4 us (5%)
    all_to_all x4, starting transfers between devices, exchange(): return lax.all_to_all(blocks, axes, split_axis=0, concat_axis=0, tiled=True)  37.9 us
    ppermute x12, starting transfers between devices, shift(): return lax.ppermute(block, 'x', [(i, (i + places) % 4) for i in range(4)])  37 us
    all_to_all x4, waiting for transfers between devices, exchange(): return lax.all_to_all(blocks, axes, split_axis=0, concat_axis=0, tiled=True)  27 us
    ppermute x12, waiting for transfers between devices, shift(): return lax.ppermute(block, 'x', [(i, (i + places) % 4) for i in range(4)])  26.7 us
    ppermute x1, waiting for transfers between devices, body(): stats = stats + lax.ppermute(stats, 'zh', [(0, 1), (1, 0)])  20.3 us
    dot_general x16, matrix products, dot32(): return lax.dot_general(left, right, dims, preferred_element_type=F32)  18.6 us
    all_gather x1, blocking collectives, body(): half = lax.all_gather(out_proj, 'zl', axis=0)  16.2 us
    all_gather x1, waiting for transfers between devices, body(): half = lax.all_gather(half, 'y', axis=0)  10.6 us
  transfers between devices with their start and end apart: 21, of which 13 were waited for; matrix products, arithmetic and copies ran while one was open for 11% of the time, Pallas kernels for 0%

profile of v2, /device:TPU:96, one launch (start us, length us, event | category | flops | bytes accessed | tf_op | source)
XLA Modules:
  0.0 247.1 jit_solution(8588764697788350632)
XLA Ops:
  6.6 16.2 %all-gather = bf16[128,512]{1,0:T(8,128)(2,1)} all-gather(bf16[32,512]{1,0:T(8,128)(2,1)} %param.19), channel_id=2, replica_groups=mesh['zl'=4,'y'=8,'c'=2,'x'=4,'zh'=2] {'zl'}, dimensions={0}, use_global_device_ids=true | all-gather | bytes 163840 | tf_op jit(solution)/shard_map/all_gather | solution.py:60
  25.5 10.1 %all-to-all-start = ((bf16[8,2,32,256]{3,2,1,0:T(8,128)(2,1)}), bf16[8,2,32,256]{3,2,1,0:T(8,128)(2,1)S(1)}, u32[]{:S(2)}, u32[]{:S(2)}) async-start(bf16[8,2,32,256]{3,2,1,0:T(8,128)(2,1)} %copy.41), calls=%async_computation | async-start | bytes 524288 | tf_op jit(solution)/shard_map/all_to_all | solution.py:17
  35.9 10.9 %all-to-all-done = bf16[8,2,32,256]{3,2,1,0:T(8,128)(2,1)S(1)} async-done(((bf16[8,2,32,256]{3,2,1,0:T(8,128)(2,1)}), bf16[8,2,32,256]{3,2,1,0:T(8,128)(2,1)S(1)}, u32[]{:S(2)}, u32[]{:S(2)}) %all-to-all-start) | async-done | bytes 262176 | tf_op jit(solution)/shard_map/all_to_all | solution.py:17
  49.4 4.2 %all-to-all-start.1 = ((bf16[8,256,256]{1,2,0:T(8,128)(2,1)}), bf16[8,256,256]{1,2,0:T(8,128)(2,1)}, u32[]{:S(2)}, u32[]{:S(2)}) async-start(bf16[8,256,256]{1,2,0:T(8,128)(2,1)} %broadcast_in_dim.40), calls=%async_computation.1 | async-start | bytes 2097152 | tf_op jit(solution)/shard_map/all_to_all | solution.py:17
  53.6 10.6 %all-gather.4.cloned.1.call-done = bf16[32,32,512]{2,1,0:T(8,128)(2,1)} async-done(((bf16[4,32,512]{2,1,0:T(8,128)(2,1)}), bf16[32,32,512]{2,1,0:T(8,128)(2,1)}) %all-gather.4.cloned.1.call-update) | async-done | bytes 1048592 | tf_op jit(solution)/shard_map/all_gather | solution.py:61
  66.2 2.8 %collective-permute-done = bf16[8,4,32,512]{3,2,1,0:T(8,128)(2,1)S(1)} collective-permute-done((bf16[8,4,32,512]{3,2,1,0:T(8,128)(2,1)}, bf16[8,4,32,512]{3,2,1,0:T(8,128)(2,1)S(1)}, u32[]{:S(2)}, u32[]{:S(2)}) %collective-permute-start) | collective-permute-done | bytes 1048608 | tf_op jit(solution)/shard_map/ppermute | solution.py:62
  70.8 9.6 %all-to-all-done.1 = bf16[8,256,256]{1,2,0:T(8,128)(2,1)} async-done(((bf16[8,256,256]{1,2,0:T(8,128)(2,1)}), bf16[8,256,256]{1,2,0:T(8,128)(2,1)}, u32[]{:S(2)}, u32[]{:S(2)}) %all-to-all-start.1) | async-done | bytes 1048608 | tf_op jit(solution)/shard_map/all_to_all | solution.py:17
  80.4 2.0 convolution_add_fusion
  83.9 9.8 %all-to-all-start.2 = ((bf16[128,8,512]{2,1,0:T(8,128)(2,1)}), bf16[128,8,512]{2,1,0:T(8,128)(2,1)S(1)}, u32[]{:S(2)}, u32[]{:S(2)}) async-start(bf16[128,8,512]{2,1,0:T(8,128)(2,1)} %bitcast.22), calls=%async_computation.2 | async-start | bytes 2097152 | tf_op jit(solution)/shard_map/all_to_all | solution.py:17
  93.8 2.5 %dynamic-slice_bitcast_fusion.5 = (bf16[1024,256]{1,0:T(8,128)(2,1)S(1)}, bf16[1024,256]{1,0:T(8,128)(2,1)}, bf16[1024,256]{1,0:T(8,128)(2,1)}) fusion(bf16[1,4096,256]{2,1,0:T(8,128)(2,1)} %param.24, s32[]{:T(128)S(6)} %select_n.71, s32[]{:T(128)S(6)} %select_n.75, s32[]{:T(128)S(6)} %select_n.73), kind=kLoop, calls=%fused_computation.44 | loop fusion | bytes 3145740 | tf_op jit(solution)/shard_map/dynamic_slice | solution.py:57
  96.3 2.7 %collective-permute-start.8 = (bf16[1024,256]{1,0:T(8,128)(2,1)}, bf16[1024,256]{1,0:T(8,128)(2,1)}, u32[]{:S(2)}, u32[]{:S(2)}) collective-permute-start(bf16[1024,256]{1,0:T(8,128)(2,1)} %get-tuple-element.13), channel_id=1, source_target_pairs={{0,6},{2,0},{4,2},{6,4},{1,7},{3,1},{5,3},{7,5},{8,14},{10,8},{12,... | collective-permute-start | bytes 1572872 | tf_op jit(solution)/shard_map/ppermute | solution.py:27
  99.0 2.4 collective-permute-start.6
  101.5 2.8 %collective-permute-start.4 = (bf16[1024,256]{1,0:T(8,128)(2,1)S(1)}, bf16[1024,256]{1,0:T(8,128)(2,1)}, u32[]{:S(2)}, u32[]{:S(2)}) collective-permute-start(bf16[1024,256]{1,0:T(8,128)(2,1)S(1)} %get-tuple-element.12), channel_id=1, source_target_pairs={{0,2},{2,4},{4,6},{6,0},{1,3},{3,5},{5,7},{7,1},{8,10},{10,12},{12... | collective-permute-start | bytes 1572872 | tf_op jit(solution)/shard_map/ppermute | solution.py:27
  104.3 2.3 dynamic-slice_bitcast_fusion.2
  106.6 5.8 %collective-permute-start.13 = (bf16[256,1024]{1,0:T(8,128)(2,1)}, bf16[256,1024]{1,0:T(8,128)(2,1)}, u32[]{:S(2)}, u32[]{:S(2)}) collective-permute-start(bf16[256,1024]{1,0:T(8,128)(2,1)} %get-tuple-element.11), channel_id=1, source_target_pairs={{0,4},{2,6},{4,0},{6,2},{1,5},{3,7},{5,1},{7,3},{8,12},{10,14},{12... | collective-permute-start | bytes 1572872 | tf_op jit(solution)/shard_map/ppermute | solution.py:27
  112.4 1.9 collective-permute-start.11
  114.4 6.5 %all-to-all-done.2 = bf16[128,8,512]{2,1,0:T(8,128)(2,1)S(1)} async-done(((bf16[128,8,512]{2,1,0:T(8,128)(2,1)}), bf16[128,8,512]{2,1,0:T(8,128)(2,1)S(1)}, u32[]{:S(2)}, u32[]{:S(2)}) %all-to-all-start.2) | async-done | bytes 1048608 | tf_op jit(solution)/shard_map/all_to_all | solution.py:17
  127.8 4.2 %collective-permute-start.7 = (bf16[512,256]{1,0:T(8,128)(2,1)S(1)}, bf16[512,256]{1,0:T(8,128)(2,1)S(1)}, u32[]{:S(2)}, u32[]{:S(2)}) collective-permute-start(bf16[512,256]{1,0:T(8,128)(2,1)S(1)} %fusion.11), channel_id=1, source_target_pairs={{0,4},{2,6},{4,0},{6,2},{1,5},{3,7},{5,1},{7,3},{8,12},{10,14},{12... | collective-permute-start | bytes 786440 | tf_op jit(solution)/shard_map/ppermute | solution.py:27
  134.5 3.1 %collective-permute-start.5 = (bf16[512,256]{1,0:T(8,128)(2,1)S(1)}, bf16[512,256]{1,0:T(8,128)(2,1)S(1)}, u32[]{:S(2)}, u32[]{:S(2)}) collective-permute-start(bf16[512,256]{1,0:T(8,128)(2,1)S(1)} %fusion.10), channel_id=1, source_target_pairs={{0,6},{2,0},{4,2},{6,4},{1,7},{3,1},{5,3},{7,5},{8,14},{10,8},{12,... | collective-permute-start | bytes 786440 | tf_op jit(solution)/shard_map/ppermute | solution.py:27
  140.1 16.6 %collective-permute-done.9 = bf16[512,256]{1,0:T(8,128)(2,1)S(1)} collective-permute-done((bf16[512,256]{1,0:T(8,128)(2,1)S(1)}, bf16[512,256]{1,0:T(8,128)(2,1)S(1)}, u32[]{:S(2)}, u32[]{:S(2)}) %collective-permute-start.9) | collective-permute-done | bytes 262176 | tf_op jit(solution)/shard_map/ppermute | solution.py:27
  156.7 2.6 %collective-permute-start.15 = (bf16[256,1024]{1,0:T(8,128)(2,1)S(1)}, bf16[256,1024]{1,0:T(8,128)(2,1)S(1)}, u32[]{:S(2)}, u32[]{:S(2)}) collective-permute-start(bf16[256,1024]{1,0:T(8,128)(2,1)S(1)} %get-tuple-element.10), channel_id=1, source_target_pairs={{0,6},{2,0},{4,2},{6,4},{1,7},{3,1},{5,3},{7,5},{8,14},{10,8},{12,... | collective-permute-start | bytes 1572872 | tf_op jit(solution)/shard_map/ppermute | solution.py:27
  159.3 2.0 collective-permute-done.7
  161.5 2.4 collective-permute-start.12
  167.4 5.1 %collective-permute-start.14 = (bf16[512,256]{1,0:T(8,128)(2,1)S(1)}, bf16[512,256]{1,0:T(8,128)(2,1)S(1)}, u32[]{:S(2)}, u32[]{:S(2)}) collective-permute-start(bf16[512,256]{1,0:T(8,128)(2,1)S(1)} %maximum_convert_fusion), channel_id=1, source_target_pairs={{0,6},{2,0},{4,2},{6,4},{1,7},{3,1},{5,3},{7,5},{8,14},{10,8},{12,... | collective-permute-start | bytes 786440 | tf_op jit(solution)/shard_map/ppermute | solution.py:27
  175.7 2.1 collective-permute-done.10
  179.2 4.4 %collective-permute-done.14 = bf16[512,256]{1,0:T(8,128)(2,1)S(1)} collective-permute-done((bf16[512,256]{1,0:T(8,128)(2,1)S(1)}, bf16[512,256]{1,0:T(8,128)(2,1)S(1)}, u32[]{:S(2)}, u32[]{:S(2)}) %collective-permute-start.14) | collective-permute-done | bytes 262176 | tf_op jit(solution)/shard_map/ppermute | solution.py:27
  185.1 13.7 %all-to-all-start.3 = ((bf16[128,8,512]{2,1,0:T(8,128)(2,1)}), bf16[128,8,512]{2,1,0:T(8,128)(2,1)S(1)}, u32[]{:S(2)}, u32[]{:S(2)}) async-start(bf16[128,8,512]{2,1,0:T(8,128)(2,1)} %bitcast.36), calls=%async_computation.3 | async-start | bytes 2097152 | tf_op jit(solution)/shard_map/all_to_all | solution.py:17
  199.4 6.8 %collective-permute-start.1 = (f32[2,256]{1,0:T(2,128)S(1)}, f32[2,256]{1,0:T(2,128)S(1)}, u32[]{:S(2)}, u32[]{:S(2)}) collective-permute-start(f32[2,256]{1,0:T(2,128)S(1)} %pad_maximum_fusion), channel_id=1, source_target_pairs={{0,1},{1,0},{2,3},{3,2},{4,5},{5,4},{6,7},{7,6},{8,9},{9,8},{10,11... | collective-permute-start | bytes 6152 | tf_op jit(solution)/shard_map/ppermute | solution.py:102
  206.3 20.3 %collective-permute-done.1 = f32[2,256]{1,0:T(2,128)S(1)} collective-permute-done((f32[2,256]{1,0:T(2,128)S(1)}, f32[2,256]{1,0:T(2,128)S(1)}, u32[]{:S(2)}, u32[]{:S(2)}) %collective-permute-start.1) | collective-permute-done | bytes 2080 | tf_op jit(solution)/shard_map/ppermute | solution.py:102
  228.5 3.6 %collective-permute-done.2 = f32[2,256]{1,0:T(2,128)S(1)} collective-permute-done((f32[2,256]{1,0:T(2,128)S(1)}, f32[2,256]{1,0:T(2,128)S(1)}, u32[]{:S(2)}, u32[]{:S(2)}) %collective-permute-start.2) | collective-permute-done | bytes 2080 | tf_op jit(solution)/shard_map/ppermute | solution.py:103
  232.1 3.9 %collective-permute-start.3 = (f32[2,256]{1,0:T(2,128)S(1)}, f32[2,256]{1,0:T(2,128)S(1)}, u32[]{:S(2)}, u32[]{:S(2)}) collective-permute-start(f32[2,256]{1,0:T(2,128)S(1)} %fusion.68), channel_id=1, source_target_pairs={{0,6},{6,0},{2,4},{4,2},{1,7},{7,1},{3,5},{5,3},{8,14},{14,8},{10,... | collective-permute-start | bytes 6152 | tf_op jit(solution)/shard_map/ppermute | solution.py:104
  236.0 2.8 %collective-permute-done.3 = f32[2,256]{1,0:T(2,128)S(1)} collective-permute-done((f32[2,256]{1,0:T(2,128)S(1)}, f32[2,256]{1,0:T(2,128)S(1)}, u32[]{:S(2)}, u32[]{:S(2)}) %collective-permute-start.3) | collective-permute-done | bytes 2080 | tf_op jit(solution)/shard_map/ppermute | solution.py:104
  (74 shorter events, 36.2 us)
Async XLA Ops:
  6.5 192.5 %copy-start = (bf16[512,64]{0,1:T(8,128)(2,1)S(1)}, bf16[512,64]{0,1:T(8,128)(2,1)}, u32[]{:S(2)}) copy-start(bf16[512,64]{0,1:T(8,128)(2,1)} %param.21) | copy-start | bytes 196612
  6.5 29.1 %copy-start.1 = (bf16[256,256]{1,0:T(8,128)(2,1)S(1)}, bf16[256,256]{1,0:T(8,128)(2,1)}, u32[]{:S(2)}) copy-start(bf16[256,256]{1,0:T(8,128)(2,1)} %param.13) | copy-start | bytes 393220
  6.5 29.2 %copy-start.4 = (s32[1,256]{1,0:T(1,128)S(1)}, s32[1,256]{1,0:T(1,128)}, u32[]{:S(2)}) copy-start(s32[1,256]{1,0:T(1,128)} %param.16) | copy-start | bytes 3076
  6.5 29.2 %copy-start.5 = (s32[1,256]{1,0:T(1,128)S(1)}, s32[1,256]{1,0:T(1,128)}, u32[]{:S(2)}) copy-start(s32[1,256]{1,0:T(1,128)} %param.17) | copy-start | bytes 3076
  6.5 57.7 %all-gather.4.cloned.1.call-start = ((), (), s32[]{:S(2)}) async-start(), calls=%async_computation.4 | async-start | bytes 1179648 | tf_op jit(solution)/shard_map/all_gather | solution.py:61
  25.5 21.3 %all-to-all-start = ((bf16[8,2,32,256]{3,2,1,0:T(8,128)(2,1)}), bf16[8,2,32,256]{3,2,1,0:T(8,128)(2,1)S(1)}, u32[]{:S(2)}, u32[]{:S(2)}) async-start(bf16[8,2,32,256]{3,2,1,0:T(8,128)(2,1)} %copy.41), calls=%async_computation | async-start | bytes 524288 | tf_op jit(solution)/shard_map/all_to_all | solution.py:17
  48.3 17.8 %copy-start.3 = (s32[1,256]{1,0:T(1,128)S(1)}, s32[1,256]{1,0:T(1,128)}, u32[]{:S(2)}) copy-start(s32[1,256]{1,0:T(1,128)} %param.22) | copy-start | bytes 3076
  48.3 17.8 %copy-start.6 = (s32[1,256]{1,0:T(1,128)S(1)}, s32[1,256]{1,0:T(1,128)}, u32[]{:S(2)}) copy-start(s32[1,256]{1,0:T(1,128)} %param.23) | copy-start | bytes 3076
  49.4 31.0 %all-to-all-start.1 = ((bf16[8,256,256]{1,2,0:T(8,128)(2,1)}), bf16[8,256,256]{1,2,0:T(8,128)(2,1)}, u32[]{:S(2)}, u32[]{:S(2)}) async-start(bf16[8,256,256]{1,2,0:T(8,128)(2,1)} %broadcast_in_dim.40), calls=%async_computation.1 | async-start | bytes 2097152 | tf_op jit(solution)/shard_map/all_to_all | solution.py:17
  64.2 4.8 %collective-permute-start = (bf16[8,4,32,512]{3,2,1,0:T(8,128)(2,1)}, bf16[8,4,32,512]{3,2,1,0:T(8,128)(2,1)S(1)}, u32[]{:S(2)}, u32[]{:S(2)}) collective-permute-start(bf16[8,4,32,512]{3,2,1,0:T(8,128)(2,1)} %bitcast.105), channel_id=1, source_target_pairs={{0,8},{8,0},{1,9},{9,1},{2,10},{10,2},{3,11},{11,3},{4,12},{12,4},... | collective-permute-start | bytes 3145736 | tf_op jit(solution)/shard_map/ppermute | solution.py:62
  70.6 9.8 %copy-start.7 = (bf16[256,512]{1,0:T(8,128)(2,1)S(1)}, bf16[256,512]{1,0:T(8,128)(2,1)}, u32[]{:S(2)}) copy-start(bf16[256,512]{1,0:T(8,128)(2,1)} %param.18) | copy-start | bytes 786436
  80.4 2.0 copy-start.2
  83.9 37.0 %all-to-all-start.2 = ((bf16[128,8,512]{2,1,0:T(8,128)(2,1)}), bf16[128,8,512]{2,1,0:T(8,128)(2,1)S(1)}, u32[]{:S(2)}, u32[]{:S(2)}) async-start(bf16[128,8,512]{2,1,0:T(8,128)(2,1)} %bitcast.22), calls=%async_computation.2 | async-start | bytes 2097152 | tf_op jit(solution)/shard_map/all_to_all | solution.py:17
  96.3 18.1 %collective-permute-start.8 = (bf16[1024,256]{1,0:T(8,128)(2,1)}, bf16[1024,256]{1,0:T(8,128)(2,1)}, u32[]{:S(2)}, u32[]{:S(2)}) collective-permute-start(bf16[1024,256]{1,0:T(8,128)(2,1)} %get-tuple-element.13), channel_id=1, source_target_pairs={{0,6},{2,0},{4,2},{6,4},{1,7},{3,1},{5,3},{7,5},{8,14},{10,8},{12,... | collective-permute-start | bytes 1572872 | tf_op jit(solution)/shard_map/ppermute | solution.py:27
  99.0 26.3 %collective-permute-start.6 = (bf16[1024,256]{1,0:T(8,128)(2,1)}, bf16[1024,256]{1,0:T(8,128)(2,1)}, u32[]{:S(2)}, u32[]{:S(2)}) collective-permute-start(bf16[1024,256]{1,0:T(8,128)(2,1)} %get-tuple-element.14), channel_id=1, source_target_pairs={{0,4},{2,6},{4,0},{6,2},{1,5},{3,7},{5,1},{7,3},{8,12},{10,14},{12... | collective-permute-start | bytes 1572872 | tf_op jit(solution)/shard_map/ppermute | solution.py:27
  101.5 30.5 %collective-permute-start.4 = (bf16[1024,256]{1,0:T(8,128)(2,1)S(1)}, bf16[1024,256]{1,0:T(8,128)(2,1)}, u32[]{:S(2)}, u32[]{:S(2)}) collective-permute-start(bf16[1024,256]{1,0:T(8,128)(2,1)S(1)} %get-tuple-element.12), channel_id=1, source_target_pairs={{0,2},{2,4},{4,6},{6,0},{1,3},{3,5},{5,7},{7,1},{8,10},{10,12},{12... | collective-permute-start | bytes 1572872 | tf_op jit(solution)/shard_map/ppermute | solution.py:27
  106.6 60.8 %collective-permute-start.13 = (bf16[256,1024]{1,0:T(8,128)(2,1)}, bf16[256,1024]{1,0:T(8,128)(2,1)}, u32[]{:S(2)}, u32[]{:S(2)}) collective-permute-start(bf16[256,1024]{1,0:T(8,128)(2,1)} %get-tuple-element.11), channel_id=1, source_target_pairs={{0,4},{2,6},{4,0},{6,2},{1,5},{3,7},{5,1},{7,3},{8,12},{10,14},{12... | collective-permute-start | bytes 1572872 | tf_op jit(solution)/shard_map/ppermute | solution.py:27
  112.4 63.2 %collective-permute-start.11 = (bf16[256,1024]{1,0:T(8,128)(2,1)S(1)}, bf16[256,1024]{1,0:T(8,128)(2,1)}, u32[]{:S(2)}, u32[]{:S(2)}) collective-permute-start(bf16[256,1024]{1,0:T(8,128)(2,1)S(1)} %get-tuple-element.9), channel_id=1, source_target_pairs={{0,2},{2,4},{4,6},{6,0},{1,3},{3,5},{5,7},{7,1},{8,10},{10,12},{12... | collective-permute-start | bytes 1572872 | tf_op jit(solution)/shard_map/ppermute | solution.py:27
  123.4 33.3 %collective-permute-start.9 = (bf16[512,256]{1,0:T(8,128)(2,1)S(1)}, bf16[512,256]{1,0:T(8,128)(2,1)S(1)}, u32[]{:S(2)}, u32[]{:S(2)}) collective-permute-start(bf16[512,256]{1,0:T(8,128)(2,1)S(1)} %fusion.12), channel_id=1, source_target_pairs={{0,2},{2,4},{4,6},{6,0},{1,3},{3,5},{5,7},{7,1},{8,10},{10,12},{12... | collective-permute-start | bytes 786440 | tf_op jit(solution)/shard_map/ppermute | solution.py:27
  127.8 33.6 %collective-permute-start.7 = (bf16[512,256]{1,0:T(8,128)(2,1)S(1)}, bf16[512,256]{1,0:T(8,128)(2,1)S(1)}, u32[]{:S(2)}, u32[]{:S(2)}) collective-permute-start(bf16[512,256]{1,0:T(8,128)(2,1)S(1)} %fusion.11), channel_id=1, source_target_pairs={{0,4},{2,6},{4,0},{6,2},{1,5},{3,7},{5,1},{7,3},{8,12},{10,14},{12... | collective-permute-start | bytes 786440 | tf_op jit(solution)/shard_map/ppermute | solution.py:27
  134.5 26.8 %collective-permute-start.5 = (bf16[512,256]{1,0:T(8,128)(2,1)S(1)}, bf16[512,256]{1,0:T(8,128)(2,1)S(1)}, u32[]{:S(2)}, u32[]{:S(2)}) collective-permute-start(bf16[512,256]{1,0:T(8,128)(2,1)S(1)} %fusion.10), channel_id=1, source_target_pairs={{0,6},{2,0},{4,2},{6,4},{1,7},{3,1},{5,3},{7,5},{8,14},{10,8},{12,... | collective-permute-start | bytes 786440 | tf_op jit(solution)/shard_map/ppermute | solution.py:27
  156.7 22.5 %collective-permute-start.15 = (bf16[256,1024]{1,0:T(8,128)(2,1)S(1)}, bf16[256,1024]{1,0:T(8,128)(2,1)S(1)}, u32[]{:S(2)}, u32[]{:S(2)}) collective-permute-start(bf16[256,1024]{1,0:T(8,128)(2,1)S(1)} %get-tuple-element.10), channel_id=1, source_target_pairs={{0,6},{2,0},{4,2},{6,4},{1,7},{3,1},{5,3},{7,5},{8,14},{10,8},{12,... | collective-permute-start | bytes 1572872 | tf_op jit(solution)/shard_map/ppermute | solution.py:27
  161.5 12.7 %collective-permute-start.12 = (bf16[512,256]{1,0:T(8,128)(2,1)S(1)}, bf16[512,256]{1,0:T(8,128)(2,1)S(1)}, u32[]{:S(2)}, u32[]{:S(2)}) collective-permute-start(bf16[512,256]{1,0:T(8,128)(2,1)S(1)} %maximum_convert_fusion), channel_id=1, source_target_pairs={{0,4},{2,6},{4,0},{6,2},{1,5},{3,7},{5,1},{7,3},{8,12},{10,14},{12... | collective-permute-start | bytes 786440 | tf_op jit(solution)/shard_map/ppermute | solution.py:27
  163.9 13.8 %collective-permute-start.10 = (bf16[512,256]{1,0:T(8,128)(2,1)S(1)}, bf16[512,256]{1,0:T(8,128)(2,1)S(1)}, u32[]{:S(2)}, u32[]{:S(2)}) collective-permute-start(bf16[512,256]{1,0:T(8,128)(2,1)S(1)} %maximum_convert_fusion), channel_id=1, source_target_pairs={{0,2},{2,4},{4,6},{6,0},{1,3},{3,5},{5,7},{7,1},{8,10},{10,12},{12... | collective-permute-start | bytes 786440 | tf_op jit(solution)/shard_map/ppermute | solution.py:27
  167.4 16.2 %collective-permute-start.14 = (bf16[512,256]{1,0:T(8,128)(2,1)S(1)}, bf16[512,256]{1,0:T(8,128)(2,1)S(1)}, u32[]{:S(2)}, u32[]{:S(2)}) collective-permute-start(bf16[512,256]{1,0:T(8,128)(2,1)S(1)} %maximum_convert_fusion), channel_id=1, source_target_pairs={{0,6},{2,0},{4,2},{6,4},{1,7},{3,1},{5,3},{7,5},{8,14},{10,8},{12,... | collective-permute-start | bytes 786440 | tf_op jit(solution)/shard_map/ppermute | solution.py:27
  185.1 53.7 %all-to-all-start.3 = ((bf16[128,8,512]{2,1,0:T(8,128)(2,1)}), bf16[128,8,512]{2,1,0:T(8,128)(2,1)S(1)}, u32[]{:S(2)}, u32[]{:S(2)}) async-start(bf16[128,8,512]{2,1,0:T(8,128)(2,1)} %bitcast.36), calls=%async_computation.3 | async-start | bytes 2097152 | tf_op jit(solution)/shard_map/all_to_all | solution.py:17
  199.4 27.1 %collective-permute-start.1 = (f32[2,256]{1,0:T(2,128)S(1)}, f32[2,256]{1,0:T(2,128)S(1)}, u32[]{:S(2)}, u32[]{:S(2)}) collective-permute-start(f32[2,256]{1,0:T(2,128)S(1)} %pad_maximum_fusion), channel_id=1, source_target_pairs={{0,1},{1,0},{2,3},{3,2},{4,5},{5,4},{6,7},{7,6},{8,9},{9,8},{10,11... | collective-permute-start | bytes 6152 | tf_op jit(solution)/shard_map/ppermute | solution.py:102
  226.6 5.5 %collective-permute-start.2 = (f32[2,256]{1,0:T(2,128)S(1)}, f32[2,256]{1,0:T(2,128)S(1)}, u32[]{:S(2)}, u32[]{:S(2)}) collective-permute-start(f32[2,256]{1,0:T(2,128)S(1)} %fusion.47), channel_id=1, source_target_pairs={{0,2},{2,0},{4,6},{6,4},{1,3},{3,1},{5,7},{7,5},{8,10},{10,8},{12,... | collective-permute-start | bytes 6152 | tf_op jit(solution)/shard_map/ppermute | solution.py:103
  232.1 6.7 %collective-permute-start.3 = (f32[2,256]{1,0:T(2,128)S(1)}, f32[2,256]{1,0:T(2,128)S(1)}, u32[]{:S(2)}, u32[]{:S(2)}) collective-permute-start(f32[2,256]{1,0:T(2,128)S(1)} %fusion.68), channel_id=1, source_target_pairs={{0,6},{6,0},{2,4},{4,2},{1,7},{7,1},{3,5},{5,3},{8,14},{14,8},{10,... | collective-permute-start | bytes 6152 | tf_op jit(solution)/shard_map/ppermute | solution.py:104
Sparse Core Ops, SparseCore 0:
  23.0 41.2 all-gather.3

commit v3 on v2

--- a/solution.py
+++ b/solution.py
@@ -1,6 +1,8 @@
 import jax
 import jax.numpy as jnp
 from jax import lax
+from jax.experimental import pallas as pl
+from jax.experimental.pallas import tpu as pltpu
 from jax.sharding import Mesh, PartitionSpec as P
 
 D = 4096
@@ -31,6 +33,42 @@
     return lax.dot_general(left, right, dims, preferred_element_type=F32)
 
 
+def pre_kernel(place, rows, own, one, two, three, out):
+    for k, weight in enumerate((own, one, two, three)):
+        total = dot32(rows[0], weight[:512]) + dot32(rows[1], weight[512:])
+        out[(place[0] - k) % 4] = total.astype(BF16)
+
+
+def hidden_kernel(parts, out):
+    total = sum(parts[k].astype(F32) for k in range(4))
+    hidden = jnp.maximum(total, 0.0).astype(BF16)
+    for k in range(4):
+        out[k] = hidden
+
+
+def result_kernel(place, hidden, own, one, two, three, out):
+    blocks = [hidden[(place[0] - k) % 4] for k in range(4)]
+    for z in range(2):
+        columns = pl.ds(512 * z, 512)
+        total = dot32(blocks[0], own[:, columns])
+        for k, weight in enumerate((one, two, three)):
+            total = total + dot32(blocks[k + 1], weight[:, columns])
+        out[z] = total.astype(BF16)
+
+
+def run(kernel, shape, place, *arrays):
+    vmem = pl.BlockSpec(memory_space=pltpu.VMEM)
+    smem = pl.BlockSpec(memory_space=pltpu.SMEM)
+    flags = [] if place is None else [place]
+    return pl.pallas_call(
+        kernel,
+        out_shape=jax.ShapeDtypeStruct(shape, BF16),
+        in_specs=[smem] * len(flags) + [vmem] * len(arrays),
+        out_specs=vmem,
+        compiler_params=pltpu.CompilerParams(vmem_limit_bytes=16 << 20),
+    )(*flags, *arrays)
+
+
 def body(
     queries,
     src_keys,
@@ -57,12 +95,10 @@
         shift(lax.dynamic_slice(w_in[0], (1024 * ((x + k) % 4), 0), (1024, 256)), k)
         for k in range(4)
     ]
-    half = lax.all_gather(out_proj, "zl", axis=0)
-    half = lax.all_gather(half, "y", axis=0)
-    other = lax.ppermute(half, "c", [(0, 1), (1, 0)])
-    low = lax.axis_index("c") == 0
-    proj = jnp.stack([jnp.where(low, half, other), jnp.where(low, other, half)])
-    proj = proj.transpose(2, 1, 0, 3, 4).reshape(2048, 512)
+    proj = lax.all_gather(out_proj, ("zl", "c"), axis=0, tiled=True)
+    proj = lax.all_gather(proj, "y", axis=0)
+    proj, first = lax.optimization_barrier((proj, first))
+    proj = proj.reshape(8, 4, 64, 512).transpose(1, 0, 2, 3).reshape(2048, 512)
 
     query_heads = queries.reshape(ROWS, heads, HEAD_DIM)
     scores = jnp.einsum("thd,shd->hts", query_heads, keys, preferred_element_type=F32)
@@ -83,36 +119,34 @@
     slot = chosen * ROOM + expert_slots[0]
     placing = (lax.broadcasted_iota(jnp.int32, (ROWS, 512), 1) == slot[:, None]).astype(BF16)
     placed = dot32(placing, gated.astype(BF16), (((0,), (0,)), ((), ()))).astype(BF16)
+    placed, tied = lax.optimization_barrier((placed, w_out[0]))
     placed = placed.reshape(1, 64, ROOM, 512)
     received = exchange(
         jnp.broadcast_to(placed, (2, 64, ROOM, 512)).reshape(128, ROOM, 512), ("zh",) + EXPERT
     )
     received = received.reshape(2, 512, 512)
-    w_out, stat_mixed, placed = lax.optimization_barrier((w_out, mixed, placed))
     second = [
-        shift(lax.dynamic_slice(w_out[0], (0, 1024 * ((x + k) % 4)), (256, 1024)), k)
+        shift(lax.dynamic_slice(tied, (0, 1024 * ((x + k) % 4)), (256, 1024)), k)
         for k in range(4)
     ]
 
+    received, second = lax.optimization_barrier((received, second))
+
     router32 = router.astype(F32)
-    logits = jnp.dot(stat_mixed * norm_gain, router32, precision=lax.Precision.HIGHEST)
+    logits = jnp.dot(mixed * norm_gain, router32, precision=lax.Precision.HIGHEST)
     column = lax.broadcasted_iota(jnp.int32, (ROWS, 64), 1)
     picked = jnp.sum(jnp.where(column == chosen[:, None], logits, 0.0), axis=1)
-    stats = jnp.stack([jnp.sum(stat_mixed * stat_mixed, axis=1), picked])
+    stats = jnp.stack([jnp.sum(mixed * mixed, axis=1), picked])
     stats = stats + lax.ppermute(stats, "zh", [(0, 1), (1, 0)])
     stats = stats + lax.ppermute(stats, "x", [(0, 1), (1, 0), (2, 3), (3, 2)])
     stats = stats + lax.ppermute(stats, "x", [(0, 3), (3, 0), (1, 2), (2, 1)])
     inverse_rms = lax.rsqrt(stats[0] / D + 1e-06)
     factor = jax.nn.sigmoid(stats[1] * inverse_rms) * inverse_rms
 
-    pre = [
-        (dot32(received[0], first[k][:512]) + dot32(received[1], first[k][512:])).astype(BF16)
-        for k in range(4)
-    ]
-    pre = sum(shift(pre[k], -k).astype(F32) for k in range(4))
-    hidden = jax.nn.relu(pre).astype(BF16)
-    result = sum(dot32(shift(hidden, k), second[k]) for k in range(4)).astype(BF16)
-    result = result.reshape(64, ROOM, 2, 512).transpose(2, 0, 1, 3).reshape(128, ROOM, 512)
+    place = x.astype(jnp.int32).reshape(1)
+    pre = exchange(run(pre_kernel, (4, 512, 256), place, received, *first), "x")
+    hidden = exchange(run(hidden_kernel, (4, 512, 256), None, pre), "x")
+    result = run(result_kernel, (2, 512, 512), place, hidden, *second).reshape(128, ROOM, 512)
     returned = exchange(result, ("zh",) + EXPERT).reshape(2, 512, 512)
     rows = dot32(placing, returned[0]) + dot32(placing, returned[1])
     return (mixed + factor[:, None] * rows).astype(BF16)

time: 249 us -> 251 us (level)
  blocking collectives: 16.2 us -> 53.1 us
  matrix products: 20.2 us -> 6.1 us
  starting transfers between devices: 89.5 us -> 76.3 us
  waiting for transfers between devices: 93.8 us -> 83.2 us
  Pallas kernels: 0 us -> 3.69 us
    all_to_all x0 -> x2, blocking collectives: none -> 35.6 us  [exchange(): return lax.all_to_all(blocks, axes, split_axis=0, concat_axis=0, tiled=True)]
    ppermute x12 -> x6, starting transfers between devices: 37 us -> 21.6 us  [shift(): return lax.ppermute(block, 'x', [(i, (i + places) % 4) for i in range(4)])]
    ppermute x12 -> x6, waiting for transfers between devices: 26.7 us -> 41.9 us  [shift(): return lax.ppermute(block, 'x', [(i, (i + places) % 4) for i in range(4)])]
    dot_general x16 -> x4, matrix products: 18.6 us -> 4.56 us  [dot32(): return lax.dot_general(left, right, dims, preferred_element_type=F32)]
    all_to_all x4, waiting for transfers between devices: 27 us -> 14.3 us  [exchange(): return lax.all_to_all(blocks, axes, split_axis=0, concat_axis=0, tiled=True)]
    all_gather x1, waiting for transfers between devices: 10.6 us -> 0.01 us  [body(): proj = lax.all_gather(proj, 'y', axis=0)]
    all_to_all x4, starting transfers between devices: 37.9 us -> 42.3 us  [exchange(): return lax.all_to_all(blocks, axes, split_axis=0, concat_axis=0, tiled=True)]
    pallas_call x0 -> x3, Pallas kernels: none -> 3.69 us  [run(): pl.pallas_call(kernel, out_shape=jax.ShapeDtypeStruct(shape, BF16), in_sp...]
  transfers between devices with their start and end apart: 21 -> 14, of which waited for: 13 -> 9; matrix products, arithmetic and copies ran while one was open for 11% -> 4% of each run, Pallas kernels for 0% -> 0%
where the time goes in v3:
time: 251 us; the launch traced here: 250 us
  waiting for transfers between devices  83.2 us (33%)
  starting transfers between devices  76.3 us (30%)
  blocking collectives  53.1 us (21%)
  local copies, waits for them, and re-layouts  13.9 us (6%)
  between operations  13.8 us (5%)
  matrix products  6.1 us (2%)
  Pallas kernels  3.69 us (1%)
    all_to_all x4, starting transfers between devices, exchange(): return lax.all_to_all(blocks, axes, split_axis=0, concat_axis=0, tiled=True)  42.3 us
    ppermute x6, waiting for transfers between devices, shift(): return lax.ppermute(block, 'x', [(i, (i + places) % 4) for i in range(4)])  41.9 us
    all_to_all x2, blocking collectives, exchange(): return lax.all_to_all(blocks, axes, split_axis=0, concat_axis=0, tiled=True)  35.6 us
    ppermute x6, starting transfers between devices, shift(): return lax.ppermute(block, 'x', [(i, (i + places) % 4) for i in range(4)])  21.6 us
    ppermute x1, waiting for transfers between devices, body(): stats = stats + lax.ppermute(stats, 'zh', [(0, 1), (1, 0)])  20.4 us
    all_gather x1, blocking collectives, body(): proj = lax.all_gather(out_proj, ('zl', 'c'), axis=0, tiled=True)  17.4 us
    all_to_all x4, waiting for transfers between devices, exchange(): return lax.all_to_all(blocks, axes, split_axis=0, concat_axis=0, tiled=True)  14.3 us
    ppermute x1, starting transfers between devices, body(): stats = stats + lax.ppermute(stats, 'zh', [(0, 1), (1, 0)])  6.81 us
  transfers between devices with their start and end apart: 14, of which 9 were waited for; matrix products, arithmetic and copies ran while one was open for 4% of the time, Pallas kernels for 0%

profile of v3, /device:TPU:96, one launch (start us, length us, event | category | flops | bytes accessed | tf_op | source)
XLA Modules:
  0.0 250.3 jit_solution(7438348310132332565)
XLA Ops:
  6.6 17.4 %all_gather.9 = bf16[256,512]{1,0:T(8,128)(2,1)} all-gather(bf16[32,512]{1,0:T(8,128)(2,1)} %param.19), channel_id=1, replica_groups=mesh['zl'=4,'y'=8,'c'=2,'x'=4,'zh'=2] {'zl','c'}, dimensions={0}, use_global_device_ids=true | all-gather | bytes 294912 | tf_op jit(solution)/shard_map/all_gather | solution.py:98
  26.7 10.0 %all-to-all-start = ((bf16[8,2,32,256]{3,2,1,0:T(8,128)(2,1)}), bf16[8,2,32,256]{3,2,1,0:T(8,128)(2,1)S(1)}, u32[]{:S(2)}, u32[]{:S(2)}) async-start(bf16[8,2,32,256]{3,2,1,0:T(8,128)(2,1)} %copy.37), calls=%async_computation | async-start | bytes 524288 | tf_op jit(solution)/shard_map/all_to_all | solution.py:19
  37.0 14.3 %all-to-all-done = bf16[8,2,32,256]{3,2,1,0:T(8,128)(2,1)S(1)} async-done(((bf16[8,2,32,256]{3,2,1,0:T(8,128)(2,1)}), bf16[8,2,32,256]{3,2,1,0:T(8,128)(2,1)S(1)}, u32[]{:S(2)}, u32[]{:S(2)}) %all-to-all-start) | async-done | bytes 262176 | tf_op jit(solution)/shard_map/all_to_all | solution.py:19
  52.7 1.1 broadcast_in_dim.40
  53.8 4.2 %all-to-all-start.1 = ((bf16[8,256,256]{1,2,0:T(8,128)(2,1)}), bf16[8,256,256]{1,2,0:T(8,128)(2,1)}, u32[]{:S(2)}, u32[]{:S(2)}) async-start(bf16[8,256,256]{1,2,0:T(8,128)(2,1)} %broadcast_in_dim.40), calls=%async_computation.1 | async-start | bytes 2097152 | tf_op jit(solution)/shard_map/all_to_all | solution.py:19
  58.3 3.7 %collective-permute-start = (bf16[1024,256]{1,0:T(8,128)(2,1)S(1)}, bf16[1024,256]{1,0:T(8,128)(2,1)S(1)}, u32[]{:S(2)}, u32[]{:S(2)}) collective-permute-start(bf16[1024,256]{1,0:T(8,128)(2,1)S(1)} %get-tuple-element.34), channel_id=1, source_target_pairs={{0,2},{2,4},{4,6},{6,0},{1,3},{3,5},{5,7},{7,1},{8,10},{10,12},{12... | collective-permute-start | bytes 1572872 | tf_op jit(solution)/shard_map/ppermute | solution.py:29
  62.0 4.6 %collective-permute-start.1 = (bf16[1024,256]{1,0:T(8,128)(2,1)S(1)}, bf16[1024,256]{1,0:T(8,128)(2,1)S(1)}, u32[]{:S(2)}, u32[]{:S(2)}) collective-permute-start(bf16[1024,256]{1,0:T(8,128)(2,1)S(1)} %get-tuple-element.36), channel_id=1, source_target_pairs={{0,4},{2,6},{4,0},{6,2},{1,5},{3,7},{5,1},{7,3},{8,12},{10,14},{12... | collective-permute-start | bytes 1572872 | tf_op jit(solution)/shard_map/ppermute | solution.py:29
  66.6 3.4 %collective-permute-start.2 = (bf16[1024,256]{1,0:T(8,128)(2,1)S(1)}, bf16[1024,256]{1,0:T(8,128)(2,1)S(1)}, u32[]{:S(2)}, u32[]{:S(2)}) collective-permute-start(bf16[1024,256]{1,0:T(8,128)(2,1)S(1)} %get-tuple-element.33), channel_id=1, source_target_pairs={{0,6},{2,0},{4,2},{6,4},{1,7},{3,1},{5,3},{7,5},{8,14},{10,8},{12,... | collective-permute-start | bytes 1572872 | tf_op jit(solution)/shard_map/ppermute | solution.py:29
  70.0 16.0 %collective-permute-done.one = bf16[1024,256]{1,0:T(8,128)(2,1)S(1)} collective-permute-done((bf16[1024,256]{1,0:T(8,128)(2,1)S(1)}, bf16[1024,256]{1,0:T(8,128)(2,1)S(1)}, u32[]{:S(2)}, u32[]{:S(2)}) %collective-permute-start) | collective-permute-done | bytes 524320 | tf_op jit(solution)/shard_map/ppermute | solution.py:29
  86.1 6.3 %collective-permute-done.1.two = bf16[1024,256]{1,0:T(8,128)(2,1)S(1)} collective-permute-done((bf16[1024,256]{1,0:T(8,128)(2,1)S(1)}, bf16[1024,256]{1,0:T(8,128)(2,1)S(1)}, u32[]{:S(2)}, u32[]{:S(2)}) %collective-permute-start.1) | collective-permute-done | bytes 524320 | tf_op jit(solution)/shard_map/ppermute | solution.py:29
  92.6 3.3 %copy.42 = bf16[4,8,64,512]{3,2,1,0:T(8,128)(2,1)} copy(bf16[4,8,64,512]{3,2,0,1:T(8,128)(2,1)} %bitcast.69) | data formatting | bytes 4194304 | tf_op jit(solution)/shard_map/transpose | solution.py:101
  96.0 2.7 %multiply_reduce_fusion = (f32[256]{0:T(256)S(1)}, f32[256,512]{1,0:T(8,128)S(1)}) fusion(bf16[256,2048]{0,1:T(8,128)(2,1)} %bitcast.8, bf16[2048,512]{1,0:T(8,128)(2,1)} %bitcast.70, bf16[256,512]{1,0:T(8,128)(2,1)S(1)} %copy-done.18), kind=kOutput, calls=%fused_computation.20 | convolution fusion | flops 537394944 | bytes 3933184 | tf_op jit(solution)/shard_map/dot_general | solution.py:33
  99.2 1.1 broadcast_in_dim.43
  100.2 14.2 %all-to-all-start.2 = ((bf16[128,8,512]{2,1,0:T(8,128)(2,1)}), bf16[128,8,512]{2,1,0:T(8,128)(2,1)S(1)}, u32[]{:S(2)}, u32[]{:S(2)}) async-start(bf16[128,8,512]{2,1,0:T(8,128)(2,1)} %bitcast.67), calls=%async_computation.2 | async-start | bytes 2097152 | tf_op jit(solution)/shard_map/all_to_all | solution.py:19
  114.4 1.7 constant_dynamic-slice_fusion
  116.2 2.8 %collective-permute-start.6 = (bf16[256,1024]{1,0:T(8,128)(2,1)S(1)}, bf16[256,1024]{1,0:T(8,128)(2,1)S(1)}, u32[]{:S(2)}, u32[]{:S(2)}) collective-permute-start(bf16[256,1024]{1,0:T(8,128)(2,1)S(1)} %get-tuple-element.31), channel_id=1, source_target_pairs={{0,2},{2,4},{4,6},{6,0},{1,3},{3,5},{5,7},{7,1},{8,10},{10,12},{12... | collective-permute-start | bytes 1572872 | tf_op jit(solution)/shard_map/ppermute | solution.py:29
  119.0 3.6 %collective-permute-start.7 = (bf16[256,1024]{1,0:T(8,128)(2,1)S(1)}, bf16[256,1024]{1,0:T(8,128)(2,1)S(1)}, u32[]{:S(2)}, u32[]{:S(2)}) collective-permute-start(bf16[256,1024]{1,0:T(8,128)(2,1)S(1)} %get-tuple-element.30), channel_id=1, source_target_pairs={{0,4},{2,6},{4,0},{6,2},{1,5},{3,7},{5,1},{7,3},{8,12},{10,14},{12... | collective-permute-start | bytes 1572872 | tf_op jit(solution)/shard_map/ppermute | solution.py:29
  122.7 3.4 %collective-permute-start.8 = (bf16[256,1024]{1,0:T(8,128)(2,1)S(1)}, bf16[256,1024]{1,0:T(8,128)(2,1)S(1)}, u32[]{:S(2)}, u32[]{:S(2)}) collective-permute-start(bf16[256,1024]{1,0:T(8,128)(2,1)S(1)} %get-tuple-element.29), channel_id=1, source_target_pairs={{0,6},{2,0},{4,2},{6,4},{1,7},{3,1},{5,3},{7,5},{8,14},{10,8},{12,... | collective-permute-start | bytes 1572872 | tf_op jit(solution)/shard_map/ppermute | solution.py:29
  126.1 18.4 %collective-permute-done.6.one = bf16[256,1024]{1,0:T(8,128)(2,1)S(1)} collective-permute-done((bf16[256,1024]{1,0:T(8,128)(2,1)S(1)}, bf16[256,1024]{1,0:T(8,128)(2,1)S(1)}, u32[]{:S(2)}, u32[]{:S(2)}) %collective-permute-start.6) | collective-permute-done | bytes 524320 | tf_op jit(solution)/shard_map/ppermute | solution.py:29
  147.8 1.0 copy-done.2
  148.8 1.3 shard_map.130
  150.1 19.0 %all_to_all.30.parts = bf16[4,512,256]{2,1,0:T(8,128)(2,1)S(1)} all-to-all(bf16[4,512,256]{2,1,0:T(8,128)(2,1)S(1)} %shard_map.130), channel_id=1, replica_groups=mesh['zl'=4,'y'=8,'c'=2,'x'=4,'zh'=2] {'x'}, dimensions={0} | all-to-all | bytes 2097152 | tf_op jit(solution)/shard_map/all_to_all | solution.py:19
  169.3 16.7 %all_to_all.31.hidden = bf16[4,512,256]{2,1,0:T(8,128)(2,1)S(1)} all-to-all(bf16[4,512,256]{2,1,0:T(8,128)(2,1)S(1)} %shard_map.131), channel_id=1, replica_groups=mesh['zl'=4,'y'=8,'c'=2,'x'=4,'zh'=2] {'x'}, dimensions={0} | all-to-all | bytes 2097152 | tf_op jit(solution)/shard_map/all_to_all | solution.py:19
  186.0 2.2 shard_map.132
  188.2 13.9 %all-to-all-start.5 = ((bf16[128,8,512]{2,1,0:T(8,128)(2,1)}), bf16[128,8,512]{2,1,0:T(8,128)(2,1)S(1)}, u32[]{:S(2)}, u32[]{:S(2)}) async-start(bf16[128,8,512]{2,1,0:T(8,128)(2,1)} %bitcast.28), calls=%async_computation.5 | async-start | bytes 2097152 | tf_op jit(solution)/shard_map/all_to_all | solution.py:19
  202.5 6.8 %collective-permute-start.3 = (f32[2,256]{1,0:T(2,128)S(1)}, f32[2,256]{1,0:T(2,128)S(1)}, u32[]{:S(2)}, u32[]{:S(2)}) collective-permute-start(f32[2,256]{1,0:T(2,128)S(1)} %pad_maximum_fusion), channel_id=1, source_target_pairs={{0,1},{1,0},{2,3},{3,2},{4,5},{5,4},{6,7},{7,6},{8,9},{9,8},{10,11... | collective-permute-start | bytes 6152 | tf_op jit(solution)/shard_map/ppermute | solution.py:140
  209.4 20.4 %collective-permute-done.3 = f32[2,256]{1,0:T(2,128)S(1)} collective-permute-done((f32[2,256]{1,0:T(2,128)S(1)}, f32[2,256]{1,0:T(2,128)S(1)}, u32[]{:S(2)}, u32[]{:S(2)}) %collective-permute-start.3) | collective-permute-done | bytes 2080 | tf_op jit(solution)/shard_map/ppermute | solution.py:140
  229.8 2.5 collective-permute-start.4
  232.3 3.0 %collective-permute-done.4 = f32[2,256]{1,0:T(2,128)S(1)} collective-permute-done((f32[2,256]{1,0:T(2,128)S(1)}, f32[2,256]{1,0:T(2,128)S(1)}, u32[]{:S(2)}, u32[]{:S(2)}) %collective-permute-start.4) | collective-permute-done | bytes 2080 | tf_op jit(solution)/shard_map/ppermute | solution.py:141
  235.3 3.1 %collective-permute-start.5 = (f32[2,256]{1,0:T(2,128)S(1)}, f32[2,256]{1,0:T(2,128)S(1)}, u32[]{:S(2)}, u32[]{:S(2)}) collective-permute-start(f32[2,256]{1,0:T(2,128)S(1)} %fusion.37), channel_id=1, source_target_pairs={{0,6},{6,0},{2,4},{4,2},{1,7},{7,1},{3,5},{5,3},{8,14},{14,8},{10,... | collective-permute-start | bytes 6152 | tf_op jit(solution)/shard_map/ppermute | solution.py:142
  238.4 3.6 %collective-permute-done.5 = f32[2,256]{1,0:T(2,128)S(1)} collective-permute-done((f32[2,256]{1,0:T(2,128)S(1)}, f32[2,256]{1,0:T(2,128)S(1)}, u32[]{:S(2)}, u32[]{:S(2)}) %collective-permute-start.5) | collective-permute-done | bytes 2080 | tf_op jit(solution)/shard_map/ppermute | solution.py:142
  242.4 1.1 fusion.7
  (70 shorter events, 9.6 us)
Async XLA Ops:
  6.5 195.5 %copy-start = (bf16[512,64]{0,1:T(8,128)(2,1)S(1)}, bf16[512,64]{0,1:T(8,128)(2,1)}, u32[]{:S(2)}) copy-start(bf16[512,64]{0,1:T(8,128)(2,1)} %param.21) | copy-start | bytes 196612
  6.5 30.2 %copy-start.12 = (bf16[256,256]{1,0:T(8,128)(2,1)S(1)}, bf16[256,256]{1,0:T(8,128)(2,1)}, u32[]{:S(2)}) copy-start(bf16[256,256]{1,0:T(8,128)(2,1)} %param.13) | copy-start | bytes 393220
  6.5 30.3 %copy-start.15 = (s32[1,256]{1,0:T(1,128)S(1)}, s32[1,256]{1,0:T(1,128)}, u32[]{:S(2)}) copy-start(s32[1,256]{1,0:T(1,128)} %param.16) | copy-start | bytes 3076
  6.5 30.3 %copy-start.16 = (s32[1,256]{1,0:T(1,128)S(1)}, s32[1,256]{1,0:T(1,128)}, u32[]{:S(2)}) copy-start(s32[1,256]{1,0:T(1,128)} %param.17) | copy-start | bytes 3076
  6.5 86.1 %all-gather.3.cloned.1.call-start = ((), (), s32[]{:S(2)}) async-start(), calls=%async_computation.6 | async-start | bytes 2359296 | tf_op jit(solution)/shard_map/all_gather | solution.py:99
  26.7 24.5 %all-to-all-start = ((bf16[8,2,32,256]{3,2,1,0:T(8,128)(2,1)}), bf16[8,2,32,256]{3,2,1,0:T(8,128)(2,1)S(1)}, u32[]{:S(2)}, u32[]{:S(2)}) async-start(bf16[8,2,32,256]{3,2,1,0:T(8,128)(2,1)} %copy.37), calls=%async_computation | async-start | bytes 524288 | tf_op jit(solution)/shard_map/all_to_all | solution.py:19
  52.7 5.4 %copy-start.11 = (bf16[1,4096,256]{2,1,0:T(8,128)(2,1)S(1)}, bf16[1,4096,256]{2,1,0:T(8,128)(2,1)}, u32[]{:S(2)}) copy-start(bf16[1,4096,256]{2,1,0:T(8,128)(2,1)} %param.24) | copy-start | bytes 6291460
  53.8 42.2 %all-to-all-start.1 = ((bf16[8,256,256]{1,2,0:T(8,128)(2,1)}), bf16[8,256,256]{1,2,0:T(8,128)(2,1)}, u32[]{:S(2)}, u32[]{:S(2)}) async-start(bf16[8,256,256]{1,2,0:T(8,128)(2,1)} %broadcast_in_dim.40), calls=%async_computation.1 | async-start | bytes 2097152 | tf_op jit(solution)/shard_map/all_to_all | solution.py:19
  58.1 11.9 %copy-start.14 = (s32[1,256]{1,0:T(1,128)S(1)}, s32[1,256]{1,0:T(1,128)}, u32[]{:S(2)}) copy-start(s32[1,256]{1,0:T(1,128)} %param.22) | copy-start | bytes 3076
  58.1 11.9 %copy-start.17 = (s32[1,256]{1,0:T(1,128)S(1)}, s32[1,256]{1,0:T(1,128)}, u32[]{:S(2)}) copy-start(s32[1,256]{1,0:T(1,128)} %param.23) | copy-start | bytes 3076
  58.3 27.8 %collective-permute-start = (bf16[1024,256]{1,0:T(8,128)(2,1)S(1)}, bf16[1024,256]{1,0:T(8,128)(2,1)S(1)}, u32[]{:S(2)}, u32[]{:S(2)}) collective-permute-start(bf16[1024,256]{1,0:T(8,128)(2,1)S(1)} %get-tuple-element.34), channel_id=1, source_target_pairs={{0,2},{2,4},{4,6},{6,0},{1,3},{3,5},{5,7},{7,1},{8,10},{10,12},{12... | collective-permute-start | bytes 1572872 | tf_op jit(solution)/shard_map/ppermute | solution.py:29
  62.0 30.3 %collective-permute-start.1 = (bf16[1024,256]{1,0:T(8,128)(2,1)S(1)}, bf16[1024,256]{1,0:T(8,128)(2,1)S(1)}, u32[]{:S(2)}, u32[]{:S(2)}) collective-permute-start(bf16[1024,256]{1,0:T(8,128)(2,1)S(1)} %get-tuple-element.36), channel_id=1, source_target_pairs={{0,4},{2,6},{4,0},{6,2},{1,5},{3,7},{5,1},{7,3},{8,12},{10,14},{12... | collective-permute-start | bytes 1572872 | tf_op jit(solution)/shard_map/ppermute | solution.py:29
  66.6 26.0 %collective-permute-start.2 = (bf16[1024,256]{1,0:T(8,128)(2,1)S(1)}, bf16[1024,256]{1,0:T(8,128)(2,1)S(1)}, u32[]{:S(2)}, u32[]{:S(2)}) collective-permute-start(bf16[1024,256]{1,0:T(8,128)(2,1)S(1)} %get-tuple-element.33), channel_id=1, source_target_pairs={{0,6},{2,0},{4,2},{6,4},{1,7},{3,1},{5,3},{7,5},{8,14},{10,8},{12,... | collective-permute-start | bytes 1572872 | tf_op jit(solution)/shard_map/ppermute | solution.py:29
  92.6 3.3 %copy-start.1 = (bf16[1024,256]{1,0:T(8,128)(2,1)}, bf16[1024,256]{1,0:T(8,128)(2,1)S(1)}, u32[]{:S(2)}) copy-start(bf16[1024,256]{1,0:T(8,128)(2,1)S(1)} %collective-permute-done.2.three) | copy-start | bytes 1572868
  92.6 3.3 %copy-start.18 = (bf16[256,512]{1,0:T(8,128)(2,1)S(1)}, bf16[256,512]{1,0:T(8,128)(2,1)}, u32[]{:S(2)}) copy-start(bf16[256,512]{1,0:T(8,128)(2,1)} %param.18) | copy-start | bytes 786436
  96.0 2.8 %copy-start.13 = (f32[512]{0:T(512)S(1)}, f32[512]{0:T(512)}, u32[]{:S(2)}) copy-start(f32[512]{0:T(512)} %param.20) | copy-start | bytes 6148
  98.7 1.5 copy-start.9
  100.2 47.6 %all-to-all-start.2 = ((bf16[128,8,512]{2,1,0:T(8,128)(2,1)}), bf16[128,8,512]{2,1,0:T(8,128)(2,1)S(1)}, u32[]{:S(2)}, u32[]{:S(2)}) async-start(bf16[128,8,512]{2,1,0:T(8,128)(2,1)} %bitcast.67), calls=%async_computation.2 | async-start | bytes 2097152 | tf_op jit(solution)/shard_map/all_to_all | solution.py:19
  116.2 28.3 %collective-permute-start.6 = (bf16[256,1024]{1,0:T(8,128)(2,1)S(1)}, bf16[256,1024]{1,0:T(8,128)(2,1)S(1)}, u32[]{:S(2)}, u32[]{:S(2)}) collective-permute-start(bf16[256,1024]{1,0:T(8,128)(2,1)S(1)} %get-tuple-element.31), channel_id=1, source_target_pairs={{0,2},{2,4},{4,6},{6,0},{1,3},{3,5},{5,7},{7,1},{8,10},{10,12},{12... | collective-permute-start | bytes 1572872 | tf_op jit(solution)/shard_map/ppermute | solution.py:29
  119.0 26.3 %collective-permute-start.7 = (bf16[256,1024]{1,0:T(8,128)(2,1)S(1)}, bf16[256,1024]{1,0:T(8,128)(2,1)S(1)}, u32[]{:S(2)}, u32[]{:S(2)}) collective-permute-start(bf16[256,1024]{1,0:T(8,128)(2,1)S(1)} %get-tuple-element.30), channel_id=1, source_target_pairs={{0,4},{2,6},{4,0},{6,2},{1,5},{3,7},{5,1},{7,3},{8,12},{10,14},{12... | collective-permute-start | bytes 1572872 | tf_op jit(solution)/shard_map/ppermute | solution.py:29
  122.7 24.4 %collective-permute-start.8 = (bf16[256,1024]{1,0:T(8,128)(2,1)S(1)}, bf16[256,1024]{1,0:T(8,128)(2,1)S(1)}, u32[]{:S(2)}, u32[]{:S(2)}) collective-permute-start(bf16[256,1024]{1,0:T(8,128)(2,1)S(1)} %get-tuple-element.29), channel_id=1, source_target_pairs={{0,6},{2,0},{4,2},{6,4},{1,7},{3,1},{5,3},{7,5},{8,14},{10,8},{12,... | collective-permute-start | bytes 1572872 | tf_op jit(solution)/shard_map/ppermute | solution.py:29
  144.5 0.8 copy-start.3
  145.3 0.8 copy-start.5
  147.8 1.0 copy-start.2
  169.1 16.8 %copy-start.4 = (bf16[256,1024]{1,0:T(8,128)(2,1)S(1)}, bf16[256,1024]{1,0:T(8,128)(2,1)}, u32[]{:S(2)}) copy-start(bf16[256,1024]{1,0:T(8,128)(2,1)} %copy-done.3) | copy-start | bytes 1572868
  169.1 16.8 %copy-start.6 = (bf16[256,1024]{1,0:T(8,128)(2,1)S(1)}, bf16[256,1024]{1,0:T(8,128)(2,1)}, u32[]{:S(2)}) copy-start(bf16[256,1024]{1,0:T(8,128)(2,1)} %copy-done.5) | copy-start | bytes 1572868
  169.1 16.8 %copy-start.8 = (bf16[256,1024]{1,0:T(8,128)(2,1)S(1)}, bf16[256,1024]{1,0:T(8,128)(2,1)}, u32[]{:S(2)}) copy-start(bf16[256,1024]{1,0:T(8,128)(2,1)} %copy-done.7) | copy-start | bytes 1572868
  188.2 13.9 %copy-start.10 = (f32[256,512]{1,0:T(8,128)S(1)}, f32[256,512]{1,0:T(8,128)}, u32[]{:S(2)}) copy-start(f32[256,512]{1,0:T(8,128)} %copy-done.9) | copy-start | bytes 1572868
  188.2 53.8 %all-to-all-start.5 = ((bf16[128,8,512]{2,1,0:T(8,128)(2,1)}), bf16[128,8,512]{2,1,0:T(8,128)(2,1)S(1)}, u32[]{:S(2)}, u32[]{:S(2)}) async-start(bf16[128,8,512]{2,1,0:T(8,128)(2,1)} %bitcast.28), calls=%async_computation.5 | async-start | bytes 2097152 | tf_op jit(solution)/shard_map/all_to_all | solution.py:19
  202.5 27.2 %collective-permute-start.3 = (f32[2,256]{1,0:T(2,128)S(1)}, f32[2,256]{1,0:T(2,128)S(1)}, u32[]{:S(2)}, u32[]{:S(2)}) collective-permute-start(f32[2,256]{1,0:T(2,128)S(1)} %pad_maximum_fusion), channel_id=1, source_target_pairs={{0,1},{1,0},{2,3},{3,2},{4,5},{5,4},{6,7},{7,6},{8,9},{9,8},{10,11... | collective-permute-start | bytes 6152 | tf_op jit(solution)/shard_map/ppermute | solution.py:140
  229.8 5.5 %collective-permute-start.4 = (f32[2,256]{1,0:T(2,128)S(1)}, f32[2,256]{1,0:T(2,128)S(1)}, u32[]{:S(2)}, u32[]{:S(2)}) collective-permute-start(f32[2,256]{1,0:T(2,128)S(1)} %fusion.25), channel_id=1, source_target_pairs={{0,2},{2,0},{4,6},{6,4},{1,3},{3,1},{5,7},{7,5},{8,10},{10,8},{12,... | collective-permute-start | bytes 6152 | tf_op jit(solution)/shard_map/ppermute | solution.py:141
  235.3 6.7 %collective-permute-start.5 = (f32[2,256]{1,0:T(2,128)S(1)}, f32[2,256]{1,0:T(2,128)S(1)}, u32[]{:S(2)}, u32[]{:S(2)}) collective-permute-start(f32[2,256]{1,0:T(2,128)S(1)} %fusion.37), channel_id=1, source_target_pairs={{0,6},{6,0},{2,4},{4,2},{1,7},{7,1},{3,5},{5,3},{8,14},{14,8},{10,... | collective-permute-start | bytes 6152 | tf_op jit(solution)/shard_map/ppermute | solution.py:142
  (1 other events, 0.8 us)
Sparse Core Ops, SparseCore 0:
  24.2 43.0 all-gather.2

commit v4 on v3

--- a/solution.py
+++ b/solution.py
@@ -56,6 +56,28 @@
         out[z] = total.astype(BF16)
 
 
+def pack_kernel(keys, values, out):
+    for k in range(8):
+        columns = pl.ds(256 * k, 256)
+        out[k, 0] = keys[:, columns]
+        out[k, 1] = values[:, columns]
+
+
+def mix_kernel(attended, proj, hidden_in, gain, slot, mixed, placed, rows):
+    for zl in range(4):
+        for y in range(8):
+            rows[pl.ds(64 * (8 * zl + y), 64)] = proj[y, zl]
+    total = hidden_in[...].astype(F32)
+    for k in range(8):
+        total = total + dot32(attended[k], rows[pl.ds(256 * k, 256)])
+    mixed[...] = total
+    taken = lax.broadcasted_iota(jnp.int32, (512, ROWS), 0) == slot[...]
+    taken = jnp.where(taken, F32(1.0), F32(0.0)).astype(BF16)
+    slots = dot32(taken, (total * gain[...]).astype(BF16)).astype(BF16)
+    placed[0] = slots
+    placed[1] = slots
+
+
 def run(kernel, shape, place, *arrays):
     vmem = pl.BlockSpec(memory_space=pltpu.VMEM)
     smem = pl.BlockSpec(memory_space=pltpu.SMEM)
@@ -86,19 +108,12 @@
 ):
     width = queries.shape[1]
     heads = width // HEAD_DIM
-    both = jnp.stack([src_keys.reshape(32, 8, width), src_values.reshape(32, 8, width)])
-    both = exchange(both.transpose(2, 0, 1, 3), MP)
+    both = exchange(run(pack_kernel, (8, 2, 32, width), None, src_keys, src_values), MP)
     keys = both[:, 0].reshape(ROWS, heads, HEAD_DIM)
     values = both[:, 1].reshape(ROWS, heads, HEAD_DIM)
     x = lax.axis_index("x")
-    first = [
-        shift(lax.dynamic_slice(w_in[0], (1024 * ((x + k) % 4), 0), (1024, 256)), k)
-        for k in range(4)
-    ]
     proj = lax.all_gather(out_proj, ("zl", "c"), axis=0, tiled=True)
     proj = lax.all_gather(proj, "y", axis=0)
-    proj, first = lax.optimization_barrier((proj, first))
-    proj = proj.reshape(8, 4, 64, 512).transpose(1, 0, 2, 3).reshape(2048, 512)
 
     query_heads = queries.reshape(ROWS, heads, HEAD_DIM)
     scores = jnp.einsum("thd,shd->hts", query_heads, keys, preferred_element_type=F32)
@@ -111,26 +126,33 @@
     attended = jnp.einsum("hts,shd->thd", weights, values, preferred_element_type=F32)
     attended = attended.astype(BF16).reshape(ROWS, width)
     attended = spread(attended, MP, 8)
-    attended = attended.transpose(1, 0, 2).reshape(ROWS, 8 * width)
-    mixed = hidden_in.astype(F32) + dot32(attended, proj)
-    gated = mixed * norm_gain
-
     chosen = expert_ids[0]
     slot = chosen * ROOM + expert_slots[0]
     placing = (lax.broadcasted_iota(jnp.int32, (ROWS, 512), 1) == slot[:, None]).astype(BF16)
-    placed = dot32(placing, gated.astype(BF16), (((0,), (0,)), ((), ()))).astype(BF16)
-    placed, tied = lax.optimization_barrier((placed, w_out[0]))
-    placed = placed.reshape(1, 64, ROOM, 512)
-    received = exchange(
-        jnp.broadcast_to(placed, (2, 64, ROOM, 512)).reshape(128, ROOM, 512), ("zh",) + EXPERT
-    )
+    vmem = pl.BlockSpec(memory_space=pltpu.VMEM)
+    mixed, placed = pl.pallas_call(
+        mix_kernel,
+        out_shape=(
+            jax.ShapeDtypeStruct((ROWS, 512), F32),
+            jax.ShapeDtypeStruct((2, 512, 512), BF16),
+        ),
+        in_specs=[vmem] * 5,
+        out_specs=(vmem, vmem),
+        scratch_shapes=[pltpu.VMEM((2048, 512), BF16)],
+        compiler_params=pltpu.CompilerParams(vmem_limit_bytes=24 << 20),
+    )(attended, proj.reshape(8, 4, 64, 512), hidden_in, norm_gain.reshape(1, 512), slot.reshape(1, ROWS))
+    placed, tied, feeding = lax.optimization_barrier((placed, w_out[0], w_in[0]))
+    received = exchange(placed.reshape(128, ROOM, 512), ("zh",) + EXPERT)
     received = received.reshape(2, 512, 512)
+    first = [
+        shift(lax.dynamic_slice(feeding, (1024 * ((x + k) % 4), 0), (1024, 256)), k)
+        for k in range(4)
+    ]
     second = [
         shift(lax.dynamic_slice(tied, (0, 1024 * ((x + k) % 4)), (256, 1024)), k)
         for k in range(4)
     ]
 
-    received, second = lax.optimization_barrier((received, second))
 
     router32 = router.astype(F32)
     logits = jnp.dot(mixed * norm_gain, router32, precision=lax.Precision.HIGHEST)
@@ -144,7 +166,9 @@
     factor = jax.nn.sigmoid(stats[1] * inverse_rms) * inverse_rms
 
     place = x.astype(jnp.int32).reshape(1)
-    pre = exchange(run(pre_kernel, (4, 512, 256), place, received, *first), "x")
+    pre = run(pre_kernel, (4, 512, 256), place, received, *first)
+    pre, second[2] = lax.optimization_barrier((pre, second[2]))
+    pre = exchange(pre, "x")
     hidden = exchange(run(hidden_kernel, (4, 512, 256), None, pre), "x")
     result = run(result_kernel, (2, 512, 512), place, hidden, *second).reshape(128, ROOM, 512)
     returned = exchange(result, ("zh",) + EXPERT).reshape(2, 512, 512)

time: 251 us -> 254 us (1.012)
  blocking collectives: 53.1 us -> 31.1 us
  waiting for transfers between devices: 83.2 us -> 105 us
  Pallas kernels: 3.69 us -> 7.35 us
  matrix products: 6.1 us -> 2.95 us
    all_to_all x4 -> x5, waiting for transfers between devices: 14.3 us -> 40.3 us  [exchange(): return lax.all_to_all(blocks, axes, split_axis=0, concat_axis=0, tiled=True)]
    all_to_all x2 -> x1, blocking collectives: 35.6 us -> 13.7 us  [exchange(): return lax.all_to_all(blocks, axes, split_axis=0, concat_axis=0, tiled=True)]
    unnamed x41 -> x35, local copies, waits for them, and re-layouts: 5.47 us -> 11.8 us
    transpose x2 -> x0, local copies, waits for them, and re-layouts: 4.08 us -> none  [the longest x1 3.32 us: body(): proj = proj.reshape(8, 4, 64, 512).transpose(1, 0, 2, 3).reshape(2048, 512)]
    ppermute x6, waiting for transfers between devices: 41.9 us -> 38.4 us  [shift(): return lax.ppermute(block, 'x', [(i, (i + places) % 4) for i in range(4)])]
    dot_general x4 -> x2, matrix products: 4.56 us -> 1.41 us  [dot32(): return lax.dot_general(left, right, dims, preferred_element_type=F32)]
    pallas_call x3 -> x4, Pallas kernels: 3.69 us -> 5.39 us  [run(): pl.pallas_call(kernel, out_shape=jax.ShapeDtypeStruct(shape, BF16), in_sp...]
    all_to_all x4 -> x5, starting transfers between devices: 42.3 us -> 41.4 us  [exchange(): return lax.all_to_all(blocks, axes, split_axis=0, concat_axis=0, tiled=True)]
  transfers between devices with their start and end apart: 14 -> 15, of which waited for: 9 -> 7; matrix products, arithmetic and copies ran while one was open for 4% -> 3% of each run, Pallas kernels for 0% -> 1%
where the time goes in v4:
time: 254 us; the launch traced here: 253 us
  waiting for transfers between devices  105 us (41%)
  starting transfers between devices  75.2 us (30%)
  blocking collectives  31.1 us (12%)
  local copies, waits for them, and re-layouts  16.3 us (6%)
  between operations  13.8 us (5%)
  Pallas kernels  7.35 us (3%)
  matrix products  2.95 us (1%)
    all_to_all x5, starting transfers between devices, exchange(): return lax.all_to_all(blocks, axes, split_axis=0, concat_axis=0, tiled=True)  41.4 us
    all_to_all x5, waiting for transfers between devices, exchange(): return lax.all_to_all(blocks, axes, split_axis=0, concat_axis=0, tiled=True)  40.3 us
    ppermute x6, waiting for transfers between devices, shift(): return lax.ppermute(block, 'x', [(i, (i + places) % 4) for i in range(4)])  38.4 us
    ppermute x6, starting transfers between devices, shift(): return lax.ppermute(block, 'x', [(i, (i + places) % 4) for i in range(4)])  20.8 us
    ppermute x1, waiting for transfers between devices, body(): stats = stats + lax.ppermute(stats, 'zh', [(0, 1), (1, 0)])  20.3 us
    all_gather x1, blocking collectives, body(): proj = lax.all_gather(out_proj, ('zl', 'c'), axis=0, tiled=True)  17.4 us
    all_to_all x1, blocking collectives, exchange(): return lax.all_to_all(blocks, axes, split_axis=0, concat_axis=0, tiled=True)  13.7 us
    unnamed x35, local copies, waits for them, and re-layouts  11.8 us
  transfers between devices with their start and end apart: 15, of which 7 were waited for; matrix products, arithmetic and copies ran while one was open for 3% of the time, Pallas kernels for 1%

profile of v4, /device:TPU:96, one launch (start us, length us, event | category | flops | bytes accessed | tf_op | source)
XLA Modules:
  0.0 252.7 jit_solution(15100251928233977823)
XLA Ops:
  6.5 17.4 %all_gather.9 = bf16[256,512]{1,0:T(8,128)(2,1)} all-gather(bf16[32,512]{1,0:T(8,128)(2,1)} %param.19), channel_id=1, replica_groups=mesh['zl'=4,'y'=8,'c'=2,'x'=4,'zh'=2] {'zl','c'}, dimensions={0}, use_global_device_ids=true | all-gather | bytes 294912 | tf_op jit(solution)/shard_map/all_gather | solution.py:115
  26.5 10.0 %all-to-all-start = ((bf16[8,2,32,256]{3,2,1,0:T(8,128)(2,1)}), bf16[8,2,32,256]{3,2,1,0:T(8,128)(2,1)S(1)}, u32[]{:S(2)}, u32[]{:S(2)}) async-start(bf16[8,2,32,256]{3,2,1,0:T(8,128)(2,1)} %shard_map.130), calls=%async_computation | async-start | bytes 524288 | tf_op jit(solution)/shard_map/all_to_all | solution.py:19
  38.4 12.7 %all-to-all-done = bf16[8,2,32,256]{3,2,1,0:T(8,128)(2,1)S(1)} async-done(((bf16[8,2,32,256]{3,2,1,0:T(8,128)(2,1)}), bf16[8,2,32,256]{3,2,1,0:T(8,128)(2,1)S(1)}, u32[]{:S(2)}, u32[]{:S(2)}) %all-to-all-start) | async-done | bytes 262176 | tf_op jit(solution)/shard_map/all_to_all | solution.py:19
  52.7 1.1 broadcast_in_dim.32
  53.7 3.6 %all-to-all-start.1 = ((bf16[8,256,256]{2,1,0:T(8,128)(2,1)}), bf16[8,256,256]{2,1,0:T(8,128)(2,1)S(1)}, u32[]{:S(2)}, u32[]{:S(2)}) async-start(bf16[8,256,256]{2,1,0:T(8,128)(2,1)} %broadcast_in_dim.32), calls=%async_computation.1 | async-start | bytes 2097152 | tf_op jit(solution)/shard_map/all_to_all | solution.py:19
  57.3 27.7 %all-to-all-done.1.attended = bf16[8,256,256]{2,1,0:T(8,128)(2,1)S(1)} async-done(((bf16[8,256,256]{2,1,0:T(8,128)(2,1)}), bf16[8,256,256]{2,1,0:T(8,128)(2,1)S(1)}, u32[]{:S(2)}, u32[]{:S(2)}) %all-to-all-start.1) | async-done | bytes 1048608 | tf_op jit(solution)/shard_map/all_to_all | solution.py:19
  85.0 1.6 copy-done.1
  86.6 2.0 shard_map.131
  88.6 10.5 %all-to-all-start.2 = ((bf16[128,8,512]{2,1,0:T(8,128)(2,1)}), bf16[128,8,512]{2,1,0:T(8,128)(2,1)S(1)}, u32[]{:S(2)}, u32[]{:S(2)}) async-start(bf16[128,8,512]{2,1,0:T(8,128)(2,1)} %bitcast.17), calls=%async_computation.2 | async-start | bytes 2097152 | tf_op jit(solution)/shard_map/all_to_all | solution.py:19
  99.2 1.8 constant_dynamic-slice_fusion.4
  101.0 2.1 collective-permute-start.3
  103.1 4.6 %collective-permute-start.4 = (bf16[1024,256]{1,0:T(8,128)(2,1)S(1)}, bf16[1024,256]{1,0:T(8,128)(2,1)S(1)}, u32[]{:S(2)}, u32[]{:S(2)}) collective-permute-start(bf16[1024,256]{1,0:T(8,128)(2,1)S(1)} %get-tuple-element.24), channel_id=1, source_target_pairs={{0,4},{2,6},{4,0},{6,2},{1,5},{3,7},{5,1},{7,3},{8,12},{10,14},{12... | collective-permute-start | bytes 1572872 | tf_op jit(solution)/shard_map/ppermute | solution.py:29
  107.7 2.5 collective-permute-start.5
  110.2 1.2 constant_dynamic-slice_fusion
  111.5 4.6 %collective-permute-start.6 = (bf16[256,1024]{1,0:T(8,128)(2,1)}, bf16[256,1024]{1,0:T(8,128)(2,1)S(1)}, u32[]{:S(2)}, u32[]{:S(2)}) collective-permute-start(bf16[256,1024]{1,0:T(8,128)(2,1)} %get-tuple-element.22), channel_id=1, source_target_pairs={{0,4},{2,6},{4,0},{6,2},{1,5},{3,7},{5,1},{7,3},{8,12},{10,14},{12... | collective-permute-start | bytes 1572872 | tf_op jit(solution)/shard_map/ppermute | solution.py:29
  116.1 24.5 %collective-permute-done.3.one = bf16[1024,256]{1,0:T(8,128)(2,1)S(1)} collective-permute-done((bf16[1024,256]{1,0:T(8,128)(2,1)S(1)}, bf16[1024,256]{1,0:T(8,128)(2,1)S(1)}, u32[]{:S(2)}, u32[]{:S(2)}) %collective-permute-start.3) | collective-permute-done | bytes 524320 | tf_op jit(solution)/shard_map/ppermute | solution.py:29
  146.1 1.3 shard_map.132
  147.4 13.7 %all_to_all.30.parts = bf16[4,512,256]{2,1,0:T(8,128)(2,1)S(1)} all-to-all(bf16[4,512,256]{2,1,0:T(8,128)(2,1)S(1)} %shard_map.132), channel_id=1, replica_groups=mesh['zl'=4,'y'=8,'c'=2,'x'=4,'zh'=2] {'x'}, dimensions={0} | all-to-all | bytes 2097152 | tf_op jit(solution)/shard_map/all_to_all | solution.py:19
  161.1 1.1 shard_map.133
  162.2 3.5 %all-to-all-start.4 = ((bf16[4,512,256]{2,1,0:T(8,128)(2,1)}), bf16[4,512,256]{2,1,0:T(8,128)(2,1)S(1)}, u32[]{:S(2)}, u32[]{:S(2)}) async-start(bf16[4,512,256]{2,1,0:T(8,128)(2,1)} %shard_map.133), calls=%async_computation.4 | async-start | bytes 2097152 | tf_op jit(solution)/shard_map/all_to_all | solution.py:19
  165.7 3.9 %collective-permute-start.7 = (bf16[256,1024]{1,0:T(8,128)(2,1)}, bf16[256,1024]{1,0:T(8,128)(2,1)S(1)}, u32[]{:S(2)}, u32[]{:S(2)}) collective-permute-start(bf16[256,1024]{1,0:T(8,128)(2,1)} %get-tuple-element.20), channel_id=1, source_target_pairs={{0,2},{2,4},{4,6},{6,0},{1,3},{3,5},{5,7},{7,1},{8,10},{10,12},{12... | collective-permute-start | bytes 1572872 | tf_op jit(solution)/shard_map/ppermute | solution.py:29
  169.6 3.2 %collective-permute-start.8 = (bf16[256,1024]{1,0:T(8,128)(2,1)}, bf16[256,1024]{1,0:T(8,128)(2,1)S(1)}, u32[]{:S(2)}, u32[]{:S(2)}) collective-permute-start(bf16[256,1024]{1,0:T(8,128)(2,1)} %get-tuple-element.19), channel_id=1, source_target_pairs={{0,6},{2,0},{4,2},{6,4},{1,7},{3,1},{5,3},{7,5},{8,14},{10,8},{12,... | collective-permute-start | bytes 1572872 | tf_op jit(solution)/shard_map/ppermute | solution.py:29
  172.8 13.9 %collective-permute-done.7.one = bf16[256,1024]{1,0:T(8,128)(2,1)S(1)} collective-permute-done((bf16[256,1024]{1,0:T(8,128)(2,1)}, bf16[256,1024]{1,0:T(8,128)(2,1)S(1)}, u32[]{:S(2)}, u32[]{:S(2)}) %collective-permute-start.7) | collective-permute-done | bytes 524320 | tf_op jit(solution)/shard_map/ppermute | solution.py:29
  188.6 2.2 shard_map.134
  190.8 13.7 %all-to-all-start.5 = ((bf16[128,8,512]{2,1,0:T(8,128)(2,1)}), bf16[128,8,512]{2,1,0:T(8,128)(2,1)S(1)}, u32[]{:S(2)}, u32[]{:S(2)}) async-start(bf16[128,8,512]{2,1,0:T(8,128)(2,1)} %bitcast.19), calls=%async_computation.5 | async-start | bytes 2097152 | tf_op jit(solution)/shard_map/all_to_all | solution.py:19
  205.1 6.8 %collective-permute-start = (f32[2,256]{1,0:T(2,128)S(1)}, f32[2,256]{1,0:T(2,128)S(1)}, u32[]{:S(2)}, u32[]{:S(2)}) collective-permute-start(f32[2,256]{1,0:T(2,128)S(1)} %pad_maximum_fusion), channel_id=1, source_target_pairs={{0,1},{1,0},{2,3},{3,2},{4,5},{5,4},{6,7},{7,6},{8,9},{9,8},{10,11... | collective-permute-start | bytes 6152 | tf_op jit(solution)/shard_map/ppermute | solution.py:162
  211.9 20.3 %collective-permute-done = f32[2,256]{1,0:T(2,128)S(1)} collective-permute-done((f32[2,256]{1,0:T(2,128)S(1)}, f32[2,256]{1,0:T(2,128)S(1)}, u32[]{:S(2)}, u32[]{:S(2)}) %collective-permute-start) | collective-permute-done | bytes 2080 | tf_op jit(solution)/shard_map/ppermute | solution.py:162
  232.3 2.8 %collective-permute-start.1 = (f32[2,256]{1,0:T(2,128)S(1)}, f32[2,256]{1,0:T(2,128)S(1)}, u32[]{:S(2)}, u32[]{:S(2)}) collective-permute-start(f32[2,256]{1,0:T(2,128)S(1)} %fusion.23), channel_id=1, source_target_pairs={{0,2},{2,0},{4,6},{6,4},{1,3},{3,1},{5,7},{7,5},{8,10},{10,8},{12,... | collective-permute-start | bytes 6152 | tf_op jit(solution)/shard_map/ppermute | solution.py:163
  235.0 2.7 %collective-permute-done.1 = f32[2,256]{1,0:T(2,128)S(1)} collective-permute-done((f32[2,256]{1,0:T(2,128)S(1)}, f32[2,256]{1,0:T(2,128)S(1)}, u32[]{:S(2)}, u32[]{:S(2)}) %collective-permute-start.1) | collective-permute-done | bytes 2080 | tf_op jit(solution)/shard_map/ppermute | solution.py:163
  237.7 3.4 %collective-permute-start.2 = (f32[2,256]{1,0:T(2,128)S(1)}, f32[2,256]{1,0:T(2,128)S(1)}, u32[]{:S(2)}, u32[]{:S(2)}) collective-permute-start(f32[2,256]{1,0:T(2,128)S(1)} %fusion.33), channel_id=1, source_target_pairs={{0,6},{6,0},{2,4},{4,2},{1,7},{7,1},{3,5},{5,3},{8,14},{14,8},{10,... | collective-permute-start | bytes 6152 | tf_op jit(solution)/shard_map/ppermute | solution.py:164
  241.1 3.3 %collective-permute-done.2 = f32[2,256]{1,0:T(2,128)S(1)} collective-permute-done((f32[2,256]{1,0:T(2,128)S(1)}, f32[2,256]{1,0:T(2,128)S(1)}, u32[]{:S(2)}, u32[]{:S(2)}) %collective-permute-start.2) | collective-permute-done | bytes 2080 | tf_op jit(solution)/shard_map/ppermute | solution.py:164
  244.8 1.1 fusion.7
  (64 shorter events, 14.3 us)
Async XLA Ops:
  6.5 198.1 %copy-start = (bf16[512,64]{0,1:T(8,128)(2,1)S(1)}, bf16[512,64]{0,1:T(8,128)(2,1)}, u32[]{:S(2)}) copy-start(bf16[512,64]{0,1:T(8,128)(2,1)} %param.21) | copy-start | bytes 196612
  6.5 78.5 %all-gather.3.cloned.1.call-start = ((), (), s32[]{:S(2)}) async-start(), calls=%async_computation.6 | async-start | bytes 2359296 | tf_op jit(solution)/shard_map/all_gather | solution.py:116
  24.0 0.9 copy-start.11
  24.9 0.9 copy-start.12
  26.5 24.5 %all-to-all-start = ((bf16[8,2,32,256]{3,2,1,0:T(8,128)(2,1)}), bf16[8,2,32,256]{3,2,1,0:T(8,128)(2,1)S(1)}, u32[]{:S(2)}, u32[]{:S(2)}) async-start(bf16[8,2,32,256]{3,2,1,0:T(8,128)(2,1)} %shard_map.130), calls=%async_computation | async-start | bytes 524288 | tf_op jit(solution)/shard_map/all_to_all | solution.py:19
  52.5 4.8 %copy-start.15 = (s32[1,256]{1,0:T(1,128)S(1)}, s32[1,256]{1,0:T(1,128)}, u32[]{:S(2)}) copy-start(s32[1,256]{1,0:T(1,128)} %param.22) | copy-start | bytes 3076
  52.5 4.8 %copy-start.16 = (s32[1,256]{1,0:T(1,128)S(1)}, s32[1,256]{1,0:T(1,128)}, u32[]{:S(2)}) copy-start(s32[1,256]{1,0:T(1,128)} %param.23) | copy-start | bytes 3076
  52.6 32.4 %copy-start.10 = (bf16[256,512]{1,0:T(8,128)(2,1)S(1)}, bf16[256,512]{1,0:T(8,128)(2,1)}, u32[]{:S(2)}) copy-start(bf16[256,512]{1,0:T(8,128)(2,1)} %hidden_in.1) | copy-start | bytes 786436
  52.6 32.4 %copy-start.13 = (f32[512]{0:T(512)S(1)}, f32[512]{0:T(512)}, u32[]{:S(2)}) copy-start(f32[512]{0:T(512)} %param.20) | copy-start | bytes 6148
  53.7 31.2 %all-to-all-start.1 = ((bf16[8,256,256]{2,1,0:T(8,128)(2,1)}), bf16[8,256,256]{2,1,0:T(8,128)(2,1)S(1)}, u32[]{:S(2)}, u32[]{:S(2)}) async-start(bf16[8,256,256]{2,1,0:T(8,128)(2,1)} %broadcast_in_dim.32), calls=%async_computation.1 | async-start | bytes 2097152 | tf_op jit(solution)/shard_map/all_to_all | solution.py:19
  85.0 1.6 copy-start.1
  88.6 54.4 %all-to-all-start.2 = ((bf16[128,8,512]{2,1,0:T(8,128)(2,1)}), bf16[128,8,512]{2,1,0:T(8,128)(2,1)S(1)}, u32[]{:S(2)}, u32[]{:S(2)}) async-start(bf16[128,8,512]{2,1,0:T(8,128)(2,1)} %bitcast.17), calls=%async_computation.2 | async-start | bytes 2097152 | tf_op jit(solution)/shard_map/all_to_all | solution.py:19
  99.2 11.0 %copy-start.14 = (bf16[1,256,4096]{2,1,0:T(8,128)(2,1)S(1)}, bf16[1,256,4096]{2,1,0:T(8,128)(2,1)}, u32[]{:S(2)}) copy-start(bf16[1,256,4096]{2,1,0:T(8,128)(2,1)} %param.25) | copy-start | bytes 6291460
  101.0 39.6 %collective-permute-start.3 = (bf16[1024,256]{1,0:T(8,128)(2,1)S(1)}, bf16[1024,256]{1,0:T(8,128)(2,1)S(1)}, u32[]{:S(2)}, u32[]{:S(2)}) collective-permute-start(bf16[1024,256]{1,0:T(8,128)(2,1)S(1)} %get-tuple-element.25), channel_id=1, source_target_pairs={{0,2},{2,4},{4,6},{6,0},{1,3},{3,5},{5,7},{7,1},{8,10},{10,12},{12... | collective-permute-start | bytes 1572872 | tf_op jit(solution)/shard_map/ppermute | solution.py:29
  103.1 38.3 %collective-permute-start.4 = (bf16[1024,256]{1,0:T(8,128)(2,1)S(1)}, bf16[1024,256]{1,0:T(8,128)(2,1)S(1)}, u32[]{:S(2)}, u32[]{:S(2)}) collective-permute-start(bf16[1024,256]{1,0:T(8,128)(2,1)S(1)} %get-tuple-element.24), channel_id=1, source_target_pairs={{0,4},{2,6},{4,0},{6,2},{1,5},{3,7},{5,1},{7,3},{8,12},{10,14},{12... | collective-permute-start | bytes 1572872 | tf_op jit(solution)/shard_map/ppermute | solution.py:29
  107.7 34.5 %collective-permute-start.5 = (bf16[1024,256]{1,0:T(8,128)(2,1)S(1)}, bf16[1024,256]{1,0:T(8,128)(2,1)S(1)}, u32[]{:S(2)}, u32[]{:S(2)}) collective-permute-start(bf16[1024,256]{1,0:T(8,128)(2,1)S(1)} %get-tuple-element.23), channel_id=1, source_target_pairs={{0,6},{2,0},{4,2},{6,4},{1,7},{3,1},{5,3},{7,5},{8,14},{10,8},{12,... | collective-permute-start | bytes 1572872 | tf_op jit(solution)/shard_map/ppermute | solution.py:29
  111.5 35.9 %collective-permute-start.6 = (bf16[256,1024]{1,0:T(8,128)(2,1)}, bf16[256,1024]{1,0:T(8,128)(2,1)S(1)}, u32[]{:S(2)}, u32[]{:S(2)}) collective-permute-start(bf16[256,1024]{1,0:T(8,128)(2,1)} %get-tuple-element.22), channel_id=1, source_target_pairs={{0,4},{2,6},{4,0},{6,2},{1,5},{3,7},{5,1},{7,3},{8,12},{10,14},{12... | collective-permute-start | bytes 1572872 | tf_op jit(solution)/shard_map/ppermute | solution.py:29
  140.5 0.8 copy-start.2
  141.3 0.8 copy-start.4
  142.2 0.8 copy-start.6
  142.9 1.0 copy-start.3
  144.0 1.0 copy-start.5
  145.0 1.0 copy-start.7
  162.2 25.3 %all-to-all-start.4 = ((bf16[4,512,256]{2,1,0:T(8,128)(2,1)}), bf16[4,512,256]{2,1,0:T(8,128)(2,1)S(1)}, u32[]{:S(2)}, u32[]{:S(2)}) async-start(bf16[4,512,256]{2,1,0:T(8,128)(2,1)} %shard_map.133), calls=%async_computation.4 | async-start | bytes 2097152 | tf_op jit(solution)/shard_map/all_to_all | solution.py:19
  165.7 21.0 %collective-permute-start.7 = (bf16[256,1024]{1,0:T(8,128)(2,1)}, bf16[256,1024]{1,0:T(8,128)(2,1)S(1)}, u32[]{:S(2)}, u32[]{:S(2)}) collective-permute-start(bf16[256,1024]{1,0:T(8,128)(2,1)} %get-tuple-element.20), channel_id=1, source_target_pairs={{0,2},{2,4},{4,6},{6,0},{1,3},{3,5},{5,7},{7,1},{8,10},{10,12},{12... | collective-permute-start | bytes 1572872 | tf_op jit(solution)/shard_map/ppermute | solution.py:29
  169.6 17.1 %collective-permute-start.8 = (bf16[256,1024]{1,0:T(8,128)(2,1)}, bf16[256,1024]{1,0:T(8,128)(2,1)S(1)}, u32[]{:S(2)}, u32[]{:S(2)}) collective-permute-start(bf16[256,1024]{1,0:T(8,128)(2,1)} %get-tuple-element.19), channel_id=1, source_target_pairs={{0,6},{2,0},{4,2},{6,4},{1,7},{3,1},{5,3},{7,5},{8,14},{10,8},{12,... | collective-permute-start | bytes 1572872 | tf_op jit(solution)/shard_map/ppermute | solution.py:29
  186.7 0.8 copy-start.8
  187.5 1.0 copy-start.9
  190.8 53.7 %all-to-all-start.5 = ((bf16[128,8,512]{2,1,0:T(8,128)(2,1)}), bf16[128,8,512]{2,1,0:T(8,128)(2,1)S(1)}, u32[]{:S(2)}, u32[]{:S(2)}) async-start(bf16[128,8,512]{2,1,0:T(8,128)(2,1)} %bitcast.19), calls=%async_computation.5 | async-start | bytes 2097152 | tf_op jit(solution)/shard_map/all_to_all | solution.py:19
  205.1 27.1 %collective-permute-start = (f32[2,256]{1,0:T(2,128)S(1)}, f32[2,256]{1,0:T(2,128)S(1)}, u32[]{:S(2)}, u32[]{:S(2)}) collective-permute-start(f32[2,256]{1,0:T(2,128)S(1)} %pad_maximum_fusion), channel_id=1, source_target_pairs={{0,1},{1,0},{2,3},{3,2},{4,5},{5,4},{6,7},{7,6},{8,9},{9,8},{10,11... | collective-permute-start | bytes 6152 | tf_op jit(solution)/shard_map/ppermute | solution.py:162
  232.3 5.5 %collective-permute-start.1 = (f32[2,256]{1,0:T(2,128)S(1)}, f32[2,256]{1,0:T(2,128)S(1)}, u32[]{:S(2)}, u32[]{:S(2)}) collective-permute-start(f32[2,256]{1,0:T(2,128)S(1)} %fusion.23), channel_id=1, source_target_pairs={{0,2},{2,0},{4,6},{6,4},{1,3},{3,1},{5,7},{7,5},{8,10},{10,8},{12,... | collective-permute-start | bytes 6152 | tf_op jit(solution)/shard_map/ppermute | solution.py:163
  237.7 6.7 %collective-permute-start.2 = (f32[2,256]{1,0:T(2,128)S(1)}, f32[2,256]{1,0:T(2,128)S(1)}, u32[]{:S(2)}, u32[]{:S(2)}) collective-permute-start(f32[2,256]{1,0:T(2,128)S(1)} %fusion.33), channel_id=1, source_target_pairs={{0,6},{6,0},{2,4},{4,2},{1,7},{7,1},{3,5},{5,3},{8,14},{14,8},{10,... | collective-permute-start | bytes 6152 | tf_op jit(solution)/shard_map/ppermute | solution.py:164
Sparse Core Ops, SparseCore 0:
  24.1 43.2 all-gather.2

commit v5 on v3

--- a/solution.py
+++ b/solution.py
@@ -33,9 +33,18 @@
     return lax.dot_general(left, right, dims, preferred_element_type=F32)
 
 
-def pre_kernel(place, rows, own, one, two, three, out):
-    for k, weight in enumerate((own, one, two, three)):
-        total = dot32(rows[0], weight[:512]) + dot32(rows[1], weight[512:])
+def fetch(weights, held, done):
+    copies = [pltpu.make_async_copy(weights[k], held.at[k], done.at[k]) for k in range(4)]
+    for copy in copies:
+        copy.start()
+    return copies
+
+
+def pre_kernel(place, rows, own, one, two, three, out, held, done):
+    copies = fetch((own, one, two, three), held, done)
+    for k in range(4):
+        copies[k].wait()
+        total = dot32(rows[0], held[k, :512]) + dot32(rows[1], held[k, 512:])
         out[(place[0] - k) % 4] = total.astype(BF16)
 
 
@@ -46,27 +55,38 @@
         out[k] = hidden
 
 
-def result_kernel(place, hidden, own, one, two, three, out):
-    blocks = [hidden[(place[0] - k) % 4] for k in range(4)]
+def result_kernel(place, hidden, own, one, two, three, out, held, done):
+    copies = fetch((own, one, two, three), held, done)
+    for copy in copies:
+        copy.wait()
     for z in range(2):
         columns = pl.ds(512 * z, 512)
-        total = dot32(blocks[0], own[:, columns])
-        for k, weight in enumerate((one, two, three)):
-            total = total + dot32(blocks[k + 1], weight[:, columns])
+        total = dot32(hidden[place[0]], held[0, :, columns])
+        for k in range(1, 4):
+            total = total + dot32(hidden[(place[0] - k) % 4], held[k, :, columns])
         out[z] = total.astype(BF16)
 
 
-def run(kernel, shape, place, *arrays):
+def run(kernel, shapes, place, arrays, weights=(), scratch=()):
     vmem = pl.BlockSpec(memory_space=pltpu.VMEM)
     smem = pl.BlockSpec(memory_space=pltpu.SMEM)
+    far = pl.BlockSpec(memory_space=pl.ANY)
     flags = [] if place is None else [place]
+    scratch = list(scratch)
+    if weights:
+        scratch = [pltpu.VMEM((4,) + weights[0].shape, BF16), pltpu.SemaphoreType.DMA((4,))]
     return pl.pallas_call(
         kernel,
-        out_shape=jax.ShapeDtypeStruct(shape, BF16),
-        in_specs=[smem] * len(flags) + [vmem] * len(arrays),
-        out_specs=vmem,
-        compiler_params=pltpu.CompilerParams(vmem_limit_bytes=16 << 20),
-    )(*flags, *arrays)
+        out_shape=shapes,
+        in_specs=[smem] * len(flags) + [vmem] * len(arrays) + [far] * len(weights),
+        out_specs=jax.tree.map(lambda leaf: vmem, shapes),
+        scratch_shapes=scratch,
+        compiler_params=pltpu.CompilerParams(vmem_limit_bytes=24 << 20),
+    )(*flags, *arrays, *weights)
+
+
+def spot(*dims, dtype=BF16):
+    return jax.ShapeDtypeStruct(dims, dtype)
 
 
 def body(
@@ -95,10 +115,13 @@
         shift(lax.dynamic_slice(w_in[0], (1024 * ((x + k) % 4), 0), (1024, 256)), k)
         for k in range(4)
     ]
-    proj = lax.all_gather(out_proj, ("zl", "c"), axis=0, tiled=True)
-    proj = lax.all_gather(proj, "y", axis=0)
-    proj, first = lax.optimization_barrier((proj, first))
-    proj = proj.reshape(8, 4, 64, 512).transpose(1, 0, 2, 3).reshape(2048, 512)
+    half = lax.all_gather(out_proj, "zl", axis=0)
+    half = lax.all_gather(half, "y", axis=0)
+    half, first = lax.optimization_barrier((half, first))
+    other = lax.ppermute(half, "c", [(0, 1), (1, 0)])
+    low = lax.axis_index("c") == 0
+    proj = jnp.stack([jnp.where(low, half, other), jnp.where(low, other, half)])
+    proj = proj.transpose(2, 1, 0, 3, 4).reshape(2048, 512)
 
     query_heads = queries.reshape(ROWS, heads, HEAD_DIM)
     scores = jnp.einsum("thd,shd->hts", query_heads, keys, preferred_element_type=F32)
@@ -130,8 +153,6 @@
         for k in range(4)
     ]
 
-    received, second = lax.optimization_barrier((received, second))
-
     router32 = router.astype(F32)
     logits = jnp.dot(mixed * norm_gain, router32, precision=lax.Precision.HIGHEST)
     column = lax.broadcasted_iota(jnp.int32, (ROWS, 64), 1)
@@ -144,9 +165,11 @@
     factor = jax.nn.sigmoid(stats[1] * inverse_rms) * inverse_rms
 
     place = x.astype(jnp.int32).reshape(1)
-    pre = exchange(run(pre_kernel, (4, 512, 256), place, received, *first), "x")
-    hidden = exchange(run(hidden_kernel, (4, 512, 256), None, pre), "x")
-    result = run(result_kernel, (2, 512, 512), place, hidden, *second).reshape(128, ROOM, 512)
+    pre = run(pre_kernel, spot(4, 512, 256), place, [received], first)
+    pre, second = lax.optimization_barrier((pre, second))
+    hidden = exchange(run(hidden_kernel, spot(4, 512, 256), None, [exchange(pre, "x")]), "x")
+    result = run(result_kernel, spot(2, 512, 512), place, [hidden], second)
+    result = result.reshape(128, ROOM, 512)
     returned = exchange(result, ("zh",) + EXPERT).reshape(2, 512, 512)
     rows = dot32(placing, returned[0]) + dot32(placing, returned[1])
     return (mixed + factor[:, None] * rows).astype(BF16)

time: 251 us -> 238 us (0.948)
  waiting for transfers between devices: 83.2 us -> 66.3 us
  Pallas kernels: 3.69 us -> 6.79 us
    ppermute x6, waiting for transfers between devices: 41.9 us -> 10.7 us  [shift(): return lax.ppermute(block, 'x', [(i, (i + places) % 4) for i in range(4)])]
    all_to_all x4, waiting for transfers between devices: 14.3 us -> 25.8 us  [exchange(): return lax.all_to_all(blocks, axes, split_axis=0, concat_axis=0, tiled=True)]
    pallas_call x3, Pallas kernels: 3.69 us -> 6.79 us  [run(): pl.pallas_call(kernel, out_shape=shapes, in_specs=[smem] * len(flags) + [...]
    ppermute x0 -> x1, waiting for transfers between devices: none -> 2.8 us  [body(): other = lax.ppermute(half, 'c', [(0, 1), (1, 0)])]
    unnamed x41 -> x31, local copies, waits for them, and re-layouts: 5.47 us -> 3.07 us
  transfers between devices with their start and end apart: 14 -> 15, of which waited for: 9 -> 9; matrix products, arithmetic and copies ran while one was open for 4% -> 7% of each run, Pallas kernels for 0% -> 1%
where the time goes in v5:
time: 238 us; the launch traced here: 237 us
  starting transfers between devices  75.9 us (32%)
  waiting for transfers between devices  66.3 us (28%)
  blocking collectives  51.7 us (22%)
  between operations  13.8 us (6%)
  local copies, waits for them, and re-layouts  12.6 us (5%)
  matrix products  7.95 us (3%)
  Pallas kernels  6.79 us (3%)
    all_to_all x4, starting transfers between devices, exchange(): return lax.all_to_all(blocks, axes, split_axis=0, concat_axis=0, tiled=True)  40.5 us
    all_to_all x2, blocking collectives, exchange(): return lax.all_to_all(blocks, axes, split_axis=0, concat_axis=0, tiled=True)  35.5 us
    all_to_all x4, waiting for transfers between devices, exchange(): return lax.all_to_all(blocks, axes, split_axis=0, concat_axis=0, tiled=True)  25.8 us
    ppermute x6, starting transfers between devices, shift(): return lax.ppermute(block, 'x', [(i, (i + places) % 4) for i in range(4)])  21.1 us
    ppermute x1, waiting for transfers between devices, body(): stats = stats + lax.ppermute(stats, 'zh', [(0, 1), (1, 0)])  20.4 us
    all_gather x1, blocking collectives, body(): half = lax.all_gather(out_proj, 'zl', axis=0)  16.2 us
    ppermute x6, waiting for transfers between devices, shift(): return lax.ppermute(block, 'x', [(i, (i + places) % 4) for i in range(4)])  10.7 us
    ppermute x1, starting transfers between devices, body(): stats = stats + lax.ppermute(stats, 'zh', [(0, 1), (1, 0)])  6.82 us
  transfers between devices with their start and end apart: 15, of which 9 were waited for; matrix products, arithmetic and copies ran while one was open for 7% of the time, Pallas kernels for 1%

profile of v5, /device:TPU:96, one launch (start us, length us, event | category | flops | bytes accessed | tf_op | source)
XLA Modules:
  0.0 236.8 jit_solution(9892510156519162948)
XLA Ops:
  6.5 16.2 %all-gather = bf16[128,512]{1,0:T(8,128)(2,1)} all-gather(bf16[32,512]{1,0:T(8,128)(2,1)} %param.19), channel_id=2, replica_groups=mesh['zl'=4,'y'=8,'c'=2,'x'=4,'zh'=2] {'zl'}, dimensions={0}, use_global_device_ids=true | all-gather | bytes 163840 | tf_op jit(solution)/shard_map/all_gather | solution.py:118
  25.5 10.1 %all-to-all-start = ((bf16[8,2,32,256]{3,2,1,0:T(8,128)(2,1)}), bf16[8,2,32,256]{3,2,1,0:T(8,128)(2,1)S(1)}, u32[]{:S(2)}, u32[]{:S(2)}) async-start(bf16[8,2,32,256]{3,2,1,0:T(8,128)(2,1)} %copy.38), calls=%async_computation | async-start | bytes 524288 | tf_op jit(solution)/shard_map/all_to_all | solution.py:19
  36.9 3.9 %collective-permute-start = (bf16[1024,256]{1,0:T(8,128)(2,1)}, bf16[1024,256]{1,0:T(8,128)(2,1)S(1)}, u32[]{:S(2)}, u32[]{:S(2)}) collective-permute-start(bf16[1024,256]{1,0:T(8,128)(2,1)} %get-tuple-element.36), channel_id=1, source_target_pairs={{0,2},{2,4},{4,6},{6,0},{1,3},{3,5},{5,7},{7,1},{8,10},{10,12},{12... | collective-permute-start | bytes 1572872 | tf_op jit(solution)/shard_map/ppermute | solution.py:29
  40.8 4.6 %collective-permute-start.1 = (bf16[1024,256]{1,0:T(8,128)(2,1)}, bf16[1024,256]{1,0:T(8,128)(2,1)S(1)}, u32[]{:S(2)}, u32[]{:S(2)}) collective-permute-start(bf16[1024,256]{1,0:T(8,128)(2,1)} %get-tuple-element.38), channel_id=1, source_target_pairs={{0,4},{2,6},{4,0},{6,2},{1,5},{3,7},{5,1},{7,3},{8,12},{10,14},{12... | collective-permute-start | bytes 1572872 | tf_op jit(solution)/shard_map/ppermute | solution.py:29
  45.4 3.4 %collective-permute-start.2 = (bf16[1024,256]{1,0:T(8,128)(2,1)}, bf16[1024,256]{1,0:T(8,128)(2,1)S(1)}, u32[]{:S(2)}, u32[]{:S(2)}) collective-permute-start(bf16[1024,256]{1,0:T(8,128)(2,1)} %get-tuple-element.35), channel_id=1, source_target_pairs={{0,6},{2,0},{4,2},{6,4},{1,7},{3,1},{5,3},{7,5},{8,14},{10,8},{12,... | collective-permute-start | bytes 1572872 | tf_op jit(solution)/shard_map/ppermute | solution.py:29
  51.8 1.3 convolution_convert_fusion.1
  54.2 6.7 %all-to-all-start.1 = ((bf16[8,256,256]{1,2,0:T(8,128)(2,1)}), bf16[8,256,256]{1,2,0:T(8,128)(2,1)}, u32[]{:S(2)}, u32[]{:S(2)}) async-start(bf16[8,256,256]{1,2,0:T(8,128)(2,1)} %broadcast_in_dim.40), calls=%async_computation.1 | async-start | bytes 2097152 | tf_op jit(solution)/shard_map/all_to_all | solution.py:19
  60.8 8.0 %collective-permute-done.1.two = bf16[1024,256]{1,0:T(8,128)(2,1)S(1)} collective-permute-done((bf16[1024,256]{1,0:T(8,128)(2,1)}, bf16[1024,256]{1,0:T(8,128)(2,1)S(1)}, u32[]{:S(2)}, u32[]{:S(2)}) %collective-permute-start.1) | collective-permute-done | bytes 524320 | tf_op jit(solution)/shard_map/ppermute | solution.py:29
  68.8 1.9 collective-permute-start.3
  70.7 2.8 %collective-permute-done.3 = bf16[8,4,32,512]{3,2,1,0:T(8,128)(2,1)S(1)} collective-permute-done((bf16[8,4,32,512]{3,2,1,0:T(8,128)(2,1)}, bf16[8,4,32,512]{3,2,1,0:T(8,128)(2,1)S(1)}, u32[]{:S(2)}, u32[]{:S(2)}) %collective-permute-start.3) | collective-permute-done | bytes 1048608 | tf_op jit(solution)/shard_map/ppermute | solution.py:121
  73.5 1.4 select_bitcast_fusion.1
  75.1 1.6 copy.43
  76.7 10.7 %all-to-all-done.1 = bf16[8,256,256]{1,2,0:T(8,128)(2,1)} async-done(((bf16[8,256,256]{1,2,0:T(8,128)(2,1)}), bf16[8,256,256]{1,2,0:T(8,128)(2,1)}, u32[]{:S(2)}, u32[]{:S(2)}) %all-to-all-start.1) | async-done | bytes 1048608 | tf_op jit(solution)/shard_map/all_to_all | solution.py:19
  87.4 2.7 %multiply_reduce_fusion = (f32[256]{0:T(256)S(1)}, f32[256,512]{1,0:T(8,128)S(1)}) fusion(bf16[256,2048]{0,1:T(8,128)(2,1)} %bitcast.8, bf16[2048,512]{1,0:T(8,128)(2,1)} %bitcast.73, bf16[256,512]{1,0:T(8,128)(2,1)S(1)} %copy-done.13), kind=kOutput, calls=%fused_computation.23 | convolution fusion | flops 537394944 | bytes 3933184 | tf_op jit(solution)/shard_map/dot_general | solution.py:33
  91.7 9.8 %all-to-all-start.2 = ((bf16[128,8,512]{2,1,0:T(8,128)(2,1)}), bf16[128,8,512]{2,1,0:T(8,128)(2,1)S(1)}, u32[]{:S(2)}, u32[]{:S(2)}) async-start(bf16[128,8,512]{2,1,0:T(8,128)(2,1)} %bitcast.71), calls=%async_computation.2 | async-start | bytes 2097152 | tf_op jit(solution)/shard_map/all_to_all | solution.py:19
  101.5 2.7 %constant_dynamic-slice_fusion = (bf16[256,1024]{1,0:T(8,128)(2,1)}, bf16[256,1024]{1,0:T(8,128)(2,1)}, bf16[256,1024]{1,0:T(8,128)(2,1)}, bf16[256,1024]{1,0:T(8,128)(2,1)S(1)}) fusion(bf16[256,4096]{1,0:T(8,128)(2,1)} %bitcast.74, s32[]{:T(128)S(6)} %select_n.72, s32[]{:T(128)S(6)} %select_n.70, s32[]{:T(128)S(6)} %select_n.68, s32[]{:T(128)S(6)} %select_n.66), kind=kLoop, calls=%fused_computation.41 | loop fusion | bytes 4194320 | tf_op jit(solution)/shard_map/dynamic_slice | solution.py:152
  104.2 1.9 collective-permute-start.7
  106.1 4.2 %collective-permute-start.8 = (bf16[256,1024]{1,0:T(8,128)(2,1)}, bf16[256,1024]{1,0:T(8,128)(2,1)}, u32[]{:S(2)}, u32[]{:S(2)}) collective-permute-start(bf16[256,1024]{1,0:T(8,128)(2,1)} %get-tuple-element.30), channel_id=1, source_target_pairs={{0,4},{2,6},{4,0},{6,2},{1,5},{3,7},{5,1},{7,3},{8,12},{10,14},{12... | collective-permute-start | bytes 1572872 | tf_op jit(solution)/shard_map/ppermute | solution.py:29
  110.4 3.2 %collective-permute-start.9 = (bf16[256,1024]{1,0:T(8,128)(2,1)}, bf16[256,1024]{1,0:T(8,128)(2,1)}, u32[]{:S(2)}, u32[]{:S(2)}) collective-permute-start(bf16[256,1024]{1,0:T(8,128)(2,1)} %get-tuple-element.29), channel_id=1, source_target_pairs={{0,6},{2,0},{4,2},{6,4},{1,7},{3,1},{5,3},{7,5},{8,14},{10,8},{12,... | collective-permute-start | bytes 1572872 | tf_op jit(solution)/shard_map/ppermute | solution.py:29
  113.5 15.1 %all-to-all-done.2 = bf16[128,8,512]{2,1,0:T(8,128)(2,1)S(1)} async-done(((bf16[128,8,512]{2,1,0:T(8,128)(2,1)}), bf16[128,8,512]{2,1,0:T(8,128)(2,1)S(1)}, u32[]{:S(2)}, u32[]{:S(2)}) %all-to-all-start.2) | async-done | bytes 1048608 | tf_op jit(solution)/shard_map/all_to_all | solution.py:19
  129.7 2.9 %shard_map.130 = bf16[4,512,256]{2,1,0:T(8,128)(2,1)S(1)} custom-call(s32[1]{0:T(128)} %bitcast.25.place, bf16[2,512,512]{2,1,0:T(8,128)(2,1)S(1)} %bitcast.70, bf16[1024,256]{1,0:T(8,128)(2,1)S(1)} %get-tuple-element.19.own, bf16[1024,256]{1,0:T(8,128)(2,1)S(1)} %collective-permute-done.one, bf16[1024,256]{1,0:T(8,128)(2,1)S(1)} %collective-permute-done.1.two, ...), custom_call_target="tpu_custom_call" | custom-call | tf_op jit(solution)/shard_map/pallas_call | solution.py:78
  132.8 2.5 %collective-permute-done.9.three = bf16[256,1024]{1,0:T(8,128)(2,1)} collective-permute-done((bf16[256,1024]{1,0:T(8,128)(2,1)}, bf16[256,1024]{1,0:T(8,128)(2,1)}, u32[]{:S(2)}, u32[]{:S(2)}) %collective-permute-start.9) | collective-permute-done | bytes 524320 | tf_op jit(solution)/shard_map/ppermute | solution.py:29
  135.4 19.0 %all_to_all.30.parts = bf16[4,512,256]{2,1,0:T(8,128)(2,1)S(1)} all-to-all(bf16[4,512,256]{2,1,0:T(8,128)(2,1)S(1)} %shard_map.130), channel_id=1, replica_groups=mesh['zl'=4,'y'=8,'c'=2,'x'=4,'zh'=2] {'x'}, dimensions={0} | all-to-all | bytes 2097152 | tf_op jit(solution)/shard_map/all_to_all | solution.py:19
  154.5 16.5 %all_to_all.31.hidden = bf16[4,512,256]{2,1,0:T(8,128)(2,1)S(1)} all-to-all(bf16[4,512,256]{2,1,0:T(8,128)(2,1)S(1)} %shard_map.131), channel_id=1, replica_groups=mesh['zl'=4,'y'=8,'c'=2,'x'=4,'zh'=2] {'x'}, dimensions={0} | all-to-all | bytes 2097152 | tf_op jit(solution)/shard_map/all_to_all | solution.py:19
  171.0 3.7 %shard_map.132 = bf16[2,512,512]{2,1,0:T(8,128)(2,1)} custom-call(s32[1]{0:T(128)} %bitcast.25.place, bf16[4,512,256]{2,1,0:T(8,128)(2,1)S(1)} %all_to_all.31.hidden, bf16[256,1024]{1,0:T(8,128)(2,1)S(1)} %get-tuple-element.25.own, bf16[256,1024]{1,0:T(8,128)(2,1)} %collective-permute-done.7.one, bf16[256,1024]{1,0:T(8,128)(2,1)} %collective-permute-done.8.two, ...), custom_call_target="tpu_custom_call" | custom-call | tf_op jit(solution)/shard_map/pallas_call | solution.py:78
  174.7 13.9 %all-to-all-start.5 = ((bf16[128,8,512]{2,1,0:T(8,128)(2,1)}), bf16[128,8,512]{2,1,0:T(8,128)(2,1)S(1)}, u32[]{:S(2)}, u32[]{:S(2)}) async-start(bf16[128,8,512]{2,1,0:T(8,128)(2,1)} %bitcast.30), calls=%async_computation.5 | async-start | bytes 2097152 | tf_op jit(solution)/shard_map/all_to_all | solution.py:19
  189.1 6.8 %collective-permute-start.4 = (f32[2,256]{1,0:T(2,128)S(1)}, f32[2,256]{1,0:T(2,128)S(1)}, u32[]{:S(2)}, u32[]{:S(2)}) collective-permute-start(f32[2,256]{1,0:T(2,128)S(1)} %pad_maximum_fusion), channel_id=1, source_target_pairs={{0,1},{1,0},{2,3},{3,2},{4,5},{5,4},{6,7},{7,6},{8,9},{9,8},{10,11... | collective-permute-start | bytes 6152 | tf_op jit(solution)/shard_map/ppermute | solution.py:161
  195.9 20.4 %collective-permute-done.4 = f32[2,256]{1,0:T(2,128)S(1)} collective-permute-done((f32[2,256]{1,0:T(2,128)S(1)}, f32[2,256]{1,0:T(2,128)S(1)}, u32[]{:S(2)}, u32[]{:S(2)}) %collective-permute-start.4) | collective-permute-done | bytes 2080 | tf_op jit(solution)/shard_map/ppermute | solution.py:161
  216.3 2.5 %collective-permute-start.5 = (f32[2,256]{1,0:T(2,128)S(1)}, f32[2,256]{1,0:T(2,128)S(1)}, u32[]{:S(2)}, u32[]{:S(2)}) collective-permute-start(f32[2,256]{1,0:T(2,128)S(1)} %fusion.25), channel_id=1, source_target_pairs={{0,2},{2,0},{4,6},{6,4},{1,3},{3,1},{5,7},{7,5},{8,10},{10,8},{12,... | collective-permute-start | bytes 6152 | tf_op jit(solution)/shard_map/ppermute | solution.py:162
  218.8 3.0 %collective-permute-done.5 = f32[2,256]{1,0:T(2,128)S(1)} collective-permute-done((f32[2,256]{1,0:T(2,128)S(1)}, f32[2,256]{1,0:T(2,128)S(1)}, u32[]{:S(2)}, u32[]{:S(2)}) %collective-permute-start.5) | collective-permute-done | bytes 2080 | tf_op jit(solution)/shard_map/ppermute | solution.py:162
  221.8 3.1 %collective-permute-start.6 = (f32[2,256]{1,0:T(2,128)S(1)}, f32[2,256]{1,0:T(2,128)S(1)}, u32[]{:S(2)}, u32[]{:S(2)}) collective-permute-start(f32[2,256]{1,0:T(2,128)S(1)} %fusion.37), channel_id=1, source_target_pairs={{0,6},{6,0},{2,4},{4,2},{1,7},{7,1},{3,5},{5,3},{8,14},{14,8},{10,... | collective-permute-start | bytes 6152 | tf_op jit(solution)/shard_map/ppermute | solution.py:163
  224.9 3.6 %collective-permute-done.6 = f32[2,256]{1,0:T(2,128)S(1)} collective-permute-done((f32[2,256]{1,0:T(2,128)S(1)}, f32[2,256]{1,0:T(2,128)S(1)}, u32[]{:S(2)}, u32[]{:S(2)}) %collective-permute-start.6) | collective-permute-done | bytes 2080 | tf_op jit(solution)/shard_map/ppermute | solution.py:163
  (64 shorter events, 13.0 us)
Async XLA Ops:
  6.5 182.1 %copy-start = (bf16[512,64]{0,1:T(8,128)(2,1)S(1)}, bf16[512,64]{0,1:T(8,128)(2,1)}, u32[]{:S(2)}) copy-start(bf16[512,64]{0,1:T(8,128)(2,1)} %param.21) | copy-start | bytes 196612
  6.5 29.1 %copy-start.5 = (bf16[1,4096,256]{2,1,0:T(8,128)(2,1)S(1)}, bf16[1,4096,256]{2,1,0:T(8,128)(2,1)}, u32[]{:S(2)}) copy-start(bf16[1,4096,256]{2,1,0:T(8,128)(2,1)} %param.24) | copy-start | bytes 6291460
  6.5 62.2 %all-gather.4.cloned.1.call-start = ((), (), s32[]{:S(2)}) async-start(), calls=%async_computation.6 | async-start | bytes 1179648 | tf_op jit(solution)/shard_map/all_gather | solution.py:119
  25.5 23.6 %all-to-all-start = ((bf16[8,2,32,256]{3,2,1,0:T(8,128)(2,1)}), bf16[8,2,32,256]{3,2,1,0:T(8,128)(2,1)S(1)}, u32[]{:S(2)}, u32[]{:S(2)}) async-start(bf16[8,2,32,256]{3,2,1,0:T(8,128)(2,1)} %copy.38), calls=%async_computation | async-start | bytes 524288 | tf_op jit(solution)/shard_map/all_to_all | solution.py:19
  35.6 13.2 %copy-start.7 = (bf16[256,256]{1,0:T(8,128)(2,1)S(1)}, bf16[256,256]{1,0:T(8,128)(2,1)}, u32[]{:S(2)}) copy-start(bf16[256,256]{1,0:T(8,128)(2,1)} %param.13) | copy-start | bytes 393220
  35.6 13.3 %copy-start.10 = (s32[1,256]{1,0:T(1,128)S(1)}, s32[1,256]{1,0:T(1,128)}, u32[]{:S(2)}) copy-start(s32[1,256]{1,0:T(1,128)} %param.16) | copy-start | bytes 3076
  35.6 13.3 %copy-start.11 = (s32[1,256]{1,0:T(1,128)S(1)}, s32[1,256]{1,0:T(1,128)}, u32[]{:S(2)}) copy-start(s32[1,256]{1,0:T(1,128)} %param.17) | copy-start | bytes 3076
  36.9 23.9 %collective-permute-start = (bf16[1024,256]{1,0:T(8,128)(2,1)}, bf16[1024,256]{1,0:T(8,128)(2,1)S(1)}, u32[]{:S(2)}, u32[]{:S(2)}) collective-permute-start(bf16[1024,256]{1,0:T(8,128)(2,1)} %get-tuple-element.36), channel_id=1, source_target_pairs={{0,2},{2,4},{4,6},{6,0},{1,3},{3,5},{5,7},{7,1},{8,10},{10,12},{12... | collective-permute-start | bytes 1572872 | tf_op jit(solution)/shard_map/ppermute | solution.py:29
  40.8 28.0 %collective-permute-start.1 = (bf16[1024,256]{1,0:T(8,128)(2,1)}, bf16[1024,256]{1,0:T(8,128)(2,1)S(1)}, u32[]{:S(2)}, u32[]{:S(2)}) collective-permute-start(bf16[1024,256]{1,0:T(8,128)(2,1)} %get-tuple-element.38), channel_id=1, source_target_pairs={{0,4},{2,6},{4,0},{6,2},{1,5},{3,7},{5,1},{7,3},{8,12},{10,14},{12... | collective-permute-start | bytes 1572872 | tf_op jit(solution)/shard_map/ppermute | solution.py:29
  45.4 23.4 %collective-permute-start.2 = (bf16[1024,256]{1,0:T(8,128)(2,1)}, bf16[1024,256]{1,0:T(8,128)(2,1)S(1)}, u32[]{:S(2)}, u32[]{:S(2)}) collective-permute-start(bf16[1024,256]{1,0:T(8,128)(2,1)} %get-tuple-element.35), channel_id=1, source_target_pairs={{0,6},{2,0},{4,2},{6,4},{1,7},{3,1},{5,3},{7,5},{8,14},{10,8},{12,... | collective-permute-start | bytes 1572872 | tf_op jit(solution)/shard_map/ppermute | solution.py:29
  48.9 1.2 copy-start.6
  53.1 17.6 %copy-start.9 = (s32[1,256]{1,0:T(1,128)S(1)}, s32[1,256]{1,0:T(1,128)}, u32[]{:S(2)}) copy-start(s32[1,256]{1,0:T(1,128)} %param.22) | copy-start | bytes 3076
  53.1 17.6 %copy-start.12 = (s32[1,256]{1,0:T(1,128)S(1)}, s32[1,256]{1,0:T(1,128)}, u32[]{:S(2)}) copy-start(s32[1,256]{1,0:T(1,128)} %param.23) | copy-start | bytes 3076
  54.2 33.2 %all-to-all-start.1 = ((bf16[8,256,256]{1,2,0:T(8,128)(2,1)}), bf16[8,256,256]{1,2,0:T(8,128)(2,1)}, u32[]{:S(2)}, u32[]{:S(2)}) async-start(bf16[8,256,256]{1,2,0:T(8,128)(2,1)} %broadcast_in_dim.40), calls=%async_computation.1 | async-start | bytes 2097152 | tf_op jit(solution)/shard_map/all_to_all | solution.py:19
  68.8 6.1 %copy-start.1 = (bf16[1024,256]{1,0:T(8,128)(2,1)}, bf16[1024,256]{1,0:T(8,128)(2,1)S(1)}, u32[]{:S(2)}) copy-start(bf16[1024,256]{1,0:T(8,128)(2,1)S(1)} %collective-permute-done.2.three) | copy-start | bytes 1572868
  68.8 4.8 %collective-permute-start.3 = (bf16[8,4,32,512]{3,2,1,0:T(8,128)(2,1)}, bf16[8,4,32,512]{3,2,1,0:T(8,128)(2,1)S(1)}, u32[]{:S(2)}, u32[]{:S(2)}) collective-permute-start(bf16[8,4,32,512]{3,2,1,0:T(8,128)(2,1)} %bitcast.75), channel_id=1, source_target_pairs={{0,8},{8,0},{1,9},{9,1},{2,10},{10,2},{3,11},{11,3},{4,12},{12,4},... | collective-permute-start | bytes 3145736 | tf_op jit(solution)/shard_map/ppermute | solution.py:121
  75.1 12.3 %copy-start.13 = (bf16[256,512]{1,0:T(8,128)(2,1)S(1)}, bf16[256,512]{1,0:T(8,128)(2,1)}, u32[]{:S(2)}) copy-start(bf16[256,512]{1,0:T(8,128)(2,1)} %param.18) | copy-start | bytes 786436
  87.4 2.8 %copy-start.8 = (f32[512]{0:T(512)S(1)}, f32[512]{0:T(512)}, u32[]{:S(2)}) copy-start(f32[512]{0:T(512)} %param.20) | copy-start | bytes 6148
  90.1 1.5 copy-start.3
  91.7 36.9 %all-to-all-start.2 = ((bf16[128,8,512]{2,1,0:T(8,128)(2,1)}), bf16[128,8,512]{2,1,0:T(8,128)(2,1)S(1)}, u32[]{:S(2)}, u32[]{:S(2)}) async-start(bf16[128,8,512]{2,1,0:T(8,128)(2,1)} %bitcast.71), calls=%async_computation.2 | async-start | bytes 2097152 | tf_op jit(solution)/shard_map/all_to_all | solution.py:19
  104.2 28.6 %collective-permute-start.7 = (bf16[256,1024]{1,0:T(8,128)(2,1)}, bf16[256,1024]{1,0:T(8,128)(2,1)}, u32[]{:S(2)}, u32[]{:S(2)}) collective-permute-start(bf16[256,1024]{1,0:T(8,128)(2,1)} %get-tuple-element.31), channel_id=1, source_target_pairs={{0,2},{2,4},{4,6},{6,0},{1,3},{3,5},{5,7},{7,1},{8,10},{10,12},{12... | collective-permute-start | bytes 1572872 | tf_op jit(solution)/shard_map/ppermute | solution.py:29
  106.1 26.7 %collective-permute-start.8 = (bf16[256,1024]{1,0:T(8,128)(2,1)}, bf16[256,1024]{1,0:T(8,128)(2,1)}, u32[]{:S(2)}, u32[]{:S(2)}) collective-permute-start(bf16[256,1024]{1,0:T(8,128)(2,1)} %get-tuple-element.30), channel_id=1, source_target_pairs={{0,4},{2,6},{4,0},{6,2},{1,5},{3,7},{5,1},{7,3},{8,12},{10,14},{12... | collective-permute-start | bytes 1572872 | tf_op jit(solution)/shard_map/ppermute | solution.py:29
  110.4 25.0 %collective-permute-start.9 = (bf16[256,1024]{1,0:T(8,128)(2,1)}, bf16[256,1024]{1,0:T(8,128)(2,1)}, u32[]{:S(2)}, u32[]{:S(2)}) collective-permute-start(bf16[256,1024]{1,0:T(8,128)(2,1)} %get-tuple-element.29), channel_id=1, source_target_pairs={{0,6},{2,0},{4,2},{6,4},{1,7},{3,1},{5,3},{7,5},{8,14},{10,8},{12,... | collective-permute-start | bytes 1572872 | tf_op jit(solution)/shard_map/ppermute | solution.py:29
  128.6 1.0 copy-start.2
  174.7 13.9 %copy-start.4 = (f32[256,512]{1,0:T(8,128)S(1)}, f32[256,512]{1,0:T(8,128)}, u32[]{:S(2)}) copy-start(f32[256,512]{1,0:T(8,128)} %copy-done.3) | copy-start | bytes 1572868
  174.7 53.8 %all-to-all-start.5 = ((bf16[128,8,512]{2,1,0:T(8,128)(2,1)}), bf16[128,8,512]{2,1,0:T(8,128)(2,1)S(1)}, u32[]{:S(2)}, u32[]{:S(2)}) async-start(bf16[128,8,512]{2,1,0:T(8,128)(2,1)} %bitcast.30), calls=%async_computation.5 | async-start | bytes 2097152 | tf_op jit(solution)/shard_map/all_to_all | solution.py:19
  189.1 27.2 %collective-permute-start.4 = (f32[2,256]{1,0:T(2,128)S(1)}, f32[2,256]{1,0:T(2,128)S(1)}, u32[]{:S(2)}, u32[]{:S(2)}) collective-permute-start(f32[2,256]{1,0:T(2,128)S(1)} %pad_maximum_fusion), channel_id=1, source_target_pairs={{0,1},{1,0},{2,3},{3,2},{4,5},{5,4},{6,7},{7,6},{8,9},{9,8},{10,11... | collective-permute-start | bytes 6152 | tf_op jit(solution)/shard_map/ppermute | solution.py:161
  216.3 5.5 %collective-permute-start.5 = (f32[2,256]{1,0:T(2,128)S(1)}, f32[2,256]{1,0:T(2,128)S(1)}, u32[]{:S(2)}, u32[]{:S(2)}) collective-permute-start(f32[2,256]{1,0:T(2,128)S(1)} %fusion.25), channel_id=1, source_target_pairs={{0,2},{2,0},{4,6},{6,4},{1,3},{3,1},{5,7},{7,5},{8,10},{10,8},{12,... | collective-permute-start | bytes 6152 | tf_op jit(solution)/shard_map/ppermute | solution.py:162
  221.8 6.7 %collective-permute-start.6 = (f32[2,256]{1,0:T(2,128)S(1)}, f32[2,256]{1,0:T(2,128)S(1)}, u32[]{:S(2)}, u32[]{:S(2)}) collective-permute-start(f32[2,256]{1,0:T(2,128)S(1)} %fusion.37), channel_id=1, source_target_pairs={{0,6},{6,0},{2,4},{4,2},{1,7},{7,1},{3,5},{5,3},{8,14},{14,8},{10,... | collective-permute-start | bytes 6152 | tf_op jit(solution)/shard_map/ppermute | solution.py:163
Sparse Core Ops, SparseCore 0:
  22.9 41.2 all-gather.3

commit v6 on v5

--- a/solution.py
+++ b/solution.py
@@ -40,11 +40,9 @@
     return copies
 
 
-def pre_kernel(place, rows, own, one, two, three, out, held, done):
-    copies = fetch((own, one, two, three), held, done)
-    for k in range(4):
-        copies[k].wait()
-        total = dot32(rows[0], held[k, :512]) + dot32(rows[1], held[k, 512:])
+def pre_kernel(place, rows, own, one, two, three, out):
+    for k, weight in enumerate((own, one, two, three)):
+        total = dot32(rows[0], weight[:512]) + dot32(rows[1], weight[512:])
         out[(place[0] - k) % 4] = total.astype(BF16)
 
 
@@ -165,7 +163,7 @@
     factor = jax.nn.sigmoid(stats[1] * inverse_rms) * inverse_rms
 
     place = x.astype(jnp.int32).reshape(1)
-    pre = run(pre_kernel, spot(4, 512, 256), place, [received], first)
+    pre = run(pre_kernel, spot(4, 512, 256), place, [received, *first])
     pre, second = lax.optimization_barrier((pre, second))
     hidden = exchange(run(hidden_kernel, spot(4, 512, 256), None, [exchange(pre, "x")]), "x")
     result = run(result_kernel, spot(2, 512, 512), place, [hidden], second)

time: 238 us -> 238 us (level)
  no operation moved by 1% of the time
where the time goes in v6:
time: 238 us; the launch traced here: 237 us
  starting transfers between devices  75.9 us (32%)
  waiting for transfers between devices  68 us (29%)
  blocking collectives  51.7 us (22%)
  between operations  13.8 us (6%)
  local copies, waits for them, and re-layouts  12.6 us (5%)
  matrix products  7.95 us (3%)
  Pallas kernels  5.14 us (2%)
    all_to_all x4, starting transfers between devices, exchange(): return lax.all_to_all(blocks, axes, split_axis=0, concat_axis=0, tiled=True)  40.5 us
    all_to_all x2, blocking collectives, exchange(): return lax.all_to_all(blocks, axes, split_axis=0, concat_axis=0, tiled=True)  35.5 us
    all_to_all x4, waiting for transfers between devices, exchange(): return lax.all_to_all(blocks, axes, split_axis=0, concat_axis=0, tiled=True)  25.8 us
    ppermute x6, starting transfers between devices, shift(): return lax.ppermute(block, 'x', [(i, (i + places) % 4) for i in range(4)])  21.1 us
    ppermute x1, waiting for transfers between devices, body(): stats = stats + lax.ppermute(stats, 'zh', [(0, 1), (1, 0)])  20.4 us
    all_gather x1, blocking collectives, body(): half = lax.all_gather(out_proj, 'zl', axis=0)  16.2 us
    ppermute x6, waiting for transfers between devices, shift(): return lax.ppermute(block, 'x', [(i, (i + places) % 4) for i in range(4)])  12.4 us
    ppermute x1, starting transfers between devices, body(): stats = stats + lax.ppermute(stats, 'zh', [(0, 1), (1, 0)])  6.82 us
  transfers between devices with their start and end apart: 15, of which 9 were waited for; matrix products, arithmetic and copies ran while one was open for 7% of the time, Pallas kernels for 1%

profile of v6, /device:TPU:96, one launch (start us, length us, event | category | flops | bytes accessed | tf_op | source)
XLA Modules:
  0.0 236.8 jit_solution(3651275489988260089)
XLA Ops:
  6.5 16.2 %all-gather = bf16[128,512]{1,0:T(8,128)(2,1)} all-gather(bf16[32,512]{1,0:T(8,128)(2,1)} %param.19), channel_id=2, replica_groups=mesh['zl'=4,'y'=8,'c'=2,'x'=4,'zh'=2] {'zl'}, dimensions={0}, use_global_device_ids=true | all-gather | bytes 163840 | tf_op jit(solution)/shard_map/all_gather | solution.py:116
  25.5 10.1 %all-to-all-start = ((bf16[8,2,32,256]{3,2,1,0:T(8,128)(2,1)}), bf16[8,2,32,256]{3,2,1,0:T(8,128)(2,1)S(1)}, u32[]{:S(2)}, u32[]{:S(2)}) async-start(bf16[8,2,32,256]{3,2,1,0:T(8,128)(2,1)} %copy.38), calls=%async_computation | async-start | bytes 524288 | tf_op jit(solution)/shard_map/all_to_all | solution.py:19
  36.9 3.9 %collective-permute-start = (bf16[1024,256]{1,0:T(8,128)(2,1)}, bf16[1024,256]{1,0:T(8,128)(2,1)S(1)}, u32[]{:S(2)}, u32[]{:S(2)}) collective-permute-start(bf16[1024,256]{1,0:T(8,128)(2,1)} %get-tuple-element.36), channel_id=1, source_target_pairs={{0,2},{2,4},{4,6},{6,0},{1,3},{3,5},{5,7},{7,1},{8,10},{10,12},{12... | collective-permute-start | bytes 1572872 | tf_op jit(solution)/shard_map/ppermute | solution.py:29
  40.8 4.6 %collective-permute-start.1 = (bf16[1024,256]{1,0:T(8,128)(2,1)}, bf16[1024,256]{1,0:T(8,128)(2,1)S(1)}, u32[]{:S(2)}, u32[]{:S(2)}) collective-permute-start(bf16[1024,256]{1,0:T(8,128)(2,1)} %get-tuple-element.38), channel_id=1, source_target_pairs={{0,4},{2,6},{4,0},{6,2},{1,5},{3,7},{5,1},{7,3},{8,12},{10,14},{12... | collective-permute-start | bytes 1572872 | tf_op jit(solution)/shard_map/ppermute | solution.py:29
  45.4 3.4 %collective-permute-start.2 = (bf16[1024,256]{1,0:T(8,128)(2,1)}, bf16[1024,256]{1,0:T(8,128)(2,1)S(1)}, u32[]{:S(2)}, u32[]{:S(2)}) collective-permute-start(bf16[1024,256]{1,0:T(8,128)(2,1)} %get-tuple-element.35), channel_id=1, source_target_pairs={{0,6},{2,0},{4,2},{6,4},{1,7},{3,1},{5,3},{7,5},{8,14},{10,8},{12,... | collective-permute-start | bytes 1572872 | tf_op jit(solution)/shard_map/ppermute | solution.py:29
  51.8 1.3 convolution_convert_fusion.1
  54.2 6.7 %all-to-all-start.1 = ((bf16[8,256,256]{1,2,0:T(8,128)(2,1)}), bf16[8,256,256]{1,2,0:T(8,128)(2,1)}, u32[]{:S(2)}, u32[]{:S(2)}) async-start(bf16[8,256,256]{1,2,0:T(8,128)(2,1)} %broadcast_in_dim.40), calls=%async_computation.1 | async-start | bytes 2097152 | tf_op jit(solution)/shard_map/all_to_all | solution.py:19
  60.8 8.0 %collective-permute-done.1.two = bf16[1024,256]{1,0:T(8,128)(2,1)S(1)} collective-permute-done((bf16[1024,256]{1,0:T(8,128)(2,1)}, bf16[1024,256]{1,0:T(8,128)(2,1)S(1)}, u32[]{:S(2)}, u32[]{:S(2)}) %collective-permute-start.1) | collective-permute-done | bytes 524320 | tf_op jit(solution)/shard_map/ppermute | solution.py:29
  68.8 1.9 collective-permute-start.3
  70.7 2.8 %collective-permute-done.3 = bf16[8,4,32,512]{3,2,1,0:T(8,128)(2,1)S(1)} collective-permute-done((bf16[8,4,32,512]{3,2,1,0:T(8,128)(2,1)}, bf16[8,4,32,512]{3,2,1,0:T(8,128)(2,1)S(1)}, u32[]{:S(2)}, u32[]{:S(2)}) %collective-permute-start.3) | collective-permute-done | bytes 1048608 | tf_op jit(solution)/shard_map/ppermute | solution.py:119
  73.5 1.4 select_bitcast_fusion.1
  75.1 1.6 copy.43
  76.7 10.7 %all-to-all-done.1 = bf16[8,256,256]{1,2,0:T(8,128)(2,1)} async-done(((bf16[8,256,256]{1,2,0:T(8,128)(2,1)}), bf16[8,256,256]{1,2,0:T(8,128)(2,1)}, u32[]{:S(2)}, u32[]{:S(2)}) %all-to-all-start.1) | async-done | bytes 1048608 | tf_op jit(solution)/shard_map/all_to_all | solution.py:19
  87.4 2.7 %multiply_reduce_fusion = (f32[256]{0:T(256)S(1)}, f32[256,512]{1,0:T(8,128)S(1)}) fusion(bf16[256,2048]{0,1:T(8,128)(2,1)} %bitcast.8, bf16[2048,512]{1,0:T(8,128)(2,1)} %bitcast.73, bf16[256,512]{1,0:T(8,128)(2,1)S(1)} %copy-done.13), kind=kOutput, calls=%fused_computation.23 | convolution fusion | flops 537394944 | bytes 3933184 | tf_op jit(solution)/shard_map/dot_general | solution.py:33
  91.7 9.8 %all-to-all-start.2 = ((bf16[128,8,512]{2,1,0:T(8,128)(2,1)}), bf16[128,8,512]{2,1,0:T(8,128)(2,1)S(1)}, u32[]{:S(2)}, u32[]{:S(2)}) async-start(bf16[128,8,512]{2,1,0:T(8,128)(2,1)} %bitcast.71), calls=%async_computation.2 | async-start | bytes 2097152 | tf_op jit(solution)/shard_map/all_to_all | solution.py:19
  101.5 2.7 %constant_dynamic-slice_fusion = (bf16[256,1024]{1,0:T(8,128)(2,1)}, bf16[256,1024]{1,0:T(8,128)(2,1)}, bf16[256,1024]{1,0:T(8,128)(2,1)}, bf16[256,1024]{1,0:T(8,128)(2,1)S(1)}) fusion(bf16[256,4096]{1,0:T(8,128)(2,1)} %bitcast.74, s32[]{:T(128)S(6)} %select_n.72, s32[]{:T(128)S(6)} %select_n.70, s32[]{:T(128)S(6)} %select_n.68, s32[]{:T(128)S(6)} %select_n.66), kind=kLoop, calls=%fused_computation.41 | loop fusion | bytes 4194320 | tf_op jit(solution)/shard_map/dynamic_slice | solution.py:150
  104.2 1.9 collective-permute-start.7
  106.1 4.2 %collective-permute-start.8 = (bf16[256,1024]{1,0:T(8,128)(2,1)}, bf16[256,1024]{1,0:T(8,128)(2,1)}, u32[]{:S(2)}, u32[]{:S(2)}) collective-permute-start(bf16[256,1024]{1,0:T(8,128)(2,1)} %get-tuple-element.30), channel_id=1, source_target_pairs={{0,4},{2,6},{4,0},{6,2},{1,5},{3,7},{5,1},{7,3},{8,12},{10,14},{12... | collective-permute-start | bytes 1572872 | tf_op jit(solution)/shard_map/ppermute | solution.py:29
  110.4 3.2 %collective-permute-start.9 = (bf16[256,1024]{1,0:T(8,128)(2,1)}, bf16[256,1024]{1,0:T(8,128)(2,1)}, u32[]{:S(2)}, u32[]{:S(2)}) collective-permute-start(bf16[256,1024]{1,0:T(8,128)(2,1)} %get-tuple-element.29), channel_id=1, source_target_pairs={{0,6},{2,0},{4,2},{6,4},{1,7},{3,1},{5,3},{7,5},{8,14},{10,8},{12,... | collective-permute-start | bytes 1572872 | tf_op jit(solution)/shard_map/ppermute | solution.py:29
  113.5 15.1 %all-to-all-done.2 = bf16[128,8,512]{2,1,0:T(8,128)(2,1)S(1)} async-done(((bf16[128,8,512]{2,1,0:T(8,128)(2,1)}), bf16[128,8,512]{2,1,0:T(8,128)(2,1)S(1)}, u32[]{:S(2)}, u32[]{:S(2)}) %all-to-all-start.2) | async-done | bytes 1048608 | tf_op jit(solution)/shard_map/all_to_all | solution.py:19
  131.0 1.9 collective-permute-done.7.one
  132.8 2.5 %collective-permute-done.9.three = bf16[256,1024]{1,0:T(8,128)(2,1)} collective-permute-done((bf16[256,1024]{1,0:T(8,128)(2,1)}, bf16[256,1024]{1,0:T(8,128)(2,1)}, u32[]{:S(2)}, u32[]{:S(2)}) %collective-permute-start.9) | collective-permute-done | bytes 524320 | tf_op jit(solution)/shard_map/ppermute | solution.py:29
  135.4 19.0 %all_to_all.30.parts = bf16[4,512,256]{2,1,0:T(8,128)(2,1)S(1)} all-to-all(bf16[4,512,256]{2,1,0:T(8,128)(2,1)S(1)} %shard_map.130), channel_id=1, replica_groups=mesh['zl'=4,'y'=8,'c'=2,'x'=4,'zh'=2] {'x'}, dimensions={0} | all-to-all | bytes 2097152 | tf_op jit(solution)/shard_map/all_to_all | solution.py:19
  154.5 16.5 %all_to_all.31.hidden = bf16[4,512,256]{2,1,0:T(8,128)(2,1)S(1)} all-to-all(bf16[4,512,256]{2,1,0:T(8,128)(2,1)S(1)} %shard_map.131), channel_id=1, replica_groups=mesh['zl'=4,'y'=8,'c'=2,'x'=4,'zh'=2] {'x'}, dimensions={0} | all-to-all | bytes 2097152 | tf_op jit(solution)/shard_map/all_to_all | solution.py:19
  171.0 3.7 %shard_map.132 = bf16[2,512,512]{2,1,0:T(8,128)(2,1)} custom-call(s32[1]{0:T(128)} %bitcast.25.place, bf16[4,512,256]{2,1,0:T(8,128)(2,1)S(1)} %all_to_all.31.hidden, bf16[256,1024]{1,0:T(8,128)(2,1)S(1)} %get-tuple-element.25.own, bf16[256,1024]{1,0:T(8,128)(2,1)} %collective-permute-done.7.one, bf16[256,1024]{1,0:T(8,128)(2,1)} %collective-permute-done.8.two, ...), custom_call_target="tpu_custom_call" | custom-call | tf_op jit(solution)/shard_map/pallas_call | solution.py:76
  174.7 13.9 %all-to-all-start.5 = ((bf16[128,8,512]{2,1,0:T(8,128)(2,1)}), bf16[128,8,512]{2,1,0:T(8,128)(2,1)S(1)}, u32[]{:S(2)}, u32[]{:S(2)}) async-start(bf16[128,8,512]{2,1,0:T(8,128)(2,1)} %bitcast.30), calls=%async_computation.5 | async-start | bytes 2097152 | tf_op jit(solution)/shard_map/all_to_all | solution.py:19
  189.1 6.8 %collective-permute-start.4 = (f32[2,256]{1,0:T(2,128)S(1)}, f32[2,256]{1,0:T(2,128)S(1)}, u32[]{:S(2)}, u32[]{:S(2)}) collective-permute-start(f32[2,256]{1,0:T(2,128)S(1)} %pad_maximum_fusion), channel_id=1, source_target_pairs={{0,1},{1,0},{2,3},{3,2},{4,5},{5,4},{6,7},{7,6},{8,9},{9,8},{10,11... | collective-permute-start | bytes 6152 | tf_op jit(solution)/shard_map/ppermute | solution.py:159
  195.9 20.4 %collective-permute-done.4 = f32[2,256]{1,0:T(2,128)S(1)} collective-permute-done((f32[2,256]{1,0:T(2,128)S(1)}, f32[2,256]{1,0:T(2,128)S(1)}, u32[]{:S(2)}, u32[]{:S(2)}) %collective-permute-start.4) | collective-permute-done | bytes 2080 | tf_op jit(solution)/shard_map/ppermute | solution.py:159
  216.3 2.5 %collective-permute-start.5 = (f32[2,256]{1,0:T(2,128)S(1)}, f32[2,256]{1,0:T(2,128)S(1)}, u32[]{:S(2)}, u32[]{:S(2)}) collective-permute-start(f32[2,256]{1,0:T(2,128)S(1)} %fusion.25), channel_id=1, source_target_pairs={{0,2},{2,0},{4,6},{6,4},{1,3},{3,1},{5,7},{7,5},{8,10},{10,8},{12,... | collective-permute-start | bytes 6152 | tf_op jit(solution)/shard_map/ppermute | solution.py:160
  218.8 3.0 %collective-permute-done.5 = f32[2,256]{1,0:T(2,128)S(1)} collective-permute-done((f32[2,256]{1,0:T(2,128)S(1)}, f32[2,256]{1,0:T(2,128)S(1)}, u32[]{:S(2)}, u32[]{:S(2)}) %collective-permute-start.5) | collective-permute-done | bytes 2080 | tf_op jit(solution)/shard_map/ppermute | solution.py:160
  221.8 3.1 %collective-permute-start.6 = (f32[2,256]{1,0:T(2,128)S(1)}, f32[2,256]{1,0:T(2,128)S(1)}, u32[]{:S(2)}, u32[]{:S(2)}) collective-permute-start(f32[2,256]{1,0:T(2,128)S(1)} %fusion.37), channel_id=1, source_target_pairs={{0,6},{6,0},{2,4},{4,2},{1,7},{7,1},{3,5},{5,3},{8,14},{14,8},{10,... | collective-permute-start | bytes 6152 | tf_op jit(solution)/shard_map/ppermute | solution.py:161
  224.9 3.6 %collective-permute-done.6 = f32[2,256]{1,0:T(2,128)S(1)} collective-permute-done((f32[2,256]{1,0:T(2,128)S(1)}, f32[2,256]{1,0:T(2,128)S(1)}, u32[]{:S(2)}, u32[]{:S(2)}) %collective-permute-start.6) | collective-permute-done | bytes 2080 | tf_op jit(solution)/shard_map/ppermute | solution.py:161
  (64 shorter events, 14.0 us)
Async XLA Ops:
  6.5 182.1 %copy-start = (bf16[512,64]{0,1:T(8,128)(2,1)S(1)}, bf16[512,64]{0,1:T(8,128)(2,1)}, u32[]{:S(2)}) copy-start(bf16[512,64]{0,1:T(8,128)(2,1)} %param.21) | copy-start | bytes 196612
  6.5 29.1 %copy-start.5 = (bf16[1,4096,256]{2,1,0:T(8,128)(2,1)S(1)}, bf16[1,4096,256]{2,1,0:T(8,128)(2,1)}, u32[]{:S(2)}) copy-start(bf16[1,4096,256]{2,1,0:T(8,128)(2,1)} %param.24) | copy-start | bytes 6291460
  6.5 62.2 %all-gather.4.cloned.1.call-start = ((), (), s32[]{:S(2)}) async-start(), calls=%async_computation.6 | async-start | bytes 1179648 | tf_op jit(solution)/shard_map/all_gather | solution.py:117
  25.5 23.6 %all-to-all-start = ((bf16[8,2,32,256]{3,2,1,0:T(8,128)(2,1)}), bf16[8,2,32,256]{3,2,1,0:T(8,128)(2,1)S(1)}, u32[]{:S(2)}, u32[]{:S(2)}) async-start(bf16[8,2,32,256]{3,2,1,0:T(8,128)(2,1)} %copy.38), calls=%async_computation | async-start | bytes 524288 | tf_op jit(solution)/shard_map/all_to_all | solution.py:19
  35.6 13.2 %copy-start.7 = (bf16[256,256]{1,0:T(8,128)(2,1)S(1)}, bf16[256,256]{1,0:T(8,128)(2,1)}, u32[]{:S(2)}) copy-start(bf16[256,256]{1,0:T(8,128)(2,1)} %param.13) | copy-start | bytes 393220
  35.6 13.3 %copy-start.10 = (s32[1,256]{1,0:T(1,128)S(1)}, s32[1,256]{1,0:T(1,128)}, u32[]{:S(2)}) copy-start(s32[1,256]{1,0:T(1,128)} %param.16) | copy-start | bytes 3076
  35.6 13.3 %copy-start.11 = (s32[1,256]{1,0:T(1,128)S(1)}, s32[1,256]{1,0:T(1,128)}, u32[]{:S(2)}) copy-start(s32[1,256]{1,0:T(1,128)} %param.17) | copy-start | bytes 3076
  36.9 23.9 %collective-permute-start = (bf16[1024,256]{1,0:T(8,128)(2,1)}, bf16[1024,256]{1,0:T(8,128)(2,1)S(1)}, u32[]{:S(2)}, u32[]{:S(2)}) collective-permute-start(bf16[1024,256]{1,0:T(8,128)(2,1)} %get-tuple-element.36), channel_id=1, source_target_pairs={{0,2},{2,4},{4,6},{6,0},{1,3},{3,5},{5,7},{7,1},{8,10},{10,12},{12... | collective-permute-start | bytes 1572872 | tf_op jit(solution)/shard_map/ppermute | solution.py:29
  40.8 28.0 %collective-permute-start.1 = (bf16[1024,256]{1,0:T(8,128)(2,1)}, bf16[1024,256]{1,0:T(8,128)(2,1)S(1)}, u32[]{:S(2)}, u32[]{:S(2)}) collective-permute-start(bf16[1024,256]{1,0:T(8,128)(2,1)} %get-tuple-element.38), channel_id=1, source_target_pairs={{0,4},{2,6},{4,0},{6,2},{1,5},{3,7},{5,1},{7,3},{8,12},{10,14},{12... | collective-permute-start | bytes 1572872 | tf_op jit(solution)/shard_map/ppermute | solution.py:29
  45.4 23.4 %collective-permute-start.2 = (bf16[1024,256]{1,0:T(8,128)(2,1)}, bf16[1024,256]{1,0:T(8,128)(2,1)S(1)}, u32[]{:S(2)}, u32[]{:S(2)}) collective-permute-start(bf16[1024,256]{1,0:T(8,128)(2,1)} %get-tuple-element.35), channel_id=1, source_target_pairs={{0,6},{2,0},{4,2},{6,4},{1,7},{3,1},{5,3},{7,5},{8,14},{10,8},{12,... | collective-permute-start | bytes 1572872 | tf_op jit(solution)/shard_map/ppermute | solution.py:29
  48.9 1.2 copy-start.6
  53.1 17.6 %copy-start.9 = (s32[1,256]{1,0:T(1,128)S(1)}, s32[1,256]{1,0:T(1,128)}, u32[]{:S(2)}) copy-start(s32[1,256]{1,0:T(1,128)} %param.22) | copy-start | bytes 3076
  53.1 17.6 %copy-start.12 = (s32[1,256]{1,0:T(1,128)S(1)}, s32[1,256]{1,0:T(1,128)}, u32[]{:S(2)}) copy-start(s32[1,256]{1,0:T(1,128)} %param.23) | copy-start | bytes 3076
  54.2 33.2 %all-to-all-start.1 = ((bf16[8,256,256]{1,2,0:T(8,128)(2,1)}), bf16[8,256,256]{1,2,0:T(8,128)(2,1)}, u32[]{:S(2)}, u32[]{:S(2)}) async-start(bf16[8,256,256]{1,2,0:T(8,128)(2,1)} %broadcast_in_dim.40), calls=%async_computation.1 | async-start | bytes 2097152 | tf_op jit(solution)/shard_map/all_to_all | solution.py:19
  68.8 6.1 %copy-start.1 = (bf16[1024,256]{1,0:T(8,128)(2,1)}, bf16[1024,256]{1,0:T(8,128)(2,1)S(1)}, u32[]{:S(2)}) copy-start(bf16[1024,256]{1,0:T(8,128)(2,1)S(1)} %collective-permute-done.2.three) | copy-start | bytes 1572868
  68.8 4.8 %collective-permute-start.3 = (bf16[8,4,32,512]{3,2,1,0:T(8,128)(2,1)}, bf16[8,4,32,512]{3,2,1,0:T(8,128)(2,1)S(1)}, u32[]{:S(2)}, u32[]{:S(2)}) collective-permute-start(bf16[8,4,32,512]{3,2,1,0:T(8,128)(2,1)} %bitcast.75), channel_id=1, source_target_pairs={{0,8},{8,0},{1,9},{9,1},{2,10},{10,2},{3,11},{11,3},{4,12},{12,4},... | collective-permute-start | bytes 3145736 | tf_op jit(solution)/shard_map/ppermute | solution.py:119
  75.1 12.3 %copy-start.13 = (bf16[256,512]{1,0:T(8,128)(2,1)S(1)}, bf16[256,512]{1,0:T(8,128)(2,1)}, u32[]{:S(2)}) copy-start(bf16[256,512]{1,0:T(8,128)(2,1)} %param.18) | copy-start | bytes 786436
  87.4 2.8 %copy-start.8 = (f32[512]{0:T(512)S(1)}, f32[512]{0:T(512)}, u32[]{:S(2)}) copy-start(f32[512]{0:T(512)} %param.20) | copy-start | bytes 6148
  90.1 1.5 copy-start.3
  91.7 36.9 %all-to-all-start.2 = ((bf16[128,8,512]{2,1,0:T(8,128)(2,1)}), bf16[128,8,512]{2,1,0:T(8,128)(2,1)S(1)}, u32[]{:S(2)}, u32[]{:S(2)}) async-start(bf16[128,8,512]{2,1,0:T(8,128)(2,1)} %bitcast.71), calls=%async_computation.2 | async-start | bytes 2097152 | tf_op jit(solution)/shard_map/all_to_all | solution.py:19
  104.2 28.6 %collective-permute-start.7 = (bf16[256,1024]{1,0:T(8,128)(2,1)}, bf16[256,1024]{1,0:T(8,128)(2,1)}, u32[]{:S(2)}, u32[]{:S(2)}) collective-permute-start(bf16[256,1024]{1,0:T(8,128)(2,1)} %get-tuple-element.31), channel_id=1, source_target_pairs={{0,2},{2,4},{4,6},{6,0},{1,3},{3,5},{5,7},{7,1},{8,10},{10,12},{12... | collective-permute-start | bytes 1572872 | tf_op jit(solution)/shard_map/ppermute | solution.py:29
  106.1 26.7 %collective-permute-start.8 = (bf16[256,1024]{1,0:T(8,128)(2,1)}, bf16[256,1024]{1,0:T(8,128)(2,1)}, u32[]{:S(2)}, u32[]{:S(2)}) collective-permute-start(bf16[256,1024]{1,0:T(8,128)(2,1)} %get-tuple-element.30), channel_id=1, source_target_pairs={{0,4},{2,6},{4,0},{6,2},{1,5},{3,7},{5,1},{7,3},{8,12},{10,14},{12... | collective-permute-start | bytes 1572872 | tf_op jit(solution)/shard_map/ppermute | solution.py:29
  110.4 25.0 %collective-permute-start.9 = (bf16[256,1024]{1,0:T(8,128)(2,1)}, bf16[256,1024]{1,0:T(8,128)(2,1)}, u32[]{:S(2)}, u32[]{:S(2)}) collective-permute-start(bf16[256,1024]{1,0:T(8,128)(2,1)} %get-tuple-element.29), channel_id=1, source_target_pairs={{0,6},{2,0},{4,2},{6,4},{1,7},{3,1},{5,3},{7,5},{8,14},{10,8},{12,... | collective-permute-start | bytes 1572872 | tf_op jit(solution)/shard_map/ppermute | solution.py:29
  128.6 1.0 copy-start.2
  174.7 13.9 %copy-start.4 = (f32[256,512]{1,0:T(8,128)S(1)}, f32[256,512]{1,0:T(8,128)}, u32[]{:S(2)}) copy-start(f32[256,512]{1,0:T(8,128)} %copy-done.3) | copy-start | bytes 1572868
  174.7 53.8 %all-to-all-start.5 = ((bf16[128,8,512]{2,1,0:T(8,128)(2,1)}), bf16[128,8,512]{2,1,0:T(8,128)(2,1)S(1)}, u32[]{:S(2)}, u32[]{:S(2)}) async-start(bf16[128,8,512]{2,1,0:T(8,128)(2,1)} %bitcast.30), calls=%async_computation.5 | async-start | bytes 2097152 | tf_op jit(solution)/shard_map/all_to_all | solution.py:19
  189.1 27.2 %collective-permute-start.4 = (f32[2,256]{1,0:T(2,128)S(1)}, f32[2,256]{1,0:T(2,128)S(1)}, u32[]{:S(2)}, u32[]{:S(2)}) collective-permute-start(f32[2,256]{1,0:T(2,128)S(1)} %pad_maximum_fusion), channel_id=1, source_target_pairs={{0,1},{1,0},{2,3},{3,2},{4,5},{5,4},{6,7},{7,6},{8,9},{9,8},{10,11... | collective-permute-start | bytes 6152 | tf_op jit(solution)/shard_map/ppermute | solution.py:159
  216.3 5.5 %collective-permute-start.5 = (f32[2,256]{1,0:T(2,128)S(1)}, f32[2,256]{1,0:T(2,128)S(1)}, u32[]{:S(2)}, u32[]{:S(2)}) collective-permute-start(f32[2,256]{1,0:T(2,128)S(1)} %fusion.25), channel_id=1, source_target_pairs={{0,2},{2,0},{4,6},{6,4},{1,3},{3,1},{5,7},{7,5},{8,10},{10,8},{12,... | collective-permute-start | bytes 6152 | tf_op jit(solution)/shard_map/ppermute | solution.py:160
  221.8 6.7 %collective-permute-start.6 = (f32[2,256]{1,0:T(2,128)S(1)}, f32[2,256]{1,0:T(2,128)S(1)}, u32[]{:S(2)}, u32[]{:S(2)}) collective-permute-start(f32[2,256]{1,0:T(2,128)S(1)} %fusion.37), channel_id=1, source_target_pairs={{0,6},{6,0},{2,4},{4,2},{1,7},{7,1},{3,5},{5,3},{8,14},{14,8},{10,... | collective-permute-start | bytes 6152 | tf_op jit(solution)/shard_map/ppermute | solution.py:161
Sparse Core Ops, SparseCore 0:
  22.9 41.2 all-gather.3
